TPU v7x, 256 devices: a whole 4x4x8 slice. The times are simulated.
256 devices in a mesh: tm: 8 (over y, core), space: 32 (over x, z).
Axes of the slice: x: 4, y: 4, z: 8, core: 2. Of those that a mesh axis runs over, the one named last changes fastest.
Arguments:
- snapshots: bfloat16 [8192, 12, 32, 256], P('tm', None, 'space'), may hold values from -6 to 6
- sketch: bfloat16 [8192, 256], P('tm'), may hold values from -0.0625 to 0.0625
- volume: float32 [32, 256], P('space'), may hold values from 0.3 to 27, as said below
- grad_weight: float32 [12], replicated, may hold values from 0.5 to 2
- dilation: int32 [12], replicated, may hold values from 1 to 4
Outputs:
- basis: float32 [256, 12, 32, 256], P('tm', None, 'space')
- upper: float32 [256, 256], replicated
Inputs may be any that keep to these rules, and one draw needn't show every extreme that they name: `volume`: positive cell volumes.
All inputs are finite; a program needn't handle non-finite values.
Results may differ from a plain program's by a relative error of at most 0.0003.
Values sent between devices are 32-bit elements; how exact they have to be, the bound alone decides.
No kernel may reach another device: no remote copies, remote signals or barrier semaphores. Data moves between devices by JAX's collectives and lax.ppermute only.
A program may use at most 128 MiB of HBM per device.

v0:
```python
import jax
import jax.numpy as jnp
from jax import lax
from jax.sharding import PartitionSpec as P

WX = 16
WY = 16


def with_halo(x, sides, width):
    for axis, dim in sides:
        peers, length = (lax.axis_size(axis), x.shape[dim])
        up = [(i, (i + 1) % peers) for i in range(peers - 1)]
        down = [(j, i) for i, j in up]
        last = lax.slice_in_dim(x, length - width, length, axis=dim)
        leading = lax.slice_in_dim(x, 0, width, axis=dim)
        before = lax.ppermute(last, axis, up)
        after = lax.ppermute(leading, axis, down)
        x = jnp.concatenate([before, x, after], axis=dim)
    return x


def line_ops(length, dilation):
    row_index = jnp.arange(length, dtype=jnp.int32)[:, None]
    col_index = jnp.arange(length, dtype=jnp.int32)[None, :]
    blur_line = jnp.where(row_index == col_index, jnp.float32(0.5), jnp.float32(0.0))
    blur_line = blur_line + jnp.where(
        jnp.abs(row_index - col_index) == 1, jnp.float32(0.25), jnp.float32(0.0)
    )
    shift_by = dilation[:, None, None]
    diff_line = jnp.where(
        col_index[None] == row_index[None] + shift_by, jnp.float32(0.5), jnp.float32(0.0)
    )
    diff_line = diff_line - jnp.where(
        col_index[None] == row_index[None] - shift_by, jnp.float32(0.5), jnp.float32(0.0)
    )
    return (blur_line, diff_line)


def filter_matrix(dilation, grad_weight):
    blur_x, diff_x = line_ops(WX, dilation)
    blur_y, diff_y = line_ops(WY, dilation)
    blur = jnp.kron(blur_y, blur_x)
    eye_x = jnp.eye(WX, dtype=jnp.float32)
    eye_y = jnp.eye(WY, dtype=jnp.float32)

    def one_field(diff_xf, diff_yf):
        return jnp.kron(eye_y, diff_xf) + jnp.kron(diff_yf, eye_x)

    gradient = jax.vmap(one_field)(diff_x, diff_y)
    mixed = jnp.einsum("fqr,rp->fqp", gradient, blur, precision=lax.Precision.HIGHEST)
    return blur[None] + grad_weight[:, None, None] * mixed


def local_gram(panel_part, volume_part):
    rank_size = panel_part.shape[3]
    weighted = (panel_part * jnp.transpose(volume_part)[:, None, :, None]).reshape(-1, rank_size)
    panel_rows = panel_part.reshape(-1, rank_size)
    return jnp.dot(
        weighted.T, panel_rows, precision=lax.Precision.HIGHEST, preferred_element_type=jnp.float32
    )


def z_combine(padded, depth):
    return (
        0.25 * padded[:, :, 0:depth]
        + 0.5 * padded[:, :, 1 : depth + 1]
        + 0.25 * padded[:, :, 2 : depth + 2]
    )


def shards(snapshots, sketch, volume, grad_weight, dilation):
    matrix = filter_matrix(dilation, grad_weight)
    snap_count, fields, depth, plane_size = snapshots.shape
    rank_size = sketch.shape[1]
    groups = lax.axis_size("tm")
    cell_share = plane_size // groups
    first_cell = lax.axis_index("tm") * cell_share
    partial_value = jnp.einsum(
        "sfzp,sk->pfzk", snapshots, sketch, preferred_element_type=jnp.float32
    )
    row_total = plane_size * fields * depth * lax.axis_size("space")
    raw_panel = lax.psum(partial_value, "tm")
    image = jnp.einsum("fqp,pfzk->qfzk", matrix, raw_panel, precision=lax.Precision.HIGHEST)
    padded = with_halo(image, (("space", 2),), 1)
    whole_panel = z_combine(padded, depth)
    gram_matrix = lax.psum(local_gram(whole_panel, volume), "space")
    panel_part = lax.dynamic_slice_in_dim(whole_panel, first_cell, cell_share, 0)
    gram_matrix = gram_matrix / row_total
    lower_factor = jnp.linalg.cholesky(gram_matrix)
    panel_rows = panel_part.reshape(-1, rank_size)
    basis_rows = lax.linalg.triangular_solve(
        lower_factor, panel_rows, left_side=False, lower=True, transpose_a=True
    )
    return (basis_rows.reshape(panel_part.shape), jnp.transpose(lower_factor))


def solution(mesh):
    return jax.shard_map(
        shards,
        mesh=mesh,
        in_specs=(P("tm", None, "space", None), P("tm", None), P("space", None), P(), P()),
        out_specs=(P("tm", None, "space", None), P()),
        check_vma=False,
    )
```

profile of v0, /device:TPU:8, one launch (start us, length us, event | category | flops | bytes accessed | tf_op | source)
XLA Modules:
  0.0 397.9 jit_solution(14498710043937404190)
XLA Ops:
  7.2 1.0 copy-done
  8.2 6.3 %fusion.12 = f32[256,12,256]{0,2,1:T(8,128)} fusion(bf16[1024,12,1,256]{3,0,2,1:T(8,128)(2,1)} %param.5, bf16[1024,256]{1,0:T(8,128)(2,1)S(1)} %copy-done), kind=kOutput, calls=%fused_computation.14 | convolution fusion | flops 1610612736 | bytes 9961472 | tf_op jit(solution)/shard_map/sfzp,sk->pfzk/dot_general | solution.py:79
  17.0 11.4 %multiply_add_fusion = f32[12,16,16,16,16]{4,3,2,1,0:T(8,128)} fusion(f32[16,16]{1,0:T(8,128)S(1)} %fusion.35, f32[12,16,16]{2,1,0:T(8,128)S(1)} %select_subtract_fusion), kind=kLoop, calls=%fused_computation.2 | loop fusion | flops 2359296 | bytes 3159040 | tf_op jit(solution)/shard_map/vmap()/add | solution.py:48
  28.4 18.6 %add.103 = f32[12,256,256]{2,1,0:T(8,128)} reshape(f32[12,16,16,16,16]{4,3,2,1,0:T(8,128)} %multiply_add_fusion) | data formatting | bytes 6291456 | tf_op jit(solution)/shard_map/vmap()/add | solution.py:48
  46.9 6.2 %fusion.37 = f32[12,256,256]{2,1,0:T(8,128)} fusion(f32[12,256,256]{2,1,0:T(8,128)} %add.103, f32[256,256,1]{1,0,2:T(8,128)S(1)} %reshape.280), kind=kOutput, calls=%fused_computation.62 | convolution fusion | flops 2415919104 | bytes 6553600 | tf_op jit(solution)/shard_map/fqr,rp->fqp/dot_general | solution.py:51
  53.1 36.2 %all-reduce.4.cloned.1.call-done = f32[256,12,256]{0,2,1:T(8,128)} async-done(((f32[256,12,256]{0,2,1:T(8,128)}), f32[256,12,256]{0,2,1:T(8,128)}) %all-reduce.4.cloned.1.call-update) | async-done | bytes 3145744 | tf_op jit(solution)/shard_map/psum | solution.py:83
  89.3 6.6 %fusion.9 = f32[256,12,1,256]{3,0,1,2:T(8,128)S(1)} fusion(f32[256,12,256]{0,2,1:T(8,128)} %all-reduce.4.cloned.1.call-done, f32[12,256,256]{2,1,0:T(8,128)} %fusion.37, f32[12]{0:T(128)S(1)} %copy-done.3, f32[256,256]{1,0:T(8,128)S(1)} %mul.135), kind=kOutput, calls=%fused_computation.13 | convolution fusion | flops 2417491968 | bytes 9699376 | tf_op jit(solution)/shard_map/fqp,pfzk->qfzk/dot_general | solution.py:84
  96.0 3.7 collective-permute-start
  99.6 1.5 collective-permute-start.1
  101.1 64.8 %collective-permute-done = f32[256,12,1,256]{3,0,1,2:T(8,128)S(1)} collective-permute-done((f32[256,12,1,256]{3,0,1,2:T(8,128)S(1)}, f32[256,12,1,256]{3,0,1,2:T(8,128)S(1)}, u32[]{:S(2)}, u32[]{:S(2)}) %collective-permute-start) | collective-permute-done | bytes 3145760 | tf_op jit(solution)/shard_map/ppermute | solution.py:17
  165.9 4.3 %collective-permute-done.1 = f32[256,12,1,256]{3,0,1,2:T(8,128)S(1)} collective-permute-done((f32[256,12,1,256]{3,0,1,2:T(8,128)S(1)}, f32[256,12,1,256]{3,0,1,2:T(8,128)S(1)}, u32[]{:S(2)}, u32[]{:S(2)}) %collective-permute-start.1) | collective-permute-done | bytes 3145760 | tf_op jit(solution)/shard_map/ppermute | solution.py:18
  170.8 1.6 copy-done.1
  172.5 6.0 %fusion.18 = f32[256,256]{0,1:T(8,128)} fusion(f32[256,12,1,256]{3,0,1,2:T(8,128)S(1)} %multiply_add_fusion.1, f32[256]{0:T(256)S(1)} %bitcast.74), kind=kOutput, calls=%fused_computation.18 | convolution fusion | flops 2416705536 | bytes 3408896 | tf_op jit(solution)/shard_map/dot_general | solution.py:59
  178.6 1.0 constant_dynamic-slice_fusion.1
  179.9 145.6 %all-reduce.6.cloned.1.call-done = f32[256,256]{0,1:T(8,128)} async-done(((f32[256,256]{0,1:T(8,128)}), f32[256,256]{0,1:T(8,128)}) %all-reduce.6.cloned.1.call-update) | async-done | bytes 262160 | tf_op jit(solution)/shard_map/psum | solution.py:87
  326.6 1.0 fusion.24
  327.6 11.7 %cholesky.50 = f32[128,128]{1,0:T(8,128)S(1)} custom-call(f32[128,128]{1,0:T(8,128)S(1)} %cholesky.118), custom_call_target="Cholesky" | custom-call | tf_op jit(solution)/shard_map/jit(cholesky)/cholesky | solution.py:90
  339.4 10.0 %custom-call.14 = f32[1,128,128]{1,2,0:T(8,128)S(1)} custom-call(f32[1,128,128]{2,1,0:T(8,128)S(1)} %get-tuple-element.29), custom_call_target="InvertDiagBlocksLowerTriangular" | custom-call | tf_op jit(solution)/shard_map/jit(cholesky)/cholesky | solution.py:90
  349.9 11.7 %cholesky.105 = f32[128,128]{1,0:T(8,128)S(1)} custom-call(f32[128,128]{1,0:T(8,128)S(1)} %convolution_subtract_fusion), custom_call_target="Cholesky" | custom-call | tf_op jit(solution)/shard_map/jit(cholesky)/cholesky | solution.py:90
  363.7 3.9 while.1
  364.3 1.3 bitcast_dynamic-update-slice_fusion.2
  366.2 1.3 bitcast_dynamic-update-slice_fusion.2
  367.6 19.7 %custom-call.15 = f32[2,128,128]{1,2,0:T(8,128)S(1)} custom-call(f32[2,128,128]{2,1,0:T(8,128)S(1)} %get-tuple-element.9), custom_call_target="InvertDiagBlocksLowerTriangular" | custom-call | tf_op jit(solution)/shard_map/triangular_solve | solution.py:92
  388.8 1.1 reshape.283
  (45 shorter events, 9.3 us)
Async XLA Ops:
  7.2 1.0 copy-start
  7.2 82.1 %all-reduce.4.cloned.1.call-start = ((), (), s32[]{:S(2)}) async-start(), calls=%async_computation | async-start | bytes 6291456 | tf_op jit(solution)/shard_map/psum | solution.py:83
  14.6 310.9 %all-reduce.6.cloned.1.call-start = ((), (), s32[]{:S(2)}) async-start(), calls=%async_computation.1 | async-start | bytes 524288 | tf_op jit(solution)/shard_map/psum | solution.py:87
  14.6 2.1 copy-start.4
  46.9 42.4 %copy-start.3 = (f32[12]{0:T(128)S(1)}, f32[12]{0:T(128)}, u32[]{:S(2)}) copy-start(f32[12]{0:T(128)} %param.8) | copy-start | bytes 148
  96.0 76.5 %copy-start.2 = (f32[1,256]{1,0:T(1,128)S(1)}, f32[1,256]{1,0:T(1,128)}, u32[]{:S(2)}) copy-start(f32[1,256]{1,0:T(1,128)} %param.7) | copy-start | bytes 3076
  96.0 69.9 %collective-permute-start = (f32[256,12,1,256]{3,0,1,2:T(8,128)S(1)}, f32[256,12,1,256]{3,0,1,2:T(8,128)S(1)}, u32[]{:S(2)}, u32[]{:S(2)}) collective-permute-start(f32[256,12,1,256]{3,0,1,2:T(8,128)S(1)} %fusion.9), channel_id=1, source_target_pairs={{0,1},{1,2},{2,3},{3,4},{4,5},{5,6},{6,7},{7,8},{8,9},{9,10},{10,1... | collective-permute-start | bytes 9437192 | tf_op jit(solution)/shard_map/ppermute | solution.py:17
  99.6 70.5 %collective-permute-start.1 = (f32[256,12,1,256]{3,0,1,2:T(8,128)S(1)}, f32[256,12,1,256]{3,0,1,2:T(8,128)S(1)}, u32[]{:S(2)}, u32[]{:S(2)}) collective-permute-start(f32[256,12,1,256]{3,0,1,2:T(8,128)S(1)} %fusion.9), channel_id=1, source_target_pairs={{1,0},{2,1},{3,2},{4,3},{5,4},{6,5},{7,6},{8,7},{9,8},{10,9},{11,1... | collective-permute-start | bytes 9437192 | tf_op jit(solution)/shard_map/ppermute | solution.py:18
  170.8 1.6 copy-start.1
Sparse Core Ops, SparseCore 0:
  14.7 74.5 all-reduce.3
  178.7 146.8 all-reduce.5
where the time goes:
time: 404 us; the launch traced here: 398 us
  waiting for transfers between devices  251 us (62%)
  other arithmetic  68.3 us (17%)
  local copies, waits for them, and re-layouts  30.6 us (8%)
  matrix products  27 us (7%)
  between operations  15.8 us (4%)
  starting transfers between devices  5.2 us (1%)
    psum x1, waiting for transfers between devices, shards(): gram_matrix = lax.psum(local_gram(whole_panel, volume), 'space')  146 us
    ppermute x1, waiting for transfers between devices, with_halo(): before = lax.ppermute(last, axis, up)  64.8 us
    psum x1, waiting for transfers between devices, shards(): raw_panel = lax.psum(partial_value, 'tm')  36.2 us
    another operation x6, other arithmetic, shards(): lower_factor = jnp.linalg.cholesky(gram_matrix)  34.2 us
    another operation x3, other arithmetic, shards(): lax.linalg.triangular_solve(lower_factor, panel_rows, left_side=False, lo...  19.7 us
    add x1, local copies, waits for them, and re-layouts, one_field(): return jnp.kron(eye_y, diff_xf) + jnp.kron(diff_yf, eye_x)  18.6 us
    add x1, other arithmetic, one_field(): return jnp.kron(eye_y, diff_xf) + jnp.kron(diff_yf, eye_x)  11.4 us
  transfers between devices with their start and end apart: 4, of which 4 were waited for; matrix products, arithmetic and copies ran while one was open for 10% of the time, Pallas kernels for 0%

commit v1 on v0

v1 whole, which is shorter than its diff:
```python
import functools

import jax
import jax.numpy as jnp
from jax import lax
from jax.experimental import pallas as pl
from jax.experimental.pallas import tpu as pltpu
from jax.sharding import PartitionSpec as P

WX = 16
WY = 16
PLANE = WX * WY
RANK = 256
FIELDS = 12
SHARE = 32
NZ = 32
ROWS = 98304
HALF = 128
EXACT = lax.Precision.HIGHEST


def hat(offset):
    return jnp.maximum(0.5 - 0.25 * jnp.abs(offset), 0.0)


def hat_slope(source, target, shift):
    ahead = jnp.where(target + shift < 16.0, hat(source - target - shift), 0.0)
    behind = jnp.where(target - shift >= 0.0, hat(source - target + shift), 0.0)
    return 0.5 * (ahead - behind)


def filter_rows(out_ref, blocks, shift, weight):
    lane = lax.broadcasted_iota(jnp.int32, (WX, PLANE), 1)
    px = (lane % WX).astype(jnp.float32)
    py = (lane[:8] // WX).astype(jnp.float32)
    qx = lax.broadcasted_iota(jnp.int32, (WX, PLANE), 0).astype(jnp.float32)
    along_x = hat(px - qx)
    mixed_x = along_x + weight * hat_slope(px, qx, shift)
    for r, block in enumerate(blocks):
        for h in range(2):
            qy = jnp.full((8, PLANE), (2 * block + h).astype(jnp.float32))
            along_y = hat(py - qy)
            slope_y = weight * hat_slope(py, qy, shift)
            for g in range(2):
                rows = slice(8 * g, 8 * g + 8)
                out_ref[pl.ds(32 * r + 16 * h + 8 * g, 8), :] = (
                    along_y * mixed_x[rows] + slope_y * along_x[rows]
                )


def split(x):
    high = x.astype(jnp.bfloat16)
    return high, (x - high.astype(jnp.float32)).astype(jnp.bfloat16)


def sketch_kernel(
    first, order, dilation, weight, snap_ref, sketch_ref, send_ref, keep_ref, turned, matrix
):
    step = pl.program_id(0)
    me = lax.axis_index("tm")
    y, core = me // 2, me % 2

    @pl.when(step == 0)
    def _():
        turned[...] = sketch_ref[...].T

    blocks = [2 * (y ^ m) + (1 - core) for m in order] + [2 * (y ^ m) + core for m in order]
    filter_rows(
        matrix, blocks, dilation[first + step].astype(jnp.float32), weight[first + step]
    )
    raw = jnp.dot(turned[...], snap_ref[0], preferred_element_type=jnp.float32)
    raw_high, raw_low = split(raw)
    mat_high, mat_low = split(matrix[...])
    dot = functools.partial(
        lax.dot_general,
        dimension_numbers=(((1,), (1,)), ((), ())),
        preferred_element_type=jnp.float32,
    )
    image = dot(mat_high, raw_high) + (dot(mat_high, raw_low) + dot(mat_low, raw_high))
    send_ref[:, 0] = image[:HALF].reshape(4, SHARE, RANK)
    keep_ref[:, 0] = image[HALF:].reshape(4, SHARE, RANK)


def sketch_call(snaps, sketch, dilation, weight, first, count, order):
    out = jax.ShapeDtypeStruct((4, count, SHARE, RANK), jnp.float32)
    smem = pl.BlockSpec(memory_space=pltpu.SMEM)
    return pl.pallas_call(
        functools.partial(sketch_kernel, first, order),
        grid=(count,),
        in_specs=[
            smem,
            smem,
            pl.BlockSpec((1, 1024, PLANE), lambda i: (first + i, 0, 0)),
            pl.BlockSpec((1024, RANK), lambda i: (0, 0)),
        ],
        out_specs=[pl.BlockSpec((4, 1, SHARE, RANK), lambda i: (0, i, 0, 0))] * 2,
        out_shape=[out, out],
        scratch_shapes=[
            pltpu.VMEM((RANK, 1024), jnp.bfloat16),
            pltpu.VMEM((PLANE, PLANE), jnp.float32),
        ],
        compiler_params=pltpu.CompilerParams(vmem_limit_bytes=16 * 2**20),
        cost_estimate=pl.CostEstimate(
            flops=count * 2 * 256 * 256 * 1792, bytes_accessed=count * 2**20, transcendentals=0
        ),
    )(dilation, weight, snaps, sketch)


def panel_kernel(counts, volume_ref, *refs):
    parts, (panel_ref, gram_ref) = refs[:-2], refs[-2:]
    me, plane = lax.axis_index("tm"), lax.axis_index("space")
    row = lax.broadcasted_iota(jnp.int32, (SHARE, PLANE), 0)
    lane = lax.broadcasted_iota(jnp.int32, (SHARE, PLANE), 1)
    volume = jnp.broadcast_to(volume_ref[...], (SHARE, PLANE))
    mine = jnp.sum(jnp.where(lane == row + me * SHARE, volume, 0.0), axis=1, keepdims=True)
    root = jnp.broadcast_to(jnp.sqrt(mine), (SHARE, RANK))
    scaled = []
    at = 0
    for n, count in enumerate(counts):
        here, below, above = parts[3 * n : 3 * n + 3]
        for f in range(count):
            panel = 0.5 * here[f]
            panel = panel + jnp.where(plane > 0, 0.25 * below[f], 0.0)
            panel = panel + jnp.where(plane < NZ - 1, 0.25 * above[f], 0.0)
            panel_ref[at] = panel
            scaled.append(panel * root)
            at += 1
    rows = jnp.concatenate(scaled, axis=0)
    gram = lax.dot_general(
        rows,
        rows,
        (((0,), (0,)), ((), ())),
        precision=EXACT,
        preferred_element_type=jnp.float32,
    )
    gram = gram * (1.0 / ROWS)
    gram_ref[:HALF] = gram[HALF:, :HALF]
    row = lax.broadcasted_iota(jnp.int32, (HALF, HALF), 0)
    lane = lax.broadcasted_iota(jnp.int32, (HALF, HALF), 1)
    last = gram[HALF:, HALF:]
    gram_ref[HALF : 2 * HALF] = jnp.where(row >= lane, gram[:HALF, :HALF], last)
    diag = jnp.sum(jnp.where(row == lane, last, 0.0), axis=0, keepdims=True)
    gram_ref[2 * HALF :] = jnp.broadcast_to(diag, (16, HALF))


def panel_call(volume, counts, parts):
    vmem = pl.BlockSpec(memory_space=pltpu.VMEM)
    return pl.pallas_call(
        functools.partial(panel_kernel, counts),
        in_specs=[vmem] * (1 + len(parts)),
        out_specs=[vmem, vmem],
        out_shape=[
            jax.ShapeDtypeStruct((FIELDS, SHARE, RANK), jnp.float32),
            jax.ShapeDtypeStruct((272, HALF), jnp.float32),
        ],
        compiler_params=pltpu.CompilerParams(vmem_limit_bytes=16 * 2**20),
    )(volume, *parts)


def factor(rows):
    shape = (8, HALF)
    sub = lax.broadcasted_iota(jnp.int32, shape, 0)
    lane = lax.broadcasted_iota(jnp.int32, shape, 1)
    rows = list(rows)
    count = len(rows)
    inverse = [jnp.where(lane == sub + 8 * t, 1.0, 0.0) for t in range(count)]
    uppers, lowers = [], []

    def column(x, j):
        return jnp.broadcast_to(x[:, j : j + 1], shape)

    def row_of(x, i):
        return jnp.broadcast_to(x[i : i + 1, :], shape)

    def total(terms):
        terms = list(terms)
        while len(terms) > 1:
            terms = [a + b for a, b in zip(terms[::2], terms[1::2])] + (
                terms[-1:] if len(terms) % 2 else []
            )
        return terms[0]

    def stack(parts):
        out = parts[-1]
        for i in range(len(parts) - 2, -1, -1):
            out = jnp.where(sub == i, parts[i], out)
        return out

    for s in range(count):
        here, there = rows[s], inverse[s]
        cols = [column(here, 8 * s + m) for m in range(8)]
        d = {(i, m): row_of(cols[m], i) for m in range(8) for i in range(m, 8)}
        low, root = {}, []
        for j in range(8):
            root.append(lax.rsqrt(d[j, j]))
            for i in range(j + 1, 8):
                low[i, j] = d[i, j] * root[j]
            for k in range(j + 1, 8):
                for i in range(k, 8):
                    d[i, k] = d[i, k] - low[i, j] * low[k, j]
        inv = {}
        for j in range(8):
            inv[j, j] = root[j]
            for i in range(j + 1, 8):
                inv[i, j] = -root[i] * total(low[i, k] * inv[k, j] for k in range(j, i))
        here_rows = [row_of(here, m) for m in range(8)]
        there_rows = [row_of(there, m) for m in range(8)]
        zero = jnp.zeros(shape, jnp.float32)
        lower_cols = [stack([inv[i, m] if i >= m else zero for i in range(8)]) for m in range(8)]
        upper = total(lower_cols[m] * here_rows[m] for m in range(8))
        uppers.append(jnp.where(lane >= sub + 8 * s, upper, 0.0))
        lowers.append(total(lower_cols[m] * there_rows[m] for m in range(8)))
        if s + 1 == count:
            break
        full = {}
        for i in range(8):
            for j in range(i + 1):
                full[i, j] = full[j, i] = total(inv[k, i] * inv[k, j] for k in range(i, 8))
        full_cols = [stack([full[i, m] for i in range(8)]) for m in range(8)]
        solved = total(full_cols[m] * here_rows[m] for m in range(8))
        solved_inv = total(full_cols[m] * there_rows[m] for m in range(8))
        solved_rows = [row_of(solved, m) for m in range(8)]
        inv_rows = [row_of(solved_inv, m) for m in range(8)]
        for t in range(s + 1, count):
            weights = [column(rows[t], 8 * s + m) for m in range(8)]
            rows[t] = rows[t] - total(weights[m] * solved_rows[m] for m in range(8))
            inverse[t] = inverse[t] - total(weights[m] * inv_rows[m] for m in range(8))
    return uppers, lowers


def basis_kernel(gram_ref, panel_ref, basis_ref, upper_ref, lower):
    row = lax.broadcasted_iota(jnp.int32, (HALF, HALF), 0)
    lane = lax.broadcasted_iota(jnp.int32, (HALF, HALF), 1)
    cross = gram_ref[:HALF]
    mixed = gram_ref[HALF : 2 * HALF]
    turned = mixed.T
    first = jnp.where(row >= lane, mixed, turned)
    diag = jnp.broadcast_to(gram_ref[2 * HALF : 2 * HALF + 1, :], (HALF, HALF))
    last = jnp.where(row < lane, mixed, jnp.where(row > lane, turned, diag))

    def dot(a, b, da, db):
        return lax.dot_general(
            a,
            b,
            (((da,), (db,)), ((), ())),
            precision=EXACT,
            preferred_element_type=jnp.float32,
        )

    groups = range(HALF // 8)
    uppers, lowers = factor([first[8 * t : 8 * t + 8] for t in groups])
    low_a = jnp.concatenate(lowers, axis=0)
    upper_ref[:HALF, :HALF] = jnp.concatenate(uppers, axis=0)
    side = dot(low_a, cross, 1, 1)
    upper_ref[:HALF, HALF:] = side
    upper_ref[HALF:, :HALF] = jnp.zeros((HALF, HALF), jnp.float32)
    last = last - dot(side, side, 0, 0)
    uppers, lowers = factor([last[8 * t : 8 * t + 8] for t in groups])
    low_b = jnp.concatenate(lowers, axis=0)
    upper_ref[HALF:, HALF:] = jnp.concatenate(uppers, axis=0)
    lower[:HALF, :HALF] = low_a
    lower[:HALF, HALF:] = jnp.zeros((HALF, HALF), jnp.float32)
    lower[HALF:, :HALF] = -dot(low_b, dot(side, low_a, 0, 0), 1, 0)
    lower[HALF:, HALF:] = low_b
    for f in range(FIELDS):
        basis_ref[:, f, 0, :] = dot(panel_ref[f], lower[...], 1, 1)


def basis_call(gram, panel):
    vmem = pl.BlockSpec(memory_space=pltpu.VMEM)
    return pl.pallas_call(
        basis_kernel,
        in_specs=[vmem, vmem],
        out_specs=[vmem, vmem],
        out_shape=[
            jax.ShapeDtypeStruct((SHARE, FIELDS, 1, RANK), jnp.float32),
            jax.ShapeDtypeStruct((RANK, RANK), jnp.float32),
        ],
        scratch_shapes=[pltpu.VMEM((RANK, RANK), jnp.float32)],
        compiler_params=pltpu.CompilerParams(vmem_limit_bytes=32 * 2**20),
    )(gram, panel)


def swap(x, axis, mask):
    return lax.ppermute(x, axis, [(i, i ^ mask) for i in range(lax.axis_size(axis))])


def ring(x, axis, step):
    n = lax.axis_size(axis)
    return lax.ppermute(x, axis, [(i, (i + step) % n) for i in range(n)])


def sum_over_tm(send, keep, near, far):
    got = swap(send, "tm", 1)
    mine = keep + got
    got = swap(mine[2:], "tm", 2 * near)
    mine = mine[:2] + got
    got = swap(mine[1], "tm", 2 * far)
    return mine[0] + got


def sum_over_all(gram):
    core = lax.axis_index("tm") % 2
    n = gram.shape[0] // 2
    mine = lax.dynamic_slice_in_dim(gram, core * n, n, 0)
    other = lax.dynamic_slice_in_dim(gram, (1 - core) * n, n, 0)
    mine = mine + swap(other, "tm", 1)
    for mask in (2, 6):
        mine = mine + swap(mine, "tm", mask)
    for mask in (8, 24, 1, 2, 7):
        mine = mine + swap(mine, "space", mask)
    other = swap(mine, "tm", 1)
    return jnp.where(
        core == 0, jnp.concatenate([mine, other], 0), jnp.concatenate([other, mine], 0)
    )


def shards(snapshots, sketch, volume, grad_weight, dilation):
    snaps = jnp.transpose(snapshots[:, :, 0, :], (1, 0, 2))
    counts = (6, 6)
    parts = []
    first = 0
    for count, (near, far) in zip(counts, ((1, 3), (3, 1))):
        order = (0, far, near, near ^ far)
        send, keep = sketch_call(snaps, sketch, dilation, grad_weight, first, count, order)
        image = sum_over_tm(send, keep, near, far)
        parts += [image, ring(image, "space", 1), ring(image, "space", -1)]
        first += count
    panel, gram = panel_call(volume, counts, parts)
    gram = sum_over_all(gram)
    basis, upper = basis_call(gram, panel)
    return basis, upper


def solution(mesh):
    return jax.shard_map(
        shards,
        mesh=mesh,
        in_specs=(P("tm", None, "space", None), P("tm", None), P("space", None), P(), P()),
        out_specs=(P("tm", None, "space", None), P()),
        check_vma=False,
    )
```

time: 404 us -> 111 us (0.27)
  the two profiles are of different devices: /device:TPU:8 before, /device:TPU:1 now
where the time goes in v1:
time: 111 us
  waiting for transfers between devices  41.8 us (38%)
  starting transfers between devices  34.5 us (31%)
  Pallas kernels  28 us (25%)
  local copies, waits for them, and re-layouts  5.23 us (5%)
    ppermute x15, waiting for transfers between devices, swap(): lax.ppermute(x, axis, [(i, i ^ mask) for i in range(lax.axis_size(axis))])  38.8 us
    ppermute x15, starting transfers between devices, swap(): lax.ppermute(x, axis, [(i, i ^ mask) for i in range(lax.axis_size(axis))])  23.3 us
    pallas_call x1, Pallas kernels, basis_call(): pl.pallas_call(basis_kernel, in_specs=[vmem, vmem], out_specs=[vmem, vmem...  15.7 us
    pallas_call x2, Pallas kernels, sketch_call(): pl.pallas_call(functools.partial(sketch_kernel, first, order), grid=(coun...  11.5 us
    ppermute x4, starting transfers between devices, ring(): return lax.ppermute(x, axis, [(i, (i + step) % n) for i in range(n)])  11.2 us
    unnamed x10, local copies, waits for them, and re-layouts  5.13 us
    ppermute x4, waiting for transfers between devices, ring(): return lax.ppermute(x, axis, [(i, (i + step) % n) for i in range(n)])  3.06 us
  transfers between devices with their start and end apart: 19, of which 14 were waited for; matrix products, arithmetic and copies ran while one was open for 0% of the time, Pallas kernels for 5%

profile of v1, /device:TPU:1, one launch (start us, length us, event | category | flops | bytes accessed | tf_op | source)
XLA Modules:
  0.0 110.8 jit_solution(15766130550750719233)
XLA Ops:
  0.6 2.8 %copy-done = bf16[1024,12,1,256]{3,0,2,1:T(8,128)(2,1)S(1)} copy-done((bf16[1024,12,1,256]{3,0,2,1:T(8,128)(2,1)S(1)}, bf16[1024,12,1,256]{3,0,2,1:T(8,128)(2,1)}, u32[]{:S(2)}) %copy-start) | copy-done | bytes 6291480
  5.8 5.7 %shard_map.68 = (f32[4,6,32,256]{3,2,1,0:T(8,128)S(1)}, f32[4,6,32,256]{3,2,1,0:T(8,128)S(1)}) custom-call(s32[12]{0:T(128)S(1)} %copy-done.2, f32[12]{0:T(128)S(1)} %copy-done.3, bf16[12,1024,256]{2,1,0:T(8,128)(2,1)S(1)} %bitcast.15, bf16[1024,256]{1,0:T(8,128)(2,1)S(1)} %copy-done.1), custom_call_target="tpu_custom_call" | custom-call | flops 1409286144 | bytes 6291456 | tf_op jit(solution)/shard_map/pallas_call | solution.py:87
  11.5 3.3 %collective-permute-start = (f32[4,6,32,256]{3,2,1,0:T(8,128)S(1)}, f32[4,6,32,256]{3,2,1,0:T(8,128)S(1)}, u32[]{:S(2)}, u32[]{:S(2)}) collective-permute-start(f32[4,6,32,256]{3,2,1,0:T(8,128)S(1)} %get-tuple-element.9), channel_id=1, source_target_pairs={{0,32},{32,0},{64,96},{96,64},{128,160},{160,128},{192,224},{224,1... | collective-permute-start | bytes 2359304 | tf_op jit(solution)/shard_map/ppermute | solution.py:285
  14.9 5.7 %shard_map.69 = (f32[4,6,32,256]{3,2,1,0:T(8,128)S(1)}, f32[4,6,32,256]{3,2,1,0:T(8,128)S(1)}) custom-call(s32[12]{0:T(128)S(1)} %copy-done.2, f32[12]{0:T(128)S(1)} %copy-done.3, bf16[12,1024,256]{2,1,0:T(8,128)(2,1)S(1)} %bitcast.16, bf16[1024,256]{1,0:T(8,128)(2,1)S(1)} %copy-done.1), custom_call_target="tpu_custom_call" | custom-call | flops 1409286144 | bytes 6291456 | tf_op jit(solution)/shard_map/pallas_call | solution.py:87
  21.0 2.0 %collective-permute-done.5 = f32[4,6,32,256]{3,2,1,0:T(8,128)S(1)} collective-permute-done((f32[4,6,32,256]{3,2,1,0:T(8,128)S(1)}, f32[4,6,32,256]{3,2,1,0:T(8,128)S(1)}, u32[]{:S(2)}, u32[]{:S(2)}) %collective-permute-start.5) | collective-permute-done | bytes 786464 | tf_op jit(solution)/shard_map/ppermute | solution.py:285
  23.1 1.1 collective-permute-start.6
  24.2 7.0 %collective-permute-done.1 = f32[2,6,32,256]{3,2,1,0:T(8,128)S(1)} collective-permute-done((f32[2,6,32,256]{3,2,1,0:T(8,128)S(1)}, f32[2,6,32,256]{3,2,1,0:T(8,128)S(1)}, u32[]{:S(2)}, u32[]{:S(2)}) %collective-permute-start.1) | collective-permute-done | bytes 393248 | tf_op jit(solution)/shard_map/ppermute | solution.py:285
  32.4 2.7 %collective-permute-done.6 = f32[2,6,32,256]{3,2,1,0:T(8,128)S(1)} collective-permute-done((f32[2,6,32,256]{3,2,1,0:T(8,128)S(1)}, f32[2,6,32,256]{3,2,1,0:T(8,128)S(1)}, u32[]{:S(2)}, u32[]{:S(2)}) %collective-permute-start.6) | collective-permute-done | bytes 393248 | tf_op jit(solution)/shard_map/ppermute | solution.py:285
  35.2 3.0 %collective-permute-done.2 = f32[6,32,256]{2,1,0:T(8,128)S(1)} collective-permute-done((f32[6,32,256]{2,1,0:T(8,128)S(1)}, f32[6,32,256]{2,1,0:T(8,128)S(1)}, u32[]{:S(2)}, u32[]{:S(2)}) %collective-permute-start.2) | collective-permute-done | bytes 196640 | tf_op jit(solution)/shard_map/ppermute | solution.py:285
  38.4 6.2 %collective-permute-start.4 = (f32[6,32,256]{2,1,0:T(8,128)S(1)}, f32[6,32,256]{2,1,0:T(8,128)S(1)}, u32[]{:S(2)}, u32[]{:S(2)}) collective-permute-start(f32[6,32,256]{2,1,0:T(8,128)S(1)} %fusion.1.refs_0_), channel_id=1, source_target_pairs={{0,31},{1,0},{2,1},{3,2},{4,3},{5,4},{6,5},{7,6},{8,7},{9,8},{10,9... | collective-permute-start | bytes 589832 | tf_op jit(solution)/shard_map/ppermute | solution.py:290
  44.7 4.8 %collective-permute-start.9 = (f32[6,32,256]{2,1,0:T(8,128)S(1)}, f32[6,32,256]{2,1,0:T(8,128)S(1)}, u32[]{:S(2)}, u32[]{:S(2)}) collective-permute-start(f32[6,32,256]{2,1,0:T(8,128)S(1)} %fusion.refs_3_), channel_id=1, source_target_pairs={{0,31},{1,0},{2,1},{3,2},{4,3},{5,4},{6,5},{7,6},{8,7},{9,8},{10,9... | collective-permute-start | bytes 589832 | tf_op jit(solution)/shard_map/ppermute | solution.py:290
  49.5 3.0 %collective-permute-done.8.refs_4_ = f32[6,32,256]{2,1,0:T(8,128)S(1)} collective-permute-done((f32[6,32,256]{2,1,0:T(8,128)S(1)}, f32[6,32,256]{2,1,0:T(8,128)S(1)}, u32[]{:S(2)}, u32[]{:S(2)}) %collective-permute-start.8) | collective-permute-done | bytes 196640 | tf_op jit(solution)/shard_map/ppermute | solution.py:290
  53.4 3.4 %collective-permute-start.10 = (f32[136,128]{1,0:T(8,128)S(1)}, f32[136,128]{1,0:T(8,128)S(1)}, u32[]{:S(2)}, u32[]{:S(2)}) collective-permute-start(f32[136,128]{1,0:T(8,128)S(1)} %constant_dynamic-slice_fusion), channel_id=1, source_target_pairs={{0,32},{32,0},{64,96},{96,64},{128,160},{160,128},{192,224},{224,1... | collective-permute-start | bytes 208904 | tf_op jit(solution)/shard_map/ppermute | solution.py:285
  57.8 3.1 %collective-permute-done.11 = f32[136,128]{1,0:T(8,128)S(1)} collective-permute-done((f32[136,128]{1,0:T(8,128)S(1)}, f32[136,128]{1,0:T(8,128)S(1)}, u32[]{:S(2)}, u32[]{:S(2)}) %collective-permute-start.11) | collective-permute-done | bytes 69664 | tf_op jit(solution)/shard_map/ppermute | solution.py:285
  60.9 2.8 %collective-permute-start.12 = (f32[136,128]{1,0:T(8,128)S(1)}, f32[136,128]{1,0:T(8,128)S(1)}, u32[]{:S(2)}, u32[]{:S(2)}) collective-permute-start(f32[136,128]{1,0:T(8,128)S(1)} %add.62), channel_id=1, source_target_pairs={{0,192},{32,224},{64,128},{96,160},{128,64},{160,96},{192,0},{224,... | collective-permute-start | bytes 208904 | tf_op jit(solution)/shard_map/ppermute | solution.py:285
  63.7 1.7 %collective-permute-done.12 = f32[136,128]{1,0:T(8,128)S(1)} collective-permute-done((f32[136,128]{1,0:T(8,128)S(1)}, f32[136,128]{1,0:T(8,128)S(1)}, u32[]{:S(2)}, u32[]{:S(2)}) %collective-permute-start.12) | collective-permute-done | bytes 69664 | tf_op jit(solution)/shard_map/ppermute | solution.py:285
  65.5 3.1 %collective-permute-done.13 = f32[136,128]{1,0:T(8,128)S(1)} collective-permute-done((f32[136,128]{1,0:T(8,128)S(1)}, f32[136,128]{1,0:T(8,128)S(1)}, u32[]{:S(2)}, u32[]{:S(2)}) %collective-permute-start.13) | collective-permute-done | bytes 69664 | tf_op jit(solution)/shard_map/ppermute | solution.py:285
  68.8 4.4 %collective-permute-done.14 = f32[136,128]{1,0:T(8,128)S(1)} collective-permute-done((f32[136,128]{1,0:T(8,128)S(1)}, f32[136,128]{1,0:T(8,128)S(1)}, u32[]{:S(2)}, u32[]{:S(2)}) %collective-permute-start.14) | collective-permute-done | bytes 69664 | tf_op jit(solution)/shard_map/ppermute | solution.py:285
  73.4 3.1 %collective-permute-done.15 = f32[136,128]{1,0:T(8,128)S(1)} collective-permute-done((f32[136,128]{1,0:T(8,128)S(1)}, f32[136,128]{1,0:T(8,128)S(1)}, u32[]{:S(2)}, u32[]{:S(2)}) %collective-permute-start.15) | collective-permute-done | bytes 69664 | tf_op jit(solution)/shard_map/ppermute | solution.py:285
  76.8 4.4 %collective-permute-done.16 = f32[136,128]{1,0:T(8,128)S(1)} collective-permute-done((f32[136,128]{1,0:T(8,128)S(1)}, f32[136,128]{1,0:T(8,128)S(1)}, u32[]{:S(2)}, u32[]{:S(2)}) %collective-permute-start.16) | collective-permute-done | bytes 69664 | tf_op jit(solution)/shard_map/ppermute | solution.py:285
  81.2 2.8 %collective-permute-start.17 = (f32[136,128]{1,0:T(8,128)S(1)}, f32[136,128]{1,0:T(8,128)S(1)}, u32[]{:S(2)}, u32[]{:S(2)}) collective-permute-start(f32[136,128]{1,0:T(8,128)S(1)} %add.67), channel_id=1, source_target_pairs={{0,7},{1,6},{2,5},{3,4},{4,3},{5,2},{6,1},{7,0},{8,15},{9,14},{10,... | collective-permute-start | bytes 208904 | tf_op jit(solution)/shard_map/ppermute | solution.py:285
  84.0 2.4 %collective-permute-done.17 = f32[136,128]{1,0:T(8,128)S(1)} collective-permute-done((f32[136,128]{1,0:T(8,128)S(1)}, f32[136,128]{1,0:T(8,128)S(1)}, u32[]{:S(2)}, u32[]{:S(2)}) %collective-permute-start.17) | collective-permute-done | bytes 69664 | tf_op jit(solution)/shard_map/ppermute | solution.py:285
  86.4 7.7 %collective-permute-start.18 = (f32[136,128]{1,0:T(8,128)S(1)}, f32[136,128]{1,0:T(8,128)S(1)}, u32[]{:S(2)}, u32[]{:S(2)}) collective-permute-start(f32[136,128]{1,0:T(8,128)S(1)} %add.68), channel_id=1, source_target_pairs={{0,32},{32,0},{64,96},{96,64},{128,160},{160,128},{192,224},{224,1... | collective-permute-start | bytes 208904 | tf_op jit(solution)/shard_map/ppermute | solution.py:285
  95.1 15.7 %shard_map.71 = (f32[32,12,1,256]{3,2,1,0:T(1,128)}, f32[256,256]{1,0:T(8,128)}) custom-call(f32[272,128]{1,0:T(8,128)S(1)} %maximum_select_fusion.gram_ref, f32[12,32,256]{2,1,0:T(8,128)S(1)} %get-tuple-element.13.panel_ref), custom_call_target="tpu_custom_call" | custom-call | tf_op jit(solution)/shard_map/pallas_call | solution.py:271
  (48 shorter events, 7.9 us)
Async XLA Ops:
  0.6 2.8 %copy-start = (bf16[1024,12,1,256]{3,0,2,1:T(8,128)(2,1)S(1)}, bf16[1024,12,1,256]{3,0,2,1:T(8,128)(2,1)}, u32[]{:S(2)}) copy-start(bf16[1024,12,1,256]{3,0,2,1:T(8,128)(2,1)} %param.5) | copy-start | bytes 18874372
  3.4 1.0 copy-start.1
  4.5 0.7 copy-start.2
  5.1 0.7 copy-start.3
  11.5 9.2 %collective-permute-start = (f32[4,6,32,256]{3,2,1,0:T(8,128)S(1)}, f32[4,6,32,256]{3,2,1,0:T(8,128)S(1)}, u32[]{:S(2)}, u32[]{:S(2)}) collective-permute-start(f32[4,6,32,256]{3,2,1,0:T(8,128)S(1)} %get-tuple-element.9), channel_id=1, source_target_pairs={{0,32},{32,0},{64,96},{96,64},{128,160},{160,128},{192,224},{224,1... | collective-permute-start | bytes 2359304 | tf_op jit(solution)/shard_map/ppermute | solution.py:285
  20.6 32.0 %copy-start.4 = (f32[1,256]{1,0:T(1,128)S(1)}, f32[1,256]{1,0:T(1,128)}, u32[]{:S(2)}) copy-start(f32[1,256]{1,0:T(1,128)} %volume_ref.1) | copy-start | bytes 3076
  20.6 2.4 %collective-permute-start.5 = (f32[4,6,32,256]{3,2,1,0:T(8,128)S(1)}, f32[4,6,32,256]{3,2,1,0:T(8,128)S(1)}, u32[]{:S(2)}, u32[]{:S(2)}) collective-permute-start(f32[4,6,32,256]{3,2,1,0:T(8,128)S(1)} %get-tuple-element.11), channel_id=1, source_target_pairs={{0,32},{32,0},{64,96},{96,64},{128,160},{160,128},{192,224},{224,1... | collective-permute-start | bytes 2359304 | tf_op jit(solution)/shard_map/ppermute | solution.py:285
  20.9 10.3 %collective-permute-start.1 = (f32[2,6,32,256]{3,2,1,0:T(8,128)S(1)}, f32[2,6,32,256]{3,2,1,0:T(8,128)S(1)}, u32[]{:S(2)}, u32[]{:S(2)}) collective-permute-start(f32[2,6,32,256]{3,2,1,0:T(8,128)S(1)} %slice.33), channel_id=1, source_target_pairs={{0,64},{32,96},{64,0},{96,32},{128,192},{160,224},{192,128},{224,1... | collective-permute-start | bytes 1179656 | tf_op jit(solution)/shard_map/ppermute | solution.py:285
  23.1 11.9 %collective-permute-start.6 = (f32[2,6,32,256]{3,2,1,0:T(8,128)S(1)}, f32[2,6,32,256]{3,2,1,0:T(8,128)S(1)}, u32[]{:S(2)}, u32[]{:S(2)}) collective-permute-start(f32[2,6,32,256]{3,2,1,0:T(8,128)S(1)} %slice.37), channel_id=1, source_target_pairs={{0,192},{32,224},{64,128},{96,160},{128,64},{160,96},{192,0},{224,... | collective-permute-start | bytes 1179656 | tf_op jit(solution)/shard_map/ppermute | solution.py:285
  31.3 7.0 %collective-permute-start.2 = (f32[6,32,256]{2,1,0:T(8,128)S(1)}, f32[6,32,256]{2,1,0:T(8,128)S(1)}, u32[]{:S(2)}, u32[]{:S(2)}) collective-permute-start(f32[6,32,256]{2,1,0:T(8,128)S(1)} %slice_bitcast_fusion.2), channel_id=1, source_target_pairs={{0,192},{32,224},{64,128},{96,160},{128,64},{160,96},{192,0},{224,... | collective-permute-start | bytes 589832 | tf_op jit(solution)/shard_map/ppermute | solution.py:285
  35.1 9.5 %collective-permute-start.7 = (f32[6,32,256]{2,1,0:T(8,128)S(1)}, f32[6,32,256]{2,1,0:T(8,128)S(1)}, u32[]{:S(2)}, u32[]{:S(2)}) collective-permute-start(f32[6,32,256]{2,1,0:T(8,128)S(1)} %slice_bitcast_fusion), channel_id=1, source_target_pairs={{0,64},{32,96},{64,0},{96,32},{128,192},{160,224},{192,128},{224,1... | collective-permute-start | bytes 589832 | tf_op jit(solution)/shard_map/ppermute | solution.py:285
  38.3 11.2 %collective-permute-start.3 = (f32[6,32,256]{2,1,0:T(8,128)S(1)}, f32[6,32,256]{2,1,0:T(8,128)S(1)}, u32[]{:S(2)}, u32[]{:S(2)}) collective-permute-start(f32[6,32,256]{2,1,0:T(8,128)S(1)} %fusion.1.refs_0_), channel_id=1, source_target_pairs={{0,1},{1,2},{2,3},{3,4},{4,5},{5,6},{6,7},{7,8},{8,9},{9,10},{10,1... | collective-permute-start | bytes 589832 | tf_op jit(solution)/shard_map/ppermute | solution.py:290
  38.4 11.1 %collective-permute-start.4 = (f32[6,32,256]{2,1,0:T(8,128)S(1)}, f32[6,32,256]{2,1,0:T(8,128)S(1)}, u32[]{:S(2)}, u32[]{:S(2)}) collective-permute-start(f32[6,32,256]{2,1,0:T(8,128)S(1)} %fusion.1.refs_0_), channel_id=1, source_target_pairs={{0,31},{1,0},{2,1},{3,2},{4,3},{5,4},{6,5},{7,6},{8,7},{9,8},{10,9... | collective-permute-start | bytes 589832 | tf_op jit(solution)/shard_map/ppermute | solution.py:290
  44.6 7.9 %collective-permute-start.8 = (f32[6,32,256]{2,1,0:T(8,128)S(1)}, f32[6,32,256]{2,1,0:T(8,128)S(1)}, u32[]{:S(2)}, u32[]{:S(2)}) collective-permute-start(f32[6,32,256]{2,1,0:T(8,128)S(1)} %fusion.refs_3_), channel_id=1, source_target_pairs={{0,1},{1,2},{2,3},{3,4},{4,5},{5,6},{6,7},{7,8},{8,9},{9,10},{10,1... | collective-permute-start | bytes 589832 | tf_op jit(solution)/shard_map/ppermute | solution.py:290
  44.7 7.8 %collective-permute-start.9 = (f32[6,32,256]{2,1,0:T(8,128)S(1)}, f32[6,32,256]{2,1,0:T(8,128)S(1)}, u32[]{:S(2)}, u32[]{:S(2)}) collective-permute-start(f32[6,32,256]{2,1,0:T(8,128)S(1)} %fusion.refs_3_), channel_id=1, source_target_pairs={{0,31},{1,0},{2,1},{3,2},{4,3},{5,4},{6,5},{7,6},{8,7},{9,8},{10,9... | collective-permute-start | bytes 589832 | tf_op jit(solution)/shard_map/ppermute | solution.py:290
  53.4 4.3 %collective-permute-start.10 = (f32[136,128]{1,0:T(8,128)S(1)}, f32[136,128]{1,0:T(8,128)S(1)}, u32[]{:S(2)}, u32[]{:S(2)}) collective-permute-start(f32[136,128]{1,0:T(8,128)S(1)} %constant_dynamic-slice_fusion), channel_id=1, source_target_pairs={{0,32},{32,0},{64,96},{96,64},{128,160},{160,128},{192,224},{224,1... | collective-permute-start | bytes 208904 | tf_op jit(solution)/shard_map/ppermute | solution.py:285
  57.7 3.2 %collective-permute-start.11 = (f32[136,128]{1,0:T(8,128)S(1)}, f32[136,128]{1,0:T(8,128)S(1)}, u32[]{:S(2)}, u32[]{:S(2)}) collective-permute-start(f32[136,128]{1,0:T(8,128)S(1)} %dynamic-slice_add_fusion), channel_id=1, source_target_pairs={{0,64},{32,96},{64,0},{96,32},{128,192},{160,224},{192,128},{224,1... | collective-permute-start | bytes 208904 | tf_op jit(solution)/shard_map/ppermute | solution.py:285
  60.9 4.5 %collective-permute-start.12 = (f32[136,128]{1,0:T(8,128)S(1)}, f32[136,128]{1,0:T(8,128)S(1)}, u32[]{:S(2)}, u32[]{:S(2)}) collective-permute-start(f32[136,128]{1,0:T(8,128)S(1)} %add.62), channel_id=1, source_target_pairs={{0,192},{32,224},{64,128},{96,160},{128,64},{160,96},{192,0},{224,... | collective-permute-start | bytes 208904 | tf_op jit(solution)/shard_map/ppermute | solution.py:285
  65.4 3.2 %collective-permute-start.13 = (f32[136,128]{1,0:T(8,128)S(1)}, f32[136,128]{1,0:T(8,128)S(1)}, u32[]{:S(2)}, u32[]{:S(2)}) collective-permute-start(f32[136,128]{1,0:T(8,128)S(1)} %add.63), channel_id=1, source_target_pairs={{0,8},{1,9},{2,10},{3,11},{4,12},{5,13},{6,14},{7,15},{8,0},{9,1},... | collective-permute-start | bytes 208904 | tf_op jit(solution)/shard_map/ppermute | solution.py:285
  68.7 4.5 %collective-permute-start.14 = (f32[136,128]{1,0:T(8,128)S(1)}, f32[136,128]{1,0:T(8,128)S(1)}, u32[]{:S(2)}, u32[]{:S(2)}) collective-permute-start(f32[136,128]{1,0:T(8,128)S(1)} %add.64), channel_id=1, source_target_pairs={{0,24},{1,25},{2,26},{3,27},{4,28},{5,29},{6,30},{7,31},{8,16},{9,... | collective-permute-start | bytes 208904 | tf_op jit(solution)/shard_map/ppermute | solution.py:285
  73.1 3.4 %collective-permute-start.15 = (f32[136,128]{1,0:T(8,128)S(1)}, f32[136,128]{1,0:T(8,128)S(1)}, u32[]{:S(2)}, u32[]{:S(2)}) collective-permute-start(f32[136,128]{1,0:T(8,128)S(1)} %add.65), channel_id=1, source_target_pairs={{0,1},{1,0},{2,3},{3,2},{4,5},{5,4},{6,7},{7,6},{8,9},{9,8},{10,11... | collective-permute-start | bytes 208904 | tf_op jit(solution)/shard_map/ppermute | solution.py:285
  76.6 4.6 %collective-permute-start.16 = (f32[136,128]{1,0:T(8,128)S(1)}, f32[136,128]{1,0:T(8,128)S(1)}, u32[]{:S(2)}, u32[]{:S(2)}) collective-permute-start(f32[136,128]{1,0:T(8,128)S(1)} %add.66), channel_id=1, source_target_pairs={{0,2},{1,3},{2,0},{3,1},{4,6},{5,7},{6,4},{7,5},{8,10},{9,11},{10,... | collective-permute-start | bytes 208904 | tf_op jit(solution)/shard_map/ppermute | solution.py:285
  81.2 5.2 %collective-permute-start.17 = (f32[136,128]{1,0:T(8,128)S(1)}, f32[136,128]{1,0:T(8,128)S(1)}, u32[]{:S(2)}, u32[]{:S(2)}) collective-permute-start(f32[136,128]{1,0:T(8,128)S(1)} %add.67), channel_id=1, source_target_pairs={{0,7},{1,6},{2,5},{3,4},{4,3},{5,2},{6,1},{7,0},{8,15},{9,14},{10,... | collective-permute-start | bytes 208904 | tf_op jit(solution)/shard_map/ppermute | solution.py:285
  86.4 8.6 %collective-permute-start.18 = (f32[136,128]{1,0:T(8,128)S(1)}, f32[136,128]{1,0:T(8,128)S(1)}, u32[]{:S(2)}, u32[]{:S(2)}) collective-permute-start(f32[136,128]{1,0:T(8,128)S(1)} %add.68), channel_id=1, source_target_pairs={{0,32},{32,0},{64,96},{96,64},{128,160},{160,128},{192,224},{224,1... | collective-permute-start | bytes 208904 | tf_op jit(solution)/shard_map/ppermute | solution.py:285

commit v2 on v1

v2 whole, which is shorter than its diff:
```python
import functools

import jax
import jax.numpy as jnp
from jax import lax
from jax.experimental import pallas as pl
from jax.experimental.pallas import tpu as pltpu
from jax.sharding import PartitionSpec as P

WX = 16
WY = 16
PLANE = WX * WY
RANK = 256
FIELDS = 12
SHARE = 32
SNAP_DEV = 1024
NZ = 32
ROWS = 98304
HALF = 128
GROUP = 4
DILATIONS = 4
EXACT = lax.Precision.HIGHEST


def hat(offset):
    return jnp.maximum(0.5 - 0.25 * jnp.abs(offset), 0.0)


def hat_slope(source, target, shift):
    ahead = jnp.where(target + shift < 16.0, hat(source - target - shift), 0.0)
    behind = jnp.where(target - shift >= 0.0, hat(source - target + shift), 0.0)
    return 0.5 * (ahead - behind)


def filter_tables(table, blocks):
    lane = lax.broadcasted_iota(jnp.int32, (WX, PLANE), 1)
    px = (lane & 15).astype(jnp.float32)
    py = (lane >> 4).astype(jnp.float32)
    qx = lax.broadcasted_iota(jnp.int32, (WX, PLANE), 0).astype(jnp.float32)
    along_x = hat(px - qx)
    slopes = [hat_slope(px, qx, float(d + 1)) for d in range(DILATIONS)]
    for r, block in enumerate(blocks):
        for h in range(2):
            qy = jnp.full((WX, PLANE), (2 * block + h).astype(jnp.float32))
            rows = pl.ds(32 * r + 16 * h, 16)
            along_y = hat(py - qy)
            table[0, rows, :] = (along_y * along_x).astype(jnp.bfloat16)
            for d in range(DILATIONS):
                mixed = along_y * slopes[d] + hat_slope(py, qy, float(d + 1)) * along_x
                table[d + 1, rows, :] = mixed.astype(jnp.bfloat16)


def split(x):
    high = x.astype(jnp.bfloat16)
    return high, (x - high.astype(jnp.float32)).astype(jnp.bfloat16)


def sketch_kernel(orders, snap_hbm, sketch_hbm, shift_hbm, weight_hbm, *refs):
    outs = refs[: 2 * len(orders)]
    snap, sketch, turned, table, shift, weight, snap_sem, sem = refs[2 * len(orders) :]
    first = [
        pltpu.make_async_copy(sketch_hbm, sketch, sem.at[0]),
        pltpu.make_async_copy(shift_hbm, shift, sem.at[1]),
        pltpu.make_async_copy(weight_hbm, weight, sem.at[2]),
    ]
    copies = [
        pltpu.make_async_copy(snap_hbm.at[f], snap.at[f], snap_sem.at[f]) for f in range(FIELDS)
    ]
    for copy in first + copies:
        copy.start()
    me = lax.axis_index("tm")
    y, core = me // 2, me % 2
    order = orders[0]
    filter_tables(
        table, [2 * (y ^ m) + (1 - core) for m in order] + [2 * (y ^ m) + core for m in order]
    )
    for copy in first:
        copy.wait()
    turned[...] = sketch[...].T
    each = FIELDS // len(orders)
    dot = functools.partial(
        lax.dot_general,
        dimension_numbers=(((1,), (1,)), ((), ())),
        preferred_element_type=jnp.float32,
    )

    def filtered(f, raw):
        high, low = split(raw)
        blur, slope = table[0], table[shift[f]]
        image = (dot(blur, high) + dot(blur, low)) + weight[f] * (
            dot(slope, high) + dot(slope, low)
        )
        n, i = divmod(f, each)
        for r, mask in enumerate(orders[n]):
            at = SHARE * order.index(mask)
            outs[2 * n][r, i] = image[at : at + SHARE]
            outs[2 * n + 1][r, i] = image[HALF + at : HALF + at + SHARE]

    held = None
    for g in range(0, FIELDS + GROUP, GROUP):
        if g < FIELDS:
            for f in range(g, g + GROUP):
                copies[f].wait()
            raws = [
                jnp.dot(turned[...], snap[f], preferred_element_type=jnp.float32)
                for f in range(g, g + GROUP)
            ]
        if held is not None:
            for k in range(GROUP):
                filtered(g - GROUP + k, held[k])
        held = raws


def sketch_call(snaps, sketch, dilation, weight, orders):
    out = jax.ShapeDtypeStruct((4, FIELDS // len(orders), SHARE, RANK), jnp.float32)
    hbm = pl.BlockSpec(memory_space=pltpu.HBM)
    vmem = pl.BlockSpec(memory_space=pltpu.VMEM)
    return pl.pallas_call(
        functools.partial(sketch_kernel, orders),
        in_specs=[hbm] * 4,
        out_specs=[vmem] * (2 * len(orders)),
        out_shape=[out] * (2 * len(orders)),
        scratch_shapes=[
            pltpu.VMEM((FIELDS, SNAP_DEV, PLANE), jnp.bfloat16),
            pltpu.VMEM((SNAP_DEV, RANK), jnp.bfloat16),
            pltpu.VMEM((RANK, SNAP_DEV), jnp.bfloat16),
            pltpu.VMEM((DILATIONS + 1, PLANE, PLANE), jnp.bfloat16),
            pltpu.SMEM((FIELDS,), jnp.int32),
            pltpu.SMEM((FIELDS,), jnp.float32),
            pltpu.SemaphoreType.DMA((FIELDS,)),
            pltpu.SemaphoreType.DMA((3,)),
        ],
        compiler_params=pltpu.CompilerParams(vmem_limit_bytes=52 * 2**20),
    )(snaps, sketch, dilation, weight)


def panel_kernel(counts, volume_ref, *refs):
    parts, (panel_ref, gram_ref) = refs[:-2], refs[-2:]
    me, plane = lax.axis_index("tm"), lax.axis_index("space")
    row = lax.broadcasted_iota(jnp.int32, (SHARE, PLANE), 0)
    lane = lax.broadcasted_iota(jnp.int32, (SHARE, PLANE), 1)
    volume = jnp.broadcast_to(volume_ref[...], (SHARE, PLANE))
    mine = jnp.sum(jnp.where(lane == row + me * SHARE, volume, 0.0), axis=1, keepdims=True)
    root = jnp.broadcast_to(jnp.sqrt(mine), (SHARE, RANK))
    scaled = []
    at = 0
    for n, count in enumerate(counts):
        here, below, above = parts[3 * n : 3 * n + 3]
        for f in range(count):
            panel = 0.5 * here[f]
            panel = panel + jnp.where(plane > 0, 0.25 * below[f], 0.0)
            panel = panel + jnp.where(plane < NZ - 1, 0.25 * above[f], 0.0)
            panel_ref[at] = panel
            scaled.append(panel * root)
            at += 1
    rows = jnp.concatenate(scaled, axis=0)
    gram = lax.dot_general(
        rows,
        rows,
        (((0,), (0,)), ((), ())),
        precision=EXACT,
        preferred_element_type=jnp.float32,
    )
    gram = gram * (1.0 / ROWS)
    gram_ref[:HALF] = gram[HALF:, :HALF]
    row = lax.broadcasted_iota(jnp.int32, (HALF, HALF), 0)
    lane = lax.broadcasted_iota(jnp.int32, (HALF, HALF), 1)
    last = gram[HALF:, HALF:]
    gram_ref[HALF : 2 * HALF] = jnp.where(row >= lane, gram[:HALF, :HALF], last)
    diag = jnp.sum(jnp.where(row == lane, last, 0.0), axis=0, keepdims=True)
    gram_ref[2 * HALF :] = jnp.broadcast_to(diag, (16, HALF))


def panel_call(volume, counts, parts):
    vmem = pl.BlockSpec(memory_space=pltpu.VMEM)
    return pl.pallas_call(
        functools.partial(panel_kernel, counts),
        in_specs=[vmem] * (1 + len(parts)),
        out_specs=[vmem, vmem],
        out_shape=[
            jax.ShapeDtypeStruct((FIELDS, SHARE, RANK), jnp.float32),
            jax.ShapeDtypeStruct((272, HALF), jnp.float32),
        ],
        compiler_params=pltpu.CompilerParams(vmem_limit_bytes=16 * 2**20),
    )(volume, *parts)


def total(terms):
    terms = list(terms)
    while len(terms) > 1:
        terms = [a + b for a, b in zip(terms[::2], terms[1::2])] + (
            terms[-1:] if len(terms) % 2 else []
        )
    return terms[0]


def factor(rows):
    shape = (8, HALF)
    sub = lax.broadcasted_iota(jnp.int32, shape, 0)
    lane = lax.broadcasted_iota(jnp.int32, shape, 1)
    rows = list(rows)
    count = len(rows)
    uppers, lowers = [], []
    at = [sub == j for j in range(8)]

    def column(x, j):
        return jnp.broadcast_to(x[:, j : j + 1], shape)

    def row_of(x, i):
        return jnp.broadcast_to(x[i : i + 1, :], shape)

    for s in range(count):
        here = rows[s]
        there = jnp.where(lane == sub + 8 * s, 1.0, 0.0)
        inside = (lane >= 8 * s) & (lane < 8 * s + 8)
        cols = [column(here, 8 * s + m) for m in range(8)]
        upper = lower = jnp.zeros(shape, jnp.float32)
        for j in range(0, 8, 2):
            p, q = cols[j], cols[j + 1]
            a, b, c = row_of(p, j), row_of(q, j), row_of(q, j + 1)
            det = a * c - b * b
            inv_det = 1.0 / det
            inv_a = 1.0 / a
            root_a, root_c = lax.rsqrt(a), lax.rsqrt(det * inv_a)
            slope = b * inv_a

            def eliminate(x, kept=None):
                x0, x1 = row_of(x, j), row_of(x, j + 1)
                y0 = (c * x0 - b * x1) * inv_det
                y1 = (a * x1 - b * x0) * inv_det
                new = jnp.where(at[j], y0, jnp.where(at[j + 1], y1, x - p * y0 - q * y1))
                if kept is None:
                    return new
                second = (x1 - slope * x0) * root_c
                return new, jnp.where(at[j], x0 * root_a, jnp.where(at[j + 1], second, kept))

            here, upper = eliminate(here, upper)
            there, lower = eliminate(there, lower)
            for m in range(j + 2, 8):
                cols[m] = eliminate(cols[m])
        uppers.append(jnp.where(lane >= sub + 8 * s, upper, 0.0))
        lowers.append(jnp.where(inside, lower, jnp.where(lane < 8 * s, upper, 0.0)))
        if s + 1 == count:
            break
        solved = jnp.where(inside, there, here)
        solved_rows = [row_of(solved, m) for m in range(8)]
        for t in range(s + 1, count):
            weights = [column(rows[t], 8 * s + m) for m in range(8)]
            rows[t] = jnp.where(inside, 0.0, rows[t]) - total(
                weights[m] * solved_rows[m] for m in range(8)
            )
    return uppers, lowers


def basis_kernel(gram_ref, panel_ref, basis_ref, upper_ref):
    row = lax.broadcasted_iota(jnp.int32, (HALF, HALF), 0)
    lane = lax.broadcasted_iota(jnp.int32, (HALF, HALF), 1)
    cross = gram_ref[:HALF]
    mixed = gram_ref[HALF : 2 * HALF]
    turned = mixed.T
    first = jnp.where(row >= lane, mixed, turned)
    diag = jnp.broadcast_to(gram_ref[2 * HALF : 2 * HALF + 1, :], (HALF, HALF))
    last = jnp.where(row < lane, mixed, jnp.where(row > lane, turned, diag))
    cells = FIELDS * SHARE

    def dot(a, b, da, db):
        return lax.dot_general(
            a,
            b,
            (((da,), (db,)), ((), ())),
            precision=EXACT,
            preferred_element_type=jnp.float32,
        )

    def put(x, h):
        for f in range(FIELDS):
            basis_ref[pl.ds(2 * f + h, SHARE, stride=2 * FIELDS), :] = x[
                SHARE * f : SHARE * f + SHARE
            ]

    groups = range(HALF // 8)
    uppers, lowers = factor([first[8 * t : 8 * t + 8] for t in groups])
    low_a = jnp.concatenate(lowers, axis=0)
    upper_ref[:HALF, :HALF] = jnp.concatenate(uppers, axis=0)
    side = dot(low_a, cross, 1, 1)
    last = last - dot(side, side, 0, 0)
    upper_ref[:HALF, HALF:] = side
    upper_ref[HALF:, :HALF] = jnp.zeros((HALF, HALF), jnp.float32)
    basis_a = dot(panel_ref[:, :, :HALF].reshape(cells, HALF), low_a, 1, 1)
    rest = panel_ref[:, :, HALF:].reshape(cells, HALF) - dot(basis_a, side, 1, 0)
    put(basis_a, 0)
    uppers, lowers = factor([last[8 * t : 8 * t + 8] for t in groups])
    low_b = jnp.concatenate(lowers, axis=0)
    upper_ref[HALF:, HALF:] = jnp.concatenate(uppers, axis=0)
    put(dot(rest, low_b, 1, 1), 1)


def basis_call(gram, panel):
    vmem = pl.BlockSpec(memory_space=pltpu.VMEM)
    basis, upper = pl.pallas_call(
        basis_kernel,
        in_specs=[vmem, vmem],
        out_specs=[vmem, vmem],
        out_shape=[
            jax.ShapeDtypeStruct((SHARE * FIELDS * 2, HALF), jnp.float32),
            jax.ShapeDtypeStruct((RANK, RANK), jnp.float32),
        ],
        compiler_params=pltpu.CompilerParams(vmem_limit_bytes=32 * 2**20),
    )(gram, panel)
    return basis.reshape(SHARE, FIELDS, 1, RANK), upper


def swap(x, axis, mask):
    return lax.ppermute(x, axis, [(i, i ^ mask) for i in range(lax.axis_size(axis))])


def ring(x, axis, step):
    n = lax.axis_size(axis)
    return lax.ppermute(x, axis, [(i, (i + step) % n) for i in range(n)])


def sum_over_tm(send, keep, near, far):
    got = swap(send, "tm", 1)
    away = swap(keep[2:] + got[2:], "tm", 2 * near)
    near_part = swap((keep[1] + got[1]) + away[1], "tm", 2 * far)
    return ((keep[0] + got[0]) + away[0]) + near_part


def sum_over_all(gram):
    core = lax.axis_index("tm") % 2
    n = gram.shape[0] // 2
    mine = lax.dynamic_slice_in_dim(gram, core * n, n, 0)
    other = lax.dynamic_slice_in_dim(gram, (1 - core) * n, n, 0)
    mine = mine + swap(other, "tm", 1)
    for mask in (2, 6):
        mine = mine + swap(mine, "tm", mask)
    for mask in (8, 24, 1, 2, 7):
        mine = mine + swap(mine, "space", mask)
    other = swap(mine, "tm", 1)
    return jnp.where(
        core == 0, jnp.concatenate([mine, other], 0), jnp.concatenate([other, mine], 0)
    )


STEPS = ((1, 3), (3, 1), (1, 3), (3, 1))


def shards(snapshots, sketch, volume, grad_weight, dilation):
    snaps = jnp.transpose(snapshots[:, :, 0, :], (1, 0, 2))
    orders = [(0, far, near, near ^ far) for near, far in STEPS]
    images = sketch_call(snaps, sketch, dilation, grad_weight, orders)
    parts = []
    for n, (near, far) in enumerate(STEPS):
        image = sum_over_tm(images[2 * n], images[2 * n + 1], near, far)
        parts += [image, ring(image, "space", 1), ring(image, "space", -1)]
    panel, gram = panel_call(volume, [FIELDS // len(STEPS)] * len(STEPS), parts)
    gram = sum_over_all(gram)
    basis, upper = basis_call(gram, panel)
    return basis, upper


def solution(mesh):
    return jax.shard_map(
        shards,
        mesh=mesh,
        in_specs=(P("tm", None, "space", None), P("tm", None), P("space", None), P(), P()),
        out_specs=(P("tm", None, "space", None), P()),
        check_vma=False,
    )
```

time: 111 us -> 112 us (level)
  starting transfers between devices: 34.5 us -> 52.1 us
  Pallas kernels: 28 us -> 18.7 us
  waiting for transfers between devices: 41.8 us -> 33.1 us
  other arithmetic: 0.49 us -> 5.83 us
  local copies, waits for them, and re-layouts: 5.23 us -> 1.32 us
    ppermute x4 -> x8, starting transfers between devices: 11.2 us -> 22.7 us  [ring(): return lax.ppermute(x, axis, [(i, (i + step) % n) for i in range(n)])]
    ppermute x15 -> x21, waiting for transfers between devices: 38.8 us -> 31.1 us  [swap(): lax.ppermute(x, axis, [(i, i ^ mask) for i in range(lax.axis_size(axis))])]
    ppermute x15 -> x21, starting transfers between devices: 23.3 us -> 29.4 us  [swap(): lax.ppermute(x, axis, [(i, i ^ mask) for i in range(lax.axis_size(axis))])]
    add x6 -> x12, other arithmetic: 0.39 us -> 5.73 us  [the longest x4 1.96 us: sum_over_tm(): away = swap(keep[2:] + got[2:], 'tm', 2 * near)]
    pallas_call x1, Pallas kernels: 15.7 us -> 10.4 us  [basis_call(): pl.pallas_call(basis_kernel, in_specs=[vmem, vmem], out_specs=[vmem, vmem...]
    pallas_call x2 -> x1, Pallas kernels: 11.5 us -> 7.45 us  [sketch_call(): pl.pallas_call(functools.partial(sketch_kernel, orders), in_specs=[hbm] *...]
    unnamed x10 -> x6, local copies, waits for them, and re-layouts: 5.13 us -> 1.31 us
    ppermute x4 -> x8, waiting for transfers between devices: 3.06 us -> 2.03 us  [ring(): return lax.ppermute(x, axis, [(i, (i + step) % n) for i in range(n)])]
  transfers between devices with their start and end apart: 19 -> 29, of which waited for: 14 -> 15; matrix products, arithmetic and copies ran while one was open for 0% -> 5% of each run, Pallas kernels for 5% -> 0%
where the time goes in v2:
time: 112 us
  starting transfers between devices  52.1 us (47%)
  waiting for transfers between devices  33.1 us (30%)
  Pallas kernels  18.7 us (17%)
  other arithmetic  5.83 us (5%)
  local copies, waits for them, and re-layouts  1.32 us (1%)
    ppermute x21, waiting for transfers between devices, swap(): lax.ppermute(x, axis, [(i, i ^ mask) for i in range(lax.axis_size(axis))])  31.1 us
    ppermute x21, starting transfers between devices, swap(): lax.ppermute(x, axis, [(i, i ^ mask) for i in range(lax.axis_size(axis))])  29.4 us
    ppermute x8, starting transfers between devices, ring(): return lax.ppermute(x, axis, [(i, (i + step) % n) for i in range(n)])  22.7 us
    pallas_call x1, Pallas kernels, basis_call(): pl.pallas_call(basis_kernel, in_specs=[vmem, vmem], out_specs=[vmem, vmem...  10.4 us
    pallas_call x1, Pallas kernels, sketch_call(): pl.pallas_call(functools.partial(sketch_kernel, orders), in_specs=[hbm] *...  7.45 us
  transfers between devices with their start and end apart: 29, of which 15 were waited for; matrix products, arithmetic and copies ran while one was open for 5% of the time, Pallas kernels for 0%

profile of v2, /device:TPU:1, one launch (start us, length us, event | category | flops | bytes accessed | tf_op | source)
XLA Modules:
  0.0 111.9 jit_solution(17784788693004533084)
XLA Ops:
  1.9 7.5 %shard_map.68 = (f32[4,3,32,256]{3,2,1,0:T(8,128)S(1)}, f32[4,3,32,256]{3,2,1,0:T(8,128)S(1)}, f32[4,3,32,256]{3,2,1,0:T(8,128)S(1)}, f32[4,3,32,256]{3,2,1,0:T(...) custom-call(bf16[12,1024,256]{2,1,0:T(8,128)(2,1)} %bitcast.28, ...), custom_call_target="tpu_custom_call" | custom-call | tf_op jit(solution)/shard_map/pallas_call | solution.py:118
  9.4 3.3 %collective-permute-start.15 = (f32[4,3,32,256]{3,2,1,0:T(8,128)}, f32[4,3,32,256]{3,2,1,0:T(8,128)S(1)}, u32[]{:S(2)}, u32[]{:S(2)}) collective-permute-start(f32[4,3,32,256]{3,2,1,0:T(8,128)} %get-tuple-element.21), channel_id=1, source_target_pairs={{0,32},{32,0},{64,96},{96,64},{128,160},{160,128},{192,224},{224,1... | collective-permute-start | bytes 1179656 | tf_op jit(solution)/shard_map/ppermute | solution.py:314
  17.4 1.8 %collective-permute-start.6 = (f32[2,3,32,256]{3,2,1,0:T(8,128)S(1)}, f32[2,3,32,256]{3,2,1,0:T(8,128)S(1)}, u32[]{:S(2)}, u32[]{:S(2)}) collective-permute-start(f32[2,3,32,256]{3,2,1,0:T(8,128)S(1)} %slice_add_fusion.2), channel_id=1, source_target_pairs={{0,192},{32,224},{64,128},{96,160},{128,64},{160,96},{192,0},{224,... | collective-permute-start | bytes 589832 | tf_op jit(solution)/shard_map/ppermute | solution.py:314
  20.2 2.5 %collective-permute-done.16 = f32[2,3,32,256]{3,2,1,0:T(8,128)S(1)} collective-permute-done((f32[2,3,32,256]{3,2,1,0:T(8,128)S(1)}, f32[2,3,32,256]{3,2,1,0:T(8,128)S(1)}, u32[]{:S(2)}, u32[]{:S(2)}) %collective-permute-start.16) | collective-permute-done | bytes 196640 | tf_op jit(solution)/shard_map/ppermute | solution.py:314
  24.6 1.2 %collective-permute-start.12 = (f32[3,32,256]{2,1,0:T(8,128)S(1)}, f32[3,32,256]{2,1,0:T(8,128)S(1)}, u32[]{:S(2)}, u32[]{:S(2)}) collective-permute-start(f32[3,32,256]{2,1,0:T(8,128)S(1)} %fusion.3), channel_id=1, source_target_pairs={{0,192},{32,224},{64,128},{96,160},{128,64},{160,96},{192,0},{224,... | collective-permute-start | bytes 294920 | tf_op jit(solution)/shard_map/ppermute | solution.py:314
  27.4 1.8 %collective-permute-start.2 = (f32[3,32,256]{2,1,0:T(8,128)S(1)}, f32[3,32,256]{2,1,0:T(8,128)S(1)}, u32[]{:S(2)}, u32[]{:S(2)}) collective-permute-start(f32[3,32,256]{2,1,0:T(8,128)S(1)} %fusion.9), channel_id=1, source_target_pairs={{0,192},{32,224},{64,128},{96,160},{128,64},{160,96},{192,0},{224,... | collective-permute-start | bytes 294920 | tf_op jit(solution)/shard_map/ppermute | solution.py:314
  30.4 1.7 %collective-permute-start.18 = (f32[3,32,256]{2,1,0:T(8,128)S(1)}, f32[3,32,256]{2,1,0:T(8,128)S(1)}, u32[]{:S(2)}, u32[]{:S(2)}) collective-permute-start(f32[3,32,256]{2,1,0:T(8,128)S(1)} %fusion.2.refs_9_), channel_id=1, source_target_pairs={{0,1},{1,2},{2,3},{3,4},{4,5},{5,6},{6,7},{7,8},{8,9},{9,10},{10,1... | collective-permute-start | bytes 294920 | tf_op jit(solution)/shard_map/ppermute | solution.py:319
  32.1 6.4 %collective-permute-start.19 = (f32[3,32,256]{2,1,0:T(8,128)S(1)}, f32[3,32,256]{2,1,0:T(8,128)S(1)}, u32[]{:S(2)}, u32[]{:S(2)}) collective-permute-start(f32[3,32,256]{2,1,0:T(8,128)S(1)} %fusion.2.refs_9_), channel_id=1, source_target_pairs={{0,31},{1,0},{2,1},{3,2},{4,3},{5,4},{6,5},{7,6},{8,7},{9,8},{10,9... | collective-permute-start | bytes 294920 | tf_op jit(solution)/shard_map/ppermute | solution.py:319
  39.6 4.8 %collective-permute-start.14 = (f32[3,32,256]{2,1,0:T(8,128)S(1)}, f32[3,32,256]{2,1,0:T(8,128)S(1)}, u32[]{:S(2)}, u32[]{:S(2)}) collective-permute-start(f32[3,32,256]{2,1,0:T(8,128)S(1)} %fusion.5.refs_6_), channel_id=1, source_target_pairs={{0,31},{1,0},{2,1},{3,2},{4,3},{5,4},{6,5},{7,6},{8,7},{9,8},{10,9... | collective-permute-start | bytes 294920 | tf_op jit(solution)/shard_map/ppermute | solution.py:319
  44.5 4.8 %collective-permute-start.9 = (f32[3,32,256]{2,1,0:T(8,128)S(1)}, f32[3,32,256]{2,1,0:T(8,128)S(1)}, u32[]{:S(2)}, u32[]{:S(2)}) collective-permute-start(f32[3,32,256]{2,1,0:T(8,128)S(1)} %fusion.8.refs_3_), channel_id=1, source_target_pairs={{0,31},{1,0},{2,1},{3,2},{4,3},{5,4},{6,5},{7,6},{8,7},{9,8},{10,9... | collective-permute-start | bytes 294920 | tf_op jit(solution)/shard_map/ppermute | solution.py:319
  49.4 4.8 %collective-permute-start.4 = (f32[3,32,256]{2,1,0:T(8,128)S(1)}, f32[3,32,256]{2,1,0:T(8,128)S(1)}, u32[]{:S(2)}, u32[]{:S(2)}) collective-permute-start(f32[3,32,256]{2,1,0:T(8,128)S(1)} %fusion.11.refs_0_), channel_id=1, source_target_pairs={{0,31},{1,0},{2,1},{3,2},{4,3},{5,4},{6,5},{7,6},{8,7},{9,8},{10,9... | collective-permute-start | bytes 294920 | tf_op jit(solution)/shard_map/ppermute | solution.py:319
  54.1 2.0 %collective-permute-done.3.refs_1_ = f32[3,32,256]{2,1,0:T(8,128)S(1)} collective-permute-done((f32[3,32,256]{2,1,0:T(8,128)S(1)}, f32[3,32,256]{2,1,0:T(8,128)S(1)}, u32[]{:S(2)}, u32[]{:S(2)}) %collective-permute-start.3) | collective-permute-done | bytes 98336 | tf_op jit(solution)/shard_map/ppermute | solution.py:319
  57.0 5.2 %collective-permute-start.20 = (f32[136,128]{1,0:T(8,128)S(1)}, f32[136,128]{1,0:T(8,128)S(1)}, u32[]{:S(2)}, u32[]{:S(2)}) collective-permute-start(f32[136,128]{1,0:T(8,128)S(1)} %constant_dynamic-slice_fusion), channel_id=1, source_target_pairs={{0,32},{32,0},{64,96},{96,64},{128,160},{160,128},{192,224},{224,1... | collective-permute-start | bytes 208904 | tf_op jit(solution)/shard_map/ppermute | solution.py:314
  63.2 3.1 %collective-permute-done.21 = f32[136,128]{1,0:T(8,128)S(1)} collective-permute-done((f32[136,128]{1,0:T(8,128)S(1)}, f32[136,128]{1,0:T(8,128)S(1)}, u32[]{:S(2)}, u32[]{:S(2)}) %collective-permute-start.21) | collective-permute-done | bytes 69664 | tf_op jit(solution)/shard_map/ppermute | solution.py:314
  66.3 1.1 %collective-permute-start.22 = (f32[136,128]{1,0:T(8,128)S(1)}, f32[136,128]{1,0:T(8,128)S(1)}, u32[]{:S(2)}, u32[]{:S(2)}) collective-permute-start(f32[136,128]{1,0:T(8,128)S(1)} %add.174), channel_id=1, source_target_pairs={{0,192},{32,224},{64,128},{96,160},{128,64},{160,96},{192,0},{224,... | collective-permute-start | bytes 208904 | tf_op jit(solution)/shard_map/ppermute | solution.py:314
  67.5 3.3 %collective-permute-done.22 = f32[136,128]{1,0:T(8,128)S(1)} collective-permute-done((f32[136,128]{1,0:T(8,128)S(1)}, f32[136,128]{1,0:T(8,128)S(1)}, u32[]{:S(2)}, u32[]{:S(2)}) %collective-permute-start.22) | collective-permute-done | bytes 69664 | tf_op jit(solution)/shard_map/ppermute | solution.py:314
  70.9 3.1 %collective-permute-done.23 = f32[136,128]{1,0:T(8,128)S(1)} collective-permute-done((f32[136,128]{1,0:T(8,128)S(1)}, f32[136,128]{1,0:T(8,128)S(1)}, u32[]{:S(2)}, u32[]{:S(2)}) %collective-permute-start.23) | collective-permute-done | bytes 69664 | tf_op jit(solution)/shard_map/ppermute | solution.py:314
  74.2 4.4 %collective-permute-done.24 = f32[136,128]{1,0:T(8,128)S(1)} collective-permute-done((f32[136,128]{1,0:T(8,128)S(1)}, f32[136,128]{1,0:T(8,128)S(1)}, u32[]{:S(2)}, u32[]{:S(2)}) %collective-permute-start.24) | collective-permute-done | bytes 69664 | tf_op jit(solution)/shard_map/ppermute | solution.py:314
  78.6 3.1 %collective-permute-done.25 = f32[136,128]{1,0:T(8,128)S(1)} collective-permute-done((f32[136,128]{1,0:T(8,128)S(1)}, f32[136,128]{1,0:T(8,128)S(1)}, u32[]{:S(2)}, u32[]{:S(2)}) %collective-permute-start.25) | collective-permute-done | bytes 69664 | tf_op jit(solution)/shard_map/ppermute | solution.py:314
  81.9 4.5 %collective-permute-done.26 = f32[136,128]{1,0:T(8,128)S(1)} collective-permute-done((f32[136,128]{1,0:T(8,128)S(1)}, f32[136,128]{1,0:T(8,128)S(1)}, u32[]{:S(2)}, u32[]{:S(2)}) %collective-permute-start.26) | collective-permute-done | bytes 69664 | tf_op jit(solution)/shard_map/ppermute | solution.py:314
  86.4 2.8 %collective-permute-start.27 = (f32[136,128]{1,0:T(8,128)S(1)}, f32[136,128]{1,0:T(8,128)S(1)}, u32[]{:S(2)}, u32[]{:S(2)}) collective-permute-start(f32[136,128]{1,0:T(8,128)S(1)} %add.179), channel_id=1, source_target_pairs={{0,7},{1,6},{2,5},{3,4},{4,3},{5,2},{6,1},{7,0},{8,15},{9,14},{10,... | collective-permute-start | bytes 208904 | tf_op jit(solution)/shard_map/ppermute | solution.py:314
  89.2 2.4 %collective-permute-done.27 = f32[136,128]{1,0:T(8,128)S(1)} collective-permute-done((f32[136,128]{1,0:T(8,128)S(1)}, f32[136,128]{1,0:T(8,128)S(1)}, u32[]{:S(2)}, u32[]{:S(2)}) %collective-permute-start.27) | collective-permute-done | bytes 69664 | tf_op jit(solution)/shard_map/ppermute | solution.py:314
  91.7 8.8 %collective-permute-start.28 = (f32[136,128]{1,0:T(8,128)S(1)}, f32[136,128]{1,0:T(8,128)S(1)}, u32[]{:S(2)}, u32[]{:S(2)}) collective-permute-start(f32[136,128]{1,0:T(8,128)S(1)} %add.180), channel_id=1, source_target_pairs={{0,32},{32,0},{64,96},{96,64},{128,160},{160,128},{192,224},{224,1... | collective-permute-start | bytes 208904 | tf_op jit(solution)/shard_map/ppermute | solution.py:314
  101.4 10.4 %shard_map.70 = (f32[768,128]{1,0:T(8,128)}, f32[256,256]{1,0:T(8,128)}) custom-call(f32[272,128]{1,0:T(8,128)S(1)} %maximum_select_fusion.gram_ref, f32[12,32,256]{2,1,0:T(8,128)S(1)} %get-tuple-element.23.panel_ref), custom_call_target="tpu_custom_call" | custom-call | tf_op jit(solution)/shard_map/pallas_call | solution.py:300
  (65 shorter events, 16.0 us)
Async XLA Ops:
  9.4 4.9 %collective-permute-start.15 = (f32[4,3,32,256]{3,2,1,0:T(8,128)}, f32[4,3,32,256]{3,2,1,0:T(8,128)S(1)}, u32[]{:S(2)}, u32[]{:S(2)}) collective-permute-start(f32[4,3,32,256]{3,2,1,0:T(8,128)} %get-tuple-element.21), channel_id=1, source_target_pairs={{0,32},{32,0},{64,96},{96,64},{128,160},{160,128},{192,224},{224,1... | collective-permute-start | bytes 1179656 | tf_op jit(solution)/shard_map/ppermute | solution.py:314
  12.8 4.6 %collective-permute-start.5 = (f32[4,3,32,256]{3,2,1,0:T(8,128)S(1)}, f32[4,3,32,256]{3,2,1,0:T(8,128)S(1)}, u32[]{:S(2)}, u32[]{:S(2)}) collective-permute-start(f32[4,3,32,256]{3,2,1,0:T(8,128)S(1)} %get-tuple-element.17), channel_id=1, source_target_pairs={{0,32},{32,0},{64,96},{96,64},{128,160},{160,128},{192,224},{224,1... | collective-permute-start | bytes 1179656 | tf_op jit(solution)/shard_map/ppermute | solution.py:314
  13.2 6.0 %collective-permute-start = (f32[4,3,32,256]{3,2,1,0:T(8,128)S(1)}, f32[4,3,32,256]{3,2,1,0:T(8,128)S(1)}, u32[]{:S(2)}, u32[]{:S(2)}) collective-permute-start(f32[4,3,32,256]{3,2,1,0:T(8,128)S(1)} %get-tuple-element.15), channel_id=1, source_target_pairs={{0,32},{32,0},{64,96},{96,64},{128,160},{160,128},{192,224},{224,1... | collective-permute-start | bytes 1179656 | tf_op jit(solution)/shard_map/ppermute | solution.py:314
  15.2 7.4 %collective-permute-start.16 = (f32[2,3,32,256]{3,2,1,0:T(8,128)S(1)}, f32[2,3,32,256]{3,2,1,0:T(8,128)S(1)}, u32[]{:S(2)}, u32[]{:S(2)}) collective-permute-start(f32[2,3,32,256]{3,2,1,0:T(8,128)S(1)} %slice_add_fusion), channel_id=1, source_target_pairs={{0,192},{32,224},{64,128},{96,160},{128,64},{160,96},{192,0},{224,... | collective-permute-start | bytes 589832 | tf_op jit(solution)/shard_map/ppermute | solution.py:314
  17.3 6.4 %collective-permute-start.11 = (f32[2,3,32,256]{3,2,1,0:T(8,128)S(1)}, f32[2,3,32,256]{3,2,1,0:T(8,128)S(1)}, u32[]{:S(2)}, u32[]{:S(2)}) collective-permute-start(f32[2,3,32,256]{3,2,1,0:T(8,128)S(1)} %slice_add_fusion.1), channel_id=1, source_target_pairs={{0,64},{32,96},{64,0},{96,32},{128,192},{160,224},{192,128},{224,1... | collective-permute-start | bytes 589832 | tf_op jit(solution)/shard_map/ppermute | solution.py:314
  17.4 9.4 %collective-permute-start.6 = (f32[2,3,32,256]{3,2,1,0:T(8,128)S(1)}, f32[2,3,32,256]{3,2,1,0:T(8,128)S(1)}, u32[]{:S(2)}, u32[]{:S(2)}) collective-permute-start(f32[2,3,32,256]{3,2,1,0:T(8,128)S(1)} %slice_add_fusion.2), channel_id=1, source_target_pairs={{0,192},{32,224},{64,128},{96,160},{128,64},{160,96},{192,0},{224,... | collective-permute-start | bytes 589832 | tf_op jit(solution)/shard_map/ppermute | solution.py:314
  19.2 8.1 %collective-permute-start.1 = (f32[2,3,32,256]{3,2,1,0:T(8,128)S(1)}, f32[2,3,32,256]{3,2,1,0:T(8,128)S(1)}, u32[]{:S(2)}, u32[]{:S(2)}) collective-permute-start(f32[2,3,32,256]{3,2,1,0:T(8,128)S(1)} %slice_add_fusion.3), channel_id=1, source_target_pairs={{0,64},{32,96},{64,0},{96,32},{128,192},{160,224},{192,128},{224,1... | collective-permute-start | bytes 589832 | tf_op jit(solution)/shard_map/ppermute | solution.py:314
  23.6 5.9 %collective-permute-start.17 = (f32[3,32,256]{2,1,0:T(8,128)S(1)}, f32[3,32,256]{2,1,0:T(8,128)S(1)}, u32[]{:S(2)}, u32[]{:S(2)}) collective-permute-start(f32[3,32,256]{2,1,0:T(8,128)S(1)} %fusion), channel_id=1, source_target_pairs={{0,64},{32,96},{64,0},{96,32},{128,192},{160,224},{192,128},{224,1... | collective-permute-start | bytes 294920 | tf_op jit(solution)/shard_map/ppermute | solution.py:314
  24.6 13.9 %collective-permute-start.12 = (f32[3,32,256]{2,1,0:T(8,128)S(1)}, f32[3,32,256]{2,1,0:T(8,128)S(1)}, u32[]{:S(2)}, u32[]{:S(2)}) collective-permute-start(f32[3,32,256]{2,1,0:T(8,128)S(1)} %fusion.3), channel_id=1, source_target_pairs={{0,192},{32,224},{64,128},{96,160},{128,64},{160,96},{192,0},{224,... | collective-permute-start | bytes 294920 | tf_op jit(solution)/shard_map/ppermute | solution.py:314
  26.9 12.7 %collective-permute-start.7 = (f32[3,32,256]{2,1,0:T(8,128)S(1)}, f32[3,32,256]{2,1,0:T(8,128)S(1)}, u32[]{:S(2)}, u32[]{:S(2)}) collective-permute-start(f32[3,32,256]{2,1,0:T(8,128)S(1)} %fusion.6), channel_id=1, source_target_pairs={{0,64},{32,96},{64,0},{96,32},{128,192},{160,224},{192,128},{224,1... | collective-permute-start | bytes 294920 | tf_op jit(solution)/shard_map/ppermute | solution.py:314
  27.4 16.9 %collective-permute-start.2 = (f32[3,32,256]{2,1,0:T(8,128)S(1)}, f32[3,32,256]{2,1,0:T(8,128)S(1)}, u32[]{:S(2)}, u32[]{:S(2)}) collective-permute-start(f32[3,32,256]{2,1,0:T(8,128)S(1)} %fusion.9), channel_id=1, source_target_pairs={{0,192},{32,224},{64,128},{96,160},{128,64},{160,96},{192,0},{224,... | collective-permute-start | bytes 294920 | tf_op jit(solution)/shard_map/ppermute | solution.py:314
  30.4 14.1 %collective-permute-start.18 = (f32[3,32,256]{2,1,0:T(8,128)S(1)}, f32[3,32,256]{2,1,0:T(8,128)S(1)}, u32[]{:S(2)}, u32[]{:S(2)}) collective-permute-start(f32[3,32,256]{2,1,0:T(8,128)S(1)} %fusion.2.refs_9_), channel_id=1, source_target_pairs={{0,1},{1,2},{2,3},{3,4},{4,5},{5,6},{6,7},{7,8},{8,9},{9,10},{10,1... | collective-permute-start | bytes 294920 | tf_op jit(solution)/shard_map/ppermute | solution.py:319
  32.1 17.2 %collective-permute-start.19 = (f32[3,32,256]{2,1,0:T(8,128)S(1)}, f32[3,32,256]{2,1,0:T(8,128)S(1)}, u32[]{:S(2)}, u32[]{:S(2)}) collective-permute-start(f32[3,32,256]{2,1,0:T(8,128)S(1)} %fusion.2.refs_9_), channel_id=1, source_target_pairs={{0,31},{1,0},{2,1},{3,2},{4,3},{5,4},{6,5},{7,6},{8,7},{9,8},{10,9... | collective-permute-start | bytes 294920 | tf_op jit(solution)/shard_map/ppermute | solution.py:319
  39.5 9.9 %collective-permute-start.13 = (f32[3,32,256]{2,1,0:T(8,128)S(1)}, f32[3,32,256]{2,1,0:T(8,128)S(1)}, u32[]{:S(2)}, u32[]{:S(2)}) collective-permute-start(f32[3,32,256]{2,1,0:T(8,128)S(1)} %fusion.5.refs_6_), channel_id=1, source_target_pairs={{0,1},{1,2},{2,3},{3,4},{4,5},{5,6},{6,7},{7,8},{8,9},{9,10},{10,1... | collective-permute-start | bytes 294920 | tf_op jit(solution)/shard_map/ppermute | solution.py:319
  39.6 14.6 %collective-permute-start.14 = (f32[3,32,256]{2,1,0:T(8,128)S(1)}, f32[3,32,256]{2,1,0:T(8,128)S(1)}, u32[]{:S(2)}, u32[]{:S(2)}) collective-permute-start(f32[3,32,256]{2,1,0:T(8,128)S(1)} %fusion.5.refs_6_), channel_id=1, source_target_pairs={{0,31},{1,0},{2,1},{3,2},{4,3},{5,4},{6,5},{7,6},{8,7},{9,8},{10,9... | collective-permute-start | bytes 294920 | tf_op jit(solution)/shard_map/ppermute | solution.py:319
  44.4 9.8 %collective-permute-start.8 = (f32[3,32,256]{2,1,0:T(8,128)S(1)}, f32[3,32,256]{2,1,0:T(8,128)S(1)}, u32[]{:S(2)}, u32[]{:S(2)}) collective-permute-start(f32[3,32,256]{2,1,0:T(8,128)S(1)} %fusion.8.refs_3_), channel_id=1, source_target_pairs={{0,1},{1,2},{2,3},{3,4},{4,5},{5,6},{6,7},{7,8},{8,9},{9,10},{10,1... | collective-permute-start | bytes 294920 | tf_op jit(solution)/shard_map/ppermute | solution.py:319
  44.5 9.6 %collective-permute-start.9 = (f32[3,32,256]{2,1,0:T(8,128)S(1)}, f32[3,32,256]{2,1,0:T(8,128)S(1)}, u32[]{:S(2)}, u32[]{:S(2)}) collective-permute-start(f32[3,32,256]{2,1,0:T(8,128)S(1)} %fusion.8.refs_3_), channel_id=1, source_target_pairs={{0,31},{1,0},{2,1},{3,2},{4,3},{5,4},{6,5},{7,6},{8,7},{9,8},{10,9... | collective-permute-start | bytes 294920 | tf_op jit(solution)/shard_map/ppermute | solution.py:319
  49.3 6.8 %collective-permute-start.3 = (f32[3,32,256]{2,1,0:T(8,128)S(1)}, f32[3,32,256]{2,1,0:T(8,128)S(1)}, u32[]{:S(2)}, u32[]{:S(2)}) collective-permute-start(f32[3,32,256]{2,1,0:T(8,128)S(1)} %fusion.11.refs_0_), channel_id=1, source_target_pairs={{0,1},{1,2},{2,3},{3,4},{4,5},{5,6},{6,7},{7,8},{8,9},{9,10},{10,1... | collective-permute-start | bytes 294920 | tf_op jit(solution)/shard_map/ppermute | solution.py:319
  49.4 6.8 %collective-permute-start.4 = (f32[3,32,256]{2,1,0:T(8,128)S(1)}, f32[3,32,256]{2,1,0:T(8,128)S(1)}, u32[]{:S(2)}, u32[]{:S(2)}) collective-permute-start(f32[3,32,256]{2,1,0:T(8,128)S(1)} %fusion.11.refs_0_), channel_id=1, source_target_pairs={{0,31},{1,0},{2,1},{3,2},{4,3},{5,4},{6,5},{7,6},{8,7},{9,8},{10,9... | collective-permute-start | bytes 294920 | tf_op jit(solution)/shard_map/ppermute | solution.py:319
  57.0 6.1 %collective-permute-start.20 = (f32[136,128]{1,0:T(8,128)S(1)}, f32[136,128]{1,0:T(8,128)S(1)}, u32[]{:S(2)}, u32[]{:S(2)}) collective-permute-start(f32[136,128]{1,0:T(8,128)S(1)} %constant_dynamic-slice_fusion), channel_id=1, source_target_pairs={{0,32},{32,0},{64,96},{96,64},{128,160},{160,128},{192,224},{224,1... | collective-permute-start | bytes 208904 | tf_op jit(solution)/shard_map/ppermute | solution.py:314
  66.3 4.5 %collective-permute-start.22 = (f32[136,128]{1,0:T(8,128)S(1)}, f32[136,128]{1,0:T(8,128)S(1)}, u32[]{:S(2)}, u32[]{:S(2)}) collective-permute-start(f32[136,128]{1,0:T(8,128)S(1)} %add.174), channel_id=1, source_target_pairs={{0,192},{32,224},{64,128},{96,160},{128,64},{160,96},{192,0},{224,... | collective-permute-start | bytes 208904 | tf_op jit(solution)/shard_map/ppermute | solution.py:314
  81.8 4.6 %collective-permute-start.26 = (f32[136,128]{1,0:T(8,128)S(1)}, f32[136,128]{1,0:T(8,128)S(1)}, u32[]{:S(2)}, u32[]{:S(2)}) collective-permute-start(f32[136,128]{1,0:T(8,128)S(1)} %add.178), channel_id=1, source_target_pairs={{0,2},{1,3},{2,0},{3,1},{4,6},{5,7},{6,4},{7,5},{8,10},{9,11},{10,... | collective-permute-start | bytes 208904 | tf_op jit(solution)/shard_map/ppermute | solution.py:314
  86.4 5.2 %collective-permute-start.27 = (f32[136,128]{1,0:T(8,128)S(1)}, f32[136,128]{1,0:T(8,128)S(1)}, u32[]{:S(2)}, u32[]{:S(2)}) collective-permute-start(f32[136,128]{1,0:T(8,128)S(1)} %add.179), channel_id=1, source_target_pairs={{0,7},{1,6},{2,5},{3,4},{4,3},{5,2},{6,1},{7,0},{8,15},{9,14},{10,... | collective-permute-start | bytes 208904 | tf_op jit(solution)/shard_map/ppermute | solution.py:314
  91.7 9.8 %collective-permute-start.28 = (f32[136,128]{1,0:T(8,128)S(1)}, f32[136,128]{1,0:T(8,128)S(1)}, u32[]{:S(2)}, u32[]{:S(2)}) collective-permute-start(f32[136,128]{1,0:T(8,128)S(1)} %add.180), channel_id=1, source_target_pairs={{0,32},{32,0},{64,96},{96,64},{128,160},{160,128},{192,224},{224,1... | collective-permute-start | bytes 208904 | tf_op jit(solution)/shard_map/ppermute | solution.py:314
  (8 other events, 73.3 us)

commit v3 on v2

--- a/solution.py
+++ b/solution.py
@@ -130,13 +130,13 @@
             pltpu.SemaphoreType.DMA((FIELDS,)),
             pltpu.SemaphoreType.DMA((3,)),
         ],
-        compiler_params=pltpu.CompilerParams(vmem_limit_bytes=52 * 2**20),
+        compiler_params=pltpu.CompilerParams(vmem_limit_bytes=49 * 2**20),
     )(snaps, sketch, dilation, weight)
 
 
 def panel_kernel(counts, volume_ref, *refs):
     parts, (panel_ref, gram_ref) = refs[:-2], refs[-2:]
-    me, plane = lax.axis_index("tm"), lax.axis_index("space")
+    me = lax.axis_index("tm")
     row = lax.broadcasted_iota(jnp.int32, (SHARE, PLANE), 0)
     lane = lax.broadcasted_iota(jnp.int32, (SHARE, PLANE), 1)
     volume = jnp.broadcast_to(volume_ref[...], (SHARE, PLANE))
@@ -145,11 +145,9 @@
     scaled = []
     at = 0
     for n, count in enumerate(counts):
-        here, below, above = parts[3 * n : 3 * n + 3]
+        here, one, other = parts[3 * n : 3 * n + 3]
         for f in range(count):
-            panel = 0.5 * here[f]
-            panel = panel + jnp.where(plane > 0, 0.25 * below[f], 0.0)
-            panel = panel + jnp.where(plane < NZ - 1, 0.25 * above[f], 0.0)
+            panel = 0.5 * here[f] + 0.25 * (one[f] + other[f])
             panel_ref[at] = panel
             scaled.append(panel * root)
             at += 1
@@ -314,46 +312,75 @@
     return lax.ppermute(x, axis, [(i, i ^ mask) for i in range(lax.axis_size(axis))])
 
 
-def ring(x, axis, step):
-    n = lax.axis_size(axis)
-    return lax.ppermute(x, axis, [(i, (i + step) % n) for i in range(n)])
+def swap_next(x):
+    n = lax.axis_size("space")
+    pairs = [(i, i + 1) for i in range(1, n - 1, 2)]
+    return lax.ppermute(x, "space", pairs + [(j, i) for i, j in pairs])
 
 
 def sum_over_tm(send, keep, near, far):
-    got = swap(send, "tm", 1)
-    away = swap(keep[2:] + got[2:], "tm", 2 * near)
-    near_part = swap((keep[1] + got[1]) + away[1], "tm", 2 * far)
-    return ((keep[0] + got[0]) + away[0]) + near_part
+    mine = keep + swap(send, "tm", 1)
+    mine = mine[:2] + swap(mine[2:], "tm", 2 * near)
+    return mine[0] + swap(mine[1], "tm", 2 * far)
+
+
+def parity(y, x, z):
+    return (y ^ x ^ z ^ (z >> 1)) & 1
+
+
+def span(masks):
+    out = []
+    for picks in range(1, 2 ** len(masks)):
+        mask = (0, 0, 0)
+        for i, part in enumerate(masks):
+            if picks >> i & 1:
+                mask = tuple(a ^ b for a, b in zip(mask, part))
+        out.append(mask)
+    return out
 
 
 def sum_over_all(gram):
-    core = lax.axis_index("tm") % 2
+    tm, space = lax.axis_index("tm"), lax.axis_index("space")
+    side = (tm & 1) ^ parity(tm >> 1, space >> 3, space & 7)
     n = gram.shape[0] // 2
-    mine = lax.dynamic_slice_in_dim(gram, core * n, n, 0)
-    other = lax.dynamic_slice_in_dim(gram, (1 - core) * n, n, 0)
+    mine = lax.dynamic_slice_in_dim(gram, side * n, n, 0)
+    other = lax.dynamic_slice_in_dim(gram, (1 - side) * n, n, 0)
     mine = mine + swap(other, "tm", 1)
-    for mask in (2, 6):
-        mine = mine + swap(mine, "tm", mask)
-    for mask in (8, 24, 1, 2, 7):
-        mine = mine + swap(mine, "space", mask)
+    for masks in GRAM_STEPS:
+        parts = []
+        for y, x, z in span(masks):
+            flip = (2 * y + parity(y, x, z)) * NZ + 8 * x + z
+            parts.append(swap(mine, ("tm", "space"), flip))
+        mine = mine + functools.reduce(jnp.add, parts)
     other = swap(mine, "tm", 1)
     return jnp.where(
-        core == 0, jnp.concatenate([mine, other], 0), jnp.concatenate([other, mine], 0)
+        side == 0, jnp.concatenate([mine, other], 0), jnp.concatenate([other, mine], 0)
     )
 
 
 STEPS = ((1, 3), (3, 1), (1, 3), (3, 1))
+JOIN = 2
+GRAM_STEPS = (
+    ((1, 0, 0), (0, 1, 0)),
+    ((3, 0, 0), (0, 3, 0)),
+    ((0, 0, 1), (0, 0, 2)),
+    ((0, 0, 6),),
+)
 
 
 def shards(snapshots, sketch, volume, grad_weight, dilation):
     snaps = jnp.transpose(snapshots[:, :, 0, :], (1, 0, 2))
     orders = [(0, far, near, near ^ far) for near, far in STEPS]
     images = sketch_call(snaps, sketch, dilation, grad_weight, orders)
+    summed = [
+        sum_over_tm(images[2 * n], images[2 * n + 1], near, far)
+        for n, (near, far) in enumerate(STEPS)
+    ]
     parts = []
-    for n, (near, far) in enumerate(STEPS):
-        image = sum_over_tm(images[2 * n], images[2 * n + 1], near, far)
-        parts += [image, ring(image, "space", 1), ring(image, "space", -1)]
-    panel, gram = panel_call(volume, [FIELDS // len(STEPS)] * len(STEPS), parts)
+    for n in range(0, len(summed), JOIN):
+        image = jnp.concatenate(summed[n : n + JOIN], 0)
+        parts += [image, swap(image, "space", 1), swap_next(image)]
+    panel, gram = panel_call(volume, [p.shape[0] for p in parts[::3]], parts)
     gram = sum_over_all(gram)
     basis, upper = basis_call(gram, panel)
     return basis, upper

time: 112 us -> 96.7 us (0.86)
  starting transfers between devices: 52.1 us -> 43.1 us
  other arithmetic: 5.83 us -> 0.53 us
  Pallas kernels: 18.7 us -> 16.7 us
  local copies, waits for them, and re-layouts: 1.32 us -> 2.46 us
    ppermute x8 -> x2, starting transfers between devices: 22.7 us -> 1.32 us  [swap_next(): return lax.ppermute(x, 'space', pairs + [(j, i) for i, j in pairs])]
    ppermute x21 -> x26, starting transfers between devices: 29.4 us -> 41.8 us  [swap(): lax.ppermute(x, axis, [(i, i ^ mask) for i in range(lax.axis_size(axis))])]
    add x19 -> x16, other arithmetic: 5.8 us -> 0.47 us  [the longest x4 0.21 us: sum_over_tm(): mine = keep + swap(send, 'tm', 1)]
    ppermute x8 -> x2, waiting for transfers between devices: 2.03 us -> 0.01 us  [swap_next(): return lax.ppermute(x, 'space', pairs + [(j, i) for i, j in pairs])]
    pallas_call x1, Pallas kernels: 7.45 us -> 5.46 us  [sketch_call(): pl.pallas_call(functools.partial(sketch_kernel, orders), in_specs=[hbm] *...]
    ppermute x21 -> x26, waiting for transfers between devices: 31.1 us -> 32.4 us  [swap(): lax.ppermute(x, axis, [(i, i ^ mask) for i in range(lax.axis_size(axis))])]
    unnamed x6 -> x8, local copies, waits for them, and re-layouts: 1.31 us -> 2.35 us
  transfers between devices with their start and end apart: 29 -> 28, of which waited for: 15 -> 17; matrix products, arithmetic and copies ran while one was open for 5% -> 1% of each run, Pallas kernels for 0% -> 0%
where the time goes in v3:
time: 96.7 us; the launch traced here: 96.1 us
  starting transfers between devices  43.1 us (45%)
  waiting for transfers between devices  32.4 us (34%)
  Pallas kernels  16.7 us (17%)
  local copies, waits for them, and re-layouts  2.46 us (3%)
    ppermute x26, starting transfers between devices, swap(): lax.ppermute(x, axis, [(i, i ^ mask) for i in range(lax.axis_size(axis))])  41.8 us
    ppermute x26, waiting for transfers between devices, swap(): lax.ppermute(x, axis, [(i, i ^ mask) for i in range(lax.axis_size(axis))])  32.4 us
    pallas_call x1, Pallas kernels, basis_call(): pl.pallas_call(basis_kernel, in_specs=[vmem, vmem], out_specs=[vmem, vmem...  10.4 us
    pallas_call x1, Pallas kernels, sketch_call(): pl.pallas_call(functools.partial(sketch_kernel, orders), in_specs=[hbm] *...  5.46 us
    unnamed x8, local copies, waits for them, and re-layouts  2.35 us
  transfers between devices with their start and end apart: 28, of which 17 were waited for; matrix products, arithmetic and copies ran while one was open for 1% of the time, Pallas kernels for 0%

profile of v3, /device:TPU:1, one launch (start us, length us, event | category | flops | bytes accessed | tf_op | source)
XLA Modules:
  0.0 96.1 jit_solution(13637000419088838047)
XLA Ops:
  3.0 5.5 %shard_map.68 = (f32[4,3,32,256]{3,2,1,0:T(8,128)S(1)}, f32[4,3,32,256]{3,2,1,0:T(8,128)S(1)}, f32[4,3,32,256]{3,2,1,0:T(8,128)S(1)}, f32[4,3,32,256]{3,2,1,0:T(...) custom-call(bf16[12,1024,256]{2,1,0:T(8,128)(2,1)} %bitcast.28, ...), custom_call_target="tpu_custom_call" | custom-call | tf_op jit(solution)/shard_map/pallas_call | solution.py:118
  8.5 3.3 %collective-permute-start.8 = (f32[4,3,32,256]{3,2,1,0:T(8,128)S(1)}, f32[4,3,32,256]{3,2,1,0:T(8,128)S(1)}, u32[]{:S(2)}, u32[]{:S(2)}) collective-permute-start(f32[4,3,32,256]{3,2,1,0:T(8,128)S(1)} %get-tuple-element.19), channel_id=1, source_target_pairs={{0,32},{32,0},{64,96},{96,64},{128,160},{160,128},{192,224},{224,1... | collective-permute-start | bytes 1179656 | tf_op jit(solution)/shard_map/ppermute | solution.py:312
  13.8 1.2 %collective-permute-start.12 = (f32[2,3,32,256]{3,2,1,0:T(8,128)S(1)}, f32[2,3,32,256]{3,2,1,0:T(8,128)S(1)}, u32[]{:S(2)}, u32[]{:S(2)}) collective-permute-start(f32[2,3,32,256]{3,2,1,0:T(8,128)S(1)} %slice.77), channel_id=1, source_target_pairs={{0,192},{32,224},{64,128},{96,160},{128,64},{160,96},{192,0},{224,... | collective-permute-start | bytes 589832 | tf_op jit(solution)/shard_map/ppermute | solution.py:312
  15.6 1.8 %collective-permute-start.4 = (f32[2,3,32,256]{3,2,1,0:T(8,128)S(1)}, f32[2,3,32,256]{3,2,1,0:T(8,128)S(1)}, u32[]{:S(2)}, u32[]{:S(2)}) collective-permute-start(f32[2,3,32,256]{3,2,1,0:T(8,128)S(1)} %slice.69), channel_id=1, source_target_pairs={{0,192},{32,224},{64,128},{96,160},{128,64},{160,96},{192,0},{224,... | collective-permute-start | bytes 589832 | tf_op jit(solution)/shard_map/ppermute | solution.py:312
  17.4 2.1 %collective-permute-done.9 = f32[2,3,32,256]{3,2,1,0:T(8,128)S(1)} collective-permute-done((f32[2,3,32,256]{3,2,1,0:T(8,128)S(1)}, f32[2,3,32,256]{3,2,1,0:T(8,128)S(1)}, u32[]{:S(2)}, u32[]{:S(2)}) %collective-permute-start.9) | collective-permute-done | bytes 196640 | tf_op jit(solution)/shard_map/ppermute | solution.py:312
  21.3 2.3 %collective-permute-done.1 = f32[2,3,32,256]{3,2,1,0:T(8,128)S(1)} collective-permute-done((f32[2,3,32,256]{3,2,1,0:T(8,128)S(1)}, f32[2,3,32,256]{3,2,1,0:T(8,128)S(1)}, u32[]{:S(2)}, u32[]{:S(2)}) %collective-permute-start.1) | collective-permute-done | bytes 196640 | tf_op jit(solution)/shard_map/ppermute | solution.py:312
  25.6 2.0 %collective-permute-done.10 = f32[3,32,256]{2,1,0:T(8,128)S(1)} collective-permute-done((f32[3,32,256]{2,1,0:T(8,128)S(1)}, f32[3,32,256]{2,1,0:T(8,128)S(1)}, u32[]{:S(2)}, u32[]{:S(2)}) %collective-permute-start.10) | collective-permute-done | bytes 98336 | tf_op jit(solution)/shard_map/ppermute | solution.py:312
  29.2 4.5 %collective-permute-start.6 = (f32[6,32,256]{2,1,0:T(8,128)S(1)}, f32[6,32,256]{2,1,0:T(8,128)S(1)}, u32[]{:S(2)}, u32[]{:S(2)}) collective-permute-start(f32[6,32,256]{2,1,0:T(8,128)S(1)} %pad_maximum_fusion.refs_0_), channel_id=1, source_target_pairs={{0,1},{1,0},{2,3},{3,2},{4,5},{5,4},{6,7},{7,6},{8,9},{9,8},{10,11... | collective-permute-start | bytes 589832 | tf_op jit(solution)/shard_map/ppermute | solution.py:312
  34.4 2.4 %collective-permute-done.6.refs_1_ = f32[6,32,256]{2,1,0:T(8,128)S(1)} collective-permute-done((f32[6,32,256]{2,1,0:T(8,128)S(1)}, f32[6,32,256]{2,1,0:T(8,128)S(1)}, u32[]{:S(2)}, u32[]{:S(2)}) %collective-permute-start.6) | collective-permute-done | bytes 196640 | tf_op jit(solution)/shard_map/ppermute | solution.py:312
  37.5 4.1 %collective-permute-start.16 = (f32[136,128]{1,0:T(8,128)S(1)}, f32[136,128]{1,0:T(8,128)S(1)}, u32[]{:S(2)}, u32[]{:S(2)}) collective-permute-start(f32[136,128]{1,0:T(8,128)S(1)} %constant_dynamic-slice_fusion), channel_id=1, source_target_pairs={{0,32},{32,0},{64,96},{96,64},{128,160},{160,128},{192,224},{224,1... | collective-permute-start | bytes 208904 | tf_op jit(solution)/shard_map/ppermute | solution.py:312
  42.7 8.6 %collective-permute-start.18 = (f32[136,128]{1,0:T(8,128)S(1)}, f32[136,128]{1,0:T(8,128)S(1)}, u32[]{:S(2)}, u32[]{:S(2)}) collective-permute-start(f32[136,128]{1,0:T(8,128)S(1)} %dynamic-slice_add_fusion), channel_id=1, source_target_pairs={{0,40},{1,41},{2,42},{3,43},{4,44},{5,45},{6,46},{7,47},{8,32},{9,... | collective-permute-start | bytes 208904 | tf_op jit(solution)/shard_map/ppermute | solution.py:312
  52.4 1.1 %collective-permute-done.18 = f32[136,128]{1,0:T(8,128)S(1)} collective-permute-done((f32[136,128]{1,0:T(8,128)S(1)}, f32[136,128]{1,0:T(8,128)S(1)}, u32[]{:S(2)}, u32[]{:S(2)}) %collective-permute-start.18) | collective-permute-done | bytes 69664 | tf_op jit(solution)/shard_map/ppermute | solution.py:312
  53.5 2.8 %collective-permute-done.19 = f32[136,128]{1,0:T(8,128)S(1)} collective-permute-done((f32[136,128]{1,0:T(8,128)S(1)}, f32[136,128]{1,0:T(8,128)S(1)}, u32[]{:S(2)}, u32[]{:S(2)}) %collective-permute-start.19) | collective-permute-done | bytes 69664 | tf_op jit(solution)/shard_map/ppermute | solution.py:312
  56.3 2.2 %collective-permute-start.20 = (f32[136,128]{1,0:T(8,128)S(1)}, f32[136,128]{1,0:T(8,128)S(1)}, u32[]{:S(2)}, u32[]{:S(2)}) collective-permute-start(f32[136,128]{1,0:T(8,128)S(1)} %add_add_fusion.2), channel_id=1, source_target_pairs={{0,224},{1,225},{2,226},{3,227},{4,228},{5,229},{6,230},{7,231},{8... | collective-permute-start | bytes 208904 | tf_op jit(solution)/shard_map/ppermute | solution.py:312
  58.5 2.6 %collective-permute-start.21 = (f32[136,128]{1,0:T(8,128)S(1)}, f32[136,128]{1,0:T(8,128)S(1)}, u32[]{:S(2)}, u32[]{:S(2)}) collective-permute-start(f32[136,128]{1,0:T(8,128)S(1)} %add_add_fusion.2), channel_id=1, source_target_pairs={{0,56},{1,57},{2,58},{3,59},{4,60},{5,61},{6,62},{7,63},{8,48},{9,... | collective-permute-start | bytes 208904 | tf_op jit(solution)/shard_map/ppermute | solution.py:312
  61.1 1.4 %collective-permute-start.22 = (f32[136,128]{1,0:T(8,128)S(1)}, f32[136,128]{1,0:T(8,128)S(1)}, u32[]{:S(2)}, u32[]{:S(2)}) collective-permute-start(f32[136,128]{1,0:T(8,128)S(1)} %add_add_fusion.2), channel_id=1, source_target_pairs={{0,216},{1,217},{2,218},{3,219},{4,220},{5,221},{6,222},{7,223},{8... | collective-permute-start | bytes 208904 | tf_op jit(solution)/shard_map/ppermute | solution.py:312
  62.5 1.6 %collective-permute-done.21 = f32[136,128]{1,0:T(8,128)S(1)} collective-permute-done((f32[136,128]{1,0:T(8,128)S(1)}, f32[136,128]{1,0:T(8,128)S(1)}, u32[]{:S(2)}, u32[]{:S(2)}) %collective-permute-start.21) | collective-permute-done | bytes 69664 | tf_op jit(solution)/shard_map/ppermute | solution.py:312
  64.1 3.5 %collective-permute-done.22 = f32[136,128]{1,0:T(8,128)S(1)} collective-permute-done((f32[136,128]{1,0:T(8,128)S(1)}, f32[136,128]{1,0:T(8,128)S(1)}, u32[]{:S(2)}, u32[]{:S(2)}) %collective-permute-start.22) | collective-permute-done | bytes 69664 | tf_op jit(solution)/shard_map/ppermute | solution.py:312
  67.6 1.6 %collective-permute-start.23 = (f32[136,128]{1,0:T(8,128)S(1)}, f32[136,128]{1,0:T(8,128)S(1)}, u32[]{:S(2)}, u32[]{:S(2)}) collective-permute-start(f32[136,128]{1,0:T(8,128)S(1)} %add_add_fusion.1), channel_id=1, source_target_pairs={{0,33},{1,32},{2,35},{3,34},{4,37},{5,36},{6,39},{7,38},{8,41},{9,... | collective-permute-start | bytes 208904 | tf_op jit(solution)/shard_map/ppermute | solution.py:312
  69.5 2.0 %collective-permute-start.25 = (f32[136,128]{1,0:T(8,128)S(1)}, f32[136,128]{1,0:T(8,128)S(1)}, u32[]{:S(2)}, u32[]{:S(2)}) collective-permute-start(f32[136,128]{1,0:T(8,128)S(1)} %add_add_fusion.1), channel_id=1, source_target_pairs={{0,3},{1,2},{2,1},{3,0},{4,7},{5,6},{6,5},{7,4},{8,11},{9,10},{10,... | collective-permute-start | bytes 208904 | tf_op jit(solution)/shard_map/ppermute | solution.py:312
  71.5 6.0 %collective-permute-done.24 = f32[136,128]{1,0:T(8,128)S(1)} collective-permute-done((f32[136,128]{1,0:T(8,128)S(1)}, f32[136,128]{1,0:T(8,128)S(1)}, u32[]{:S(2)}, u32[]{:S(2)}) %collective-permute-start.24) | collective-permute-done | bytes 69664 | tf_op jit(solution)/shard_map/ppermute | solution.py:312
  77.6 2.2 %collective-permute-start.26 = (f32[136,128]{1,0:T(8,128)S(1)}, f32[136,128]{1,0:T(8,128)S(1)}, u32[]{:S(2)}, u32[]{:S(2)}) collective-permute-start(f32[136,128]{1,0:T(8,128)S(1)} %add_add_fusion), channel_id=1, source_target_pairs={{0,38},{1,39},{2,36},{3,37},{4,34},{5,35},{6,32},{7,33},{8,46},{9,... | collective-permute-start | bytes 208904 | tf_op jit(solution)/shard_map/ppermute | solution.py:312
  79.8 4.3 %collective-permute-done.26 = f32[136,128]{1,0:T(8,128)S(1)} collective-permute-done((f32[136,128]{1,0:T(8,128)S(1)}, f32[136,128]{1,0:T(8,128)S(1)}, u32[]{:S(2)}, u32[]{:S(2)}) %collective-permute-start.26) | collective-permute-done | bytes 69664 | tf_op jit(solution)/shard_map/ppermute | solution.py:312
  85.7 10.4 %shard_map.70 = (f32[768,128]{1,0:T(8,128)}, f32[256,256]{1,0:T(8,128)}) custom-call(f32[272,128]{1,0:T(8,128)S(1)} %maximum_select_fusion.gram_ref, f32[12,32,256]{2,1,0:T(8,128)S(1)} %get-tuple-element.23.panel_ref), custom_call_target="tpu_custom_call" | custom-call | tf_op jit(solution)/shard_map/pallas_call | solution.py:298
  (72 shorter events, 15.9 us)
Async XLA Ops:
  8.5 4.7 %collective-permute-start.8 = (f32[4,3,32,256]{3,2,1,0:T(8,128)S(1)}, f32[4,3,32,256]{3,2,1,0:T(8,128)S(1)}, u32[]{:S(2)}, u32[]{:S(2)}) collective-permute-start(f32[4,3,32,256]{3,2,1,0:T(8,128)S(1)} %get-tuple-element.19), channel_id=1, source_target_pairs={{0,32},{32,0},{64,96},{96,64},{128,160},{160,128},{192,224},{224,1... | collective-permute-start | bytes 1179656 | tf_op jit(solution)/shard_map/ppermute | solution.py:312
  12.3 3.2 %collective-permute-start.3 = (f32[4,3,32,256]{3,2,1,0:T(8,128)S(1)}, f32[4,3,32,256]{3,2,1,0:T(8,128)S(1)}, u32[]{:S(2)}, u32[]{:S(2)}) collective-permute-start(f32[4,3,32,256]{3,2,1,0:T(8,128)S(1)} %get-tuple-element.17), channel_id=1, source_target_pairs={{0,32},{32,0},{64,96},{96,64},{128,160},{160,128},{192,224},{224,1... | collective-permute-start | bytes 1179656 | tf_op jit(solution)/shard_map/ppermute | solution.py:312
  13.2 6.2 %collective-permute-start.9 = (f32[2,3,32,256]{3,2,1,0:T(8,128)S(1)}, f32[2,3,32,256]{3,2,1,0:T(8,128)S(1)}, u32[]{:S(2)}, u32[]{:S(2)}) collective-permute-start(f32[2,3,32,256]{3,2,1,0:T(8,128)S(1)} %slice.73), channel_id=1, source_target_pairs={{0,64},{32,96},{64,0},{96,32},{128,192},{160,224},{192,128},{224,1... | collective-permute-start | bytes 589832 | tf_op jit(solution)/shard_map/ppermute | solution.py:312
  13.8 7.4 %collective-permute-start.12 = (f32[2,3,32,256]{3,2,1,0:T(8,128)S(1)}, f32[2,3,32,256]{3,2,1,0:T(8,128)S(1)}, u32[]{:S(2)}, u32[]{:S(2)}) collective-permute-start(f32[2,3,32,256]{3,2,1,0:T(8,128)S(1)} %slice.77), channel_id=1, source_target_pairs={{0,192},{32,224},{64,128},{96,160},{128,64},{160,96},{192,0},{224,... | collective-permute-start | bytes 589832 | tf_op jit(solution)/shard_map/ppermute | solution.py:312
  15.0 8.6 %collective-permute-start.1 = (f32[2,3,32,256]{3,2,1,0:T(8,128)S(1)}, f32[2,3,32,256]{3,2,1,0:T(8,128)S(1)}, u32[]{:S(2)}, u32[]{:S(2)}) collective-permute-start(f32[2,3,32,256]{3,2,1,0:T(8,128)S(1)} %slice.65), channel_id=1, source_target_pairs={{0,64},{32,96},{64,0},{96,32},{128,192},{160,224},{192,128},{224,1... | collective-permute-start | bytes 589832 | tf_op jit(solution)/shard_map/ppermute | solution.py:312
  15.6 9.8 %collective-permute-start.4 = (f32[2,3,32,256]{3,2,1,0:T(8,128)S(1)}, f32[2,3,32,256]{3,2,1,0:T(8,128)S(1)}, u32[]{:S(2)}, u32[]{:S(2)}) collective-permute-start(f32[2,3,32,256]{3,2,1,0:T(8,128)S(1)} %slice.69), channel_id=1, source_target_pairs={{0,192},{32,224},{64,128},{96,160},{128,64},{160,96},{192,0},{224,... | collective-permute-start | bytes 589832 | tf_op jit(solution)/shard_map/ppermute | solution.py:312
  19.5 8.0 %collective-permute-start.10 = (f32[3,32,256]{2,1,0:T(8,128)S(1)}, f32[3,32,256]{2,1,0:T(8,128)S(1)}, u32[]{:S(2)}, u32[]{:S(2)}) collective-permute-start(f32[3,32,256]{2,1,0:T(8,128)S(1)} %slice_bitcast_fusion.2), channel_id=1, source_target_pairs={{0,192},{32,224},{64,128},{96,160},{128,64},{160,96},{192,0},{224,... | collective-permute-start | bytes 294920 | tf_op jit(solution)/shard_map/ppermute | solution.py:312
  21.2 6.3 %collective-permute-start.13 = (f32[3,32,256]{2,1,0:T(8,128)S(1)}, f32[3,32,256]{2,1,0:T(8,128)S(1)}, u32[]{:S(2)}, u32[]{:S(2)}) collective-permute-start(f32[3,32,256]{2,1,0:T(8,128)S(1)} %slice_bitcast_fusion), channel_id=1, source_target_pairs={{0,64},{32,96},{64,0},{96,32},{128,192},{160,224},{192,128},{224,1... | collective-permute-start | bytes 294920 | tf_op jit(solution)/shard_map/ppermute | solution.py:312
  23.7 5.4 %collective-permute-start.2 = (f32[3,32,256]{2,1,0:T(8,128)S(1)}, f32[3,32,256]{2,1,0:T(8,128)S(1)}, u32[]{:S(2)}, u32[]{:S(2)}) collective-permute-start(f32[3,32,256]{2,1,0:T(8,128)S(1)} %slice_bitcast_fusion.6), channel_id=1, source_target_pairs={{0,192},{32,224},{64,128},{96,160},{128,64},{160,96},{192,0},{224,... | collective-permute-start | bytes 294920 | tf_op jit(solution)/shard_map/ppermute | solution.py:312
  25.5 3.6 %collective-permute-start.5 = (f32[3,32,256]{2,1,0:T(8,128)S(1)}, f32[3,32,256]{2,1,0:T(8,128)S(1)}, u32[]{:S(2)}, u32[]{:S(2)}) collective-permute-start(f32[3,32,256]{2,1,0:T(8,128)S(1)} %slice_bitcast_fusion.4), channel_id=1, source_target_pairs={{0,64},{32,96},{64,0},{96,32},{128,192},{160,224},{192,128},{224,1... | collective-permute-start | bytes 294920 | tf_op jit(solution)/shard_map/ppermute | solution.py:312
  27.6 6.8 %collective-permute-start.14 = (f32[6,32,256]{2,1,0:T(8,128)S(1)}, f32[6,32,256]{2,1,0:T(8,128)S(1)}, u32[]{:S(2)}, u32[]{:S(2)}) collective-permute-start(f32[6,32,256]{2,1,0:T(8,128)S(1)} %pad_maximum_fusion.1.refs_3_), channel_id=1, source_target_pairs={{0,1},{1,0},{2,3},{3,2},{4,5},{5,4},{6,7},{7,6},{8,9},{9,8},{10,11... | collective-permute-start | bytes 589832 | tf_op jit(solution)/shard_map/ppermute | solution.py:312
  28.2 6.2 %collective-permute-start.15 = (f32[6,32,256]{2,1,0:T(8,128)S(1)}, f32[6,32,256]{2,1,0:T(8,128)S(1)}, u32[]{:S(2)}, u32[]{:S(2)}) collective-permute-start(f32[6,32,256]{2,1,0:T(8,128)S(1)} %pad_maximum_fusion.1.refs_3_), channel_id=1, source_target_pairs={{1,2},{3,4},{5,6},{7,8},{9,10},{11,12},{13,14},{15,16},{17,18},{19... | collective-permute-start | bytes 589832 | tf_op jit(solution)/shard_map/ppermute | solution.py:318
  29.2 7.6 %collective-permute-start.6 = (f32[6,32,256]{2,1,0:T(8,128)S(1)}, f32[6,32,256]{2,1,0:T(8,128)S(1)}, u32[]{:S(2)}, u32[]{:S(2)}) collective-permute-start(f32[6,32,256]{2,1,0:T(8,128)S(1)} %pad_maximum_fusion.refs_0_), channel_id=1, source_target_pairs={{0,1},{1,0},{2,3},{3,2},{4,5},{5,4},{6,7},{7,6},{8,9},{9,8},{10,11... | collective-permute-start | bytes 589832 | tf_op jit(solution)/shard_map/ppermute | solution.py:312
  37.5 5.0 %collective-permute-start.16 = (f32[136,128]{1,0:T(8,128)S(1)}, f32[136,128]{1,0:T(8,128)S(1)}, u32[]{:S(2)}, u32[]{:S(2)}) collective-permute-start(f32[136,128]{1,0:T(8,128)S(1)} %constant_dynamic-slice_fusion), channel_id=1, source_target_pairs={{0,32},{32,0},{64,96},{96,64},{128,160},{160,128},{192,224},{224,1... | collective-permute-start | bytes 208904 | tf_op jit(solution)/shard_map/ppermute | solution.py:312
  42.6 9.8 %collective-permute-start.17 = (f32[136,128]{1,0:T(8,128)S(1)}, f32[136,128]{1,0:T(8,128)S(1)}, u32[]{:S(2)}, u32[]{:S(2)}) collective-permute-start(f32[136,128]{1,0:T(8,128)S(1)} %dynamic-slice_add_fusion), channel_id=1, source_target_pairs={{0,96},{1,97},{2,98},{3,99},{4,100},{5,101},{6,102},{7,103},{8,104... | collective-permute-start | bytes 208904 | tf_op jit(solution)/shard_map/ppermute | solution.py:312
  42.7 10.8 %collective-permute-start.18 = (f32[136,128]{1,0:T(8,128)S(1)}, f32[136,128]{1,0:T(8,128)S(1)}, u32[]{:S(2)}, u32[]{:S(2)}) collective-permute-start(f32[136,128]{1,0:T(8,128)S(1)} %dynamic-slice_add_fusion), channel_id=1, source_target_pairs={{0,40},{1,41},{2,42},{3,43},{4,44},{5,45},{6,46},{7,47},{8,32},{9,... | collective-permute-start | bytes 208904 | tf_op jit(solution)/shard_map/ppermute | solution.py:312
  51.3 5.0 %collective-permute-start.19 = (f32[136,128]{1,0:T(8,128)S(1)}, f32[136,128]{1,0:T(8,128)S(1)}, u32[]{:S(2)}, u32[]{:S(2)}) collective-permute-start(f32[136,128]{1,0:T(8,128)S(1)} %dynamic-slice_add_fusion), channel_id=1, source_target_pairs={{0,72},{1,73},{2,74},{3,75},{4,76},{5,77},{6,78},{7,79},{8,64},{9,... | collective-permute-start | bytes 208904 | tf_op jit(solution)/shard_map/ppermute | solution.py:312
  56.3 6.2 %collective-permute-start.20 = (f32[136,128]{1,0:T(8,128)S(1)}, f32[136,128]{1,0:T(8,128)S(1)}, u32[]{:S(2)}, u32[]{:S(2)}) collective-permute-start(f32[136,128]{1,0:T(8,128)S(1)} %add_add_fusion.2), channel_id=1, source_target_pairs={{0,224},{1,225},{2,226},{3,227},{4,228},{5,229},{6,230},{7,231},{8... | collective-permute-start | bytes 208904 | tf_op jit(solution)/shard_map/ppermute | solution.py:312
  58.5 5.6 %collective-permute-start.21 = (f32[136,128]{1,0:T(8,128)S(1)}, f32[136,128]{1,0:T(8,128)S(1)}, u32[]{:S(2)}, u32[]{:S(2)}) collective-permute-start(f32[136,128]{1,0:T(8,128)S(1)} %add_add_fusion.2), channel_id=1, source_target_pairs={{0,56},{1,57},{2,58},{3,59},{4,60},{5,61},{6,62},{7,63},{8,48},{9,... | collective-permute-start | bytes 208904 | tf_op jit(solution)/shard_map/ppermute | solution.py:312
  61.1 6.5 %collective-permute-start.22 = (f32[136,128]{1,0:T(8,128)S(1)}, f32[136,128]{1,0:T(8,128)S(1)}, u32[]{:S(2)}, u32[]{:S(2)}) collective-permute-start(f32[136,128]{1,0:T(8,128)S(1)} %add_add_fusion.2), channel_id=1, source_target_pairs={{0,216},{1,217},{2,218},{3,219},{4,220},{5,221},{6,222},{7,223},{8... | collective-permute-start | bytes 208904 | tf_op jit(solution)/shard_map/ppermute | solution.py:312
  67.6 3.9 %collective-permute-start.23 = (f32[136,128]{1,0:T(8,128)S(1)}, f32[136,128]{1,0:T(8,128)S(1)}, u32[]{:S(2)}, u32[]{:S(2)}) collective-permute-start(f32[136,128]{1,0:T(8,128)S(1)} %add_add_fusion.1), channel_id=1, source_target_pairs={{0,33},{1,32},{2,35},{3,34},{4,37},{5,36},{6,39},{7,38},{8,41},{9,... | collective-permute-start | bytes 208904 | tf_op jit(solution)/shard_map/ppermute | solution.py:312
  69.2 8.4 %collective-permute-start.24 = (f32[136,128]{1,0:T(8,128)S(1)}, f32[136,128]{1,0:T(8,128)S(1)}, u32[]{:S(2)}, u32[]{:S(2)}) collective-permute-start(f32[136,128]{1,0:T(8,128)S(1)} %add_add_fusion.1), channel_id=1, source_target_pairs={{0,34},{1,35},{2,32},{3,33},{4,38},{5,39},{6,36},{7,37},{8,42},{9,... | collective-permute-start | bytes 208904 | tf_op jit(solution)/shard_map/ppermute | solution.py:312
  69.5 8.1 %collective-permute-start.25 = (f32[136,128]{1,0:T(8,128)S(1)}, f32[136,128]{1,0:T(8,128)S(1)}, u32[]{:S(2)}, u32[]{:S(2)}) collective-permute-start(f32[136,128]{1,0:T(8,128)S(1)} %add_add_fusion.1), channel_id=1, source_target_pairs={{0,3},{1,2},{2,1},{3,0},{4,7},{5,6},{6,5},{7,4},{8,11},{9,10},{10,... | collective-permute-start | bytes 208904 | tf_op jit(solution)/shard_map/ppermute | solution.py:312
  77.6 6.5 %collective-permute-start.26 = (f32[136,128]{1,0:T(8,128)S(1)}, f32[136,128]{1,0:T(8,128)S(1)}, u32[]{:S(2)}, u32[]{:S(2)}) collective-permute-start(f32[136,128]{1,0:T(8,128)S(1)} %add_add_fusion), channel_id=1, source_target_pairs={{0,38},{1,39},{2,36},{3,37},{4,34},{5,35},{6,32},{7,33},{8,46},{9,... | collective-permute-start | bytes 208904 | tf_op jit(solution)/shard_map/ppermute | solution.py:312
  (8 other events, 40.3 us)

commit v4 on v2

--- a/solution.py
+++ b/solution.py
@@ -17,7 +17,7 @@
 NZ = 32
 ROWS = 98304
 HALF = 128
-GROUP = 4
+GROUP = 3
 DILATIONS = 4
 EXACT = lax.Precision.HIGHEST
 
@@ -50,34 +50,44 @@
                 table[d + 1, rows, :] = mixed.astype(jnp.bfloat16)
 
 
+def step_masks(core):
+    return 1 + 2 * core, 3 - 2 * core
+
+
+def step_order(core):
+    near, far = step_masks(core)
+    return 0, far, near, near ^ far
+
+
 def split(x):
     high = x.astype(jnp.bfloat16)
     return high, (x - high.astype(jnp.float32)).astype(jnp.bfloat16)
 
 
-def sketch_kernel(orders, snap_hbm, sketch_hbm, shift_hbm, weight_hbm, *refs):
-    outs = refs[: 2 * len(orders)]
-    snap, sketch, turned, table, shift, weight, snap_sem, sem = refs[2 * len(orders) :]
-    first = [
+def sketch_kernel(first, count, snap_hbm, sketch_hbm, shift_hbm, weight_hbm, *refs):
+    send_ref, keep_ref, snap, sketch, turned, table, shift, weight, snap_sem, sem = refs
+    heads = [
         pltpu.make_async_copy(sketch_hbm, sketch, sem.at[0]),
         pltpu.make_async_copy(shift_hbm, shift, sem.at[1]),
         pltpu.make_async_copy(weight_hbm, weight, sem.at[2]),
     ]
     copies = [
-        pltpu.make_async_copy(snap_hbm.at[f], snap.at[f], snap_sem.at[f]) for f in range(FIELDS)
+        pltpu.make_async_copy(snap_hbm.at[first + f], snap.at[f], snap_sem.at[f])
+        for f in range(count)
     ]
-    for copy in first + copies:
+    for copy in heads + copies:
         copy.start()
     me = lax.axis_index("tm")
     y, core = me // 2, me % 2
-    order = orders[0]
+    other = 1 - core
     filter_tables(
-        table, [2 * (y ^ m) + (1 - core) for m in order] + [2 * (y ^ m) + core for m in order]
+        table,
+        [2 * (y ^ m) + other for m in step_order(other)]
+        + [2 * (y ^ m) + core for m in step_order(core)],
     )
-    for copy in first:
+    for copy in heads:
         copy.wait()
     turned[...] = sketch[...].T
-    each = FIELDS // len(orders)
     dot = functools.partial(
         lax.dot_general,
         dimension_numbers=(((1,), (1,)), ((), ())),
@@ -86,19 +96,16 @@
 
     def filtered(f, raw):
         high, low = split(raw)
-        blur, slope = table[0], table[shift[f]]
-        image = (dot(blur, high) + dot(blur, low)) + weight[f] * (
+        blur, slope = table[0], table[shift[first + f]]
+        image = (dot(blur, high) + dot(blur, low)) + weight[first + f] * (
             dot(slope, high) + dot(slope, low)
         )
-        n, i = divmod(f, each)
-        for r, mask in enumerate(orders[n]):
-            at = SHARE * order.index(mask)
-            outs[2 * n][r, i] = image[at : at + SHARE]
-            outs[2 * n + 1][r, i] = image[HALF + at : HALF + at + SHARE]
+        send_ref[:, f] = image[:HALF].reshape(4, SHARE, RANK)
+        keep_ref[:, f] = image[HALF:].reshape(4, SHARE, RANK)
 
     held = None
-    for g in range(0, FIELDS + GROUP, GROUP):
-        if g < FIELDS:
+    for g in range(0, count + GROUP, GROUP):
+        if g < count:
             for f in range(g, g + GROUP):
                 copies[f].wait()
             raws = [
@@ -111,32 +118,37 @@
         held = raws
 
 
-def sketch_call(snaps, sketch, dilation, weight, orders):
-    out = jax.ShapeDtypeStruct((4, FIELDS // len(orders), SHARE, RANK), jnp.float32)
+def sketch_call(snaps, sketch, dilation, weight, first, count):
+    out = jax.ShapeDtypeStruct((4, count, SHARE, RANK), jnp.float32)
     hbm = pl.BlockSpec(memory_space=pltpu.HBM)
     vmem = pl.BlockSpec(memory_space=pltpu.VMEM)
     return pl.pallas_call(
-        functools.partial(sketch_kernel, orders),
+        functools.partial(sketch_kernel, first, count),
         in_specs=[hbm] * 4,
-        out_specs=[vmem] * (2 * len(orders)),
-        out_shape=[out] * (2 * len(orders)),
+        out_specs=[vmem] * 2,
+        out_shape=[out] * 2,
         scratch_shapes=[
-            pltpu.VMEM((FIELDS, SNAP_DEV, PLANE), jnp.bfloat16),
+            pltpu.VMEM((count, SNAP_DEV, PLANE), jnp.bfloat16),
             pltpu.VMEM((SNAP_DEV, RANK), jnp.bfloat16),
             pltpu.VMEM((RANK, SNAP_DEV), jnp.bfloat16),
             pltpu.VMEM((DILATIONS + 1, PLANE, PLANE), jnp.bfloat16),
             pltpu.SMEM((FIELDS,), jnp.int32),
             pltpu.SMEM((FIELDS,), jnp.float32),
-            pltpu.SemaphoreType.DMA((FIELDS,)),
+            pltpu.SemaphoreType.DMA((count,)),
             pltpu.SemaphoreType.DMA((3,)),
         ],
-        compiler_params=pltpu.CompilerParams(vmem_limit_bytes=52 * 2**20),
+        compiler_params=pltpu.CompilerParams(vmem_limit_bytes=50 * 2**20),
+        cost_estimate=pl.CostEstimate(
+            flops=count * 2**28, bytes_accessed=count * 2**20, transcendentals=0
+        ),
     )(snaps, sketch, dilation, weight)
 
 
 def panel_kernel(counts, volume_ref, *refs):
     parts, (panel_ref, gram_ref) = refs[:-2], refs[-2:]
     me, plane = lax.axis_index("tm"), lax.axis_index("space")
+    inner = (plane > 0) & (plane < NZ - 1)
+    use_first, use_second = inner | (me % 2 == 0), inner | (me % 2 == 1)
     row = lax.broadcasted_iota(jnp.int32, (SHARE, PLANE), 0)
     lane = lax.broadcasted_iota(jnp.int32, (SHARE, PLANE), 1)
     volume = jnp.broadcast_to(volume_ref[...], (SHARE, PLANE))
@@ -145,11 +157,11 @@
     scaled = []
     at = 0
     for n, count in enumerate(counts):
-        here, below, above = parts[3 * n : 3 * n + 3]
+        here, first, second = parts[3 * n : 3 * n + 3]
         for f in range(count):
             panel = 0.5 * here[f]
-            panel = panel + jnp.where(plane > 0, 0.25 * below[f], 0.0)
-            panel = panel + jnp.where(plane < NZ - 1, 0.25 * above[f], 0.0)
+            panel = panel + jnp.where(use_first, 0.25 * first[f], 0.0)
+            panel = panel + jnp.where(use_second, 0.25 * second[f], 0.0)
             panel_ref[at] = panel
             scaled.append(panel * root)
             at += 1
@@ -209,11 +221,13 @@
     def row_of(x, i):
         return jnp.broadcast_to(x[i : i + 1, :], shape)
 
+    cols = [column(rows[0], m) for m in range(8)]
     for s in range(count):
         here = rows[s]
         there = jnp.where(lane == sub + 8 * s, 1.0, 0.0)
         inside = (lane >= 8 * s) & (lane < 8 * s + 8)
-        cols = [column(here, 8 * s + m) for m in range(8)]
+        last = s + 1 == count
+        ahead = [] if last else [column(here, 8 * s + 8 + m) for m in range(8)]
         upper = lower = jnp.zeros(shape, jnp.float32)
         for j in range(0, 8, 2):
             p, q = cols[j], cols[j + 1]
@@ -223,29 +237,39 @@
             inv_a = 1.0 / a
             root_a, root_c = lax.rsqrt(a), lax.rsqrt(det * inv_a)
             slope = b * inv_a
-
-            def eliminate(x, kept=None):
+            into_a, into_b, into_c = a * inv_det, b * inv_det, c * inv_det
+
+            def eliminate(x):
                 x0, x1 = row_of(x, j), row_of(x, j + 1)
-                y0 = (c * x0 - b * x1) * inv_det
-                y1 = (a * x1 - b * x0) * inv_det
-                new = jnp.where(at[j], y0, jnp.where(at[j + 1], y1, x - p * y0 - q * y1))
-                if kept is None:
-                    return new
+                y0 = into_c * x0 - into_b * x1
+                y1 = into_a * x1 - into_b * x0
+                return jnp.where(at[j], y0, jnp.where(at[j + 1], y1, x - p * y0 - q * y1))
+
+            def factored(x, kept):
+                x0, x1 = row_of(x, j), row_of(x, j + 1)
                 second = (x1 - slope * x0) * root_c
-                return new, jnp.where(at[j], x0 * root_a, jnp.where(at[j + 1], second, kept))
-
-            here, upper = eliminate(here, upper)
-            there, lower = eliminate(there, lower)
+                return jnp.where(at[j], x0 * root_a, jnp.where(at[j + 1], second, kept))
+
+            upper, lower = factored(here, upper), factored(there, lower)
+            here, there = eliminate(here), eliminate(there)
             for m in range(j + 2, 8):
                 cols[m] = eliminate(cols[m])
+            ahead = [eliminate(x) for x in ahead]
         uppers.append(jnp.where(lane >= sub + 8 * s, upper, 0.0))
         lowers.append(jnp.where(inside, lower, jnp.where(lane < 8 * s, upper, 0.0)))
-        if s + 1 == count:
+        if last:
             break
+        weights = [column(rows[s + 1], 8 * s + m) for m in range(8)]
+        cols = [
+            column(rows[s + 1], 8 * s + 8 + m)
+            - total(weights[k] * row_of(ahead[m], k) for k in range(8))
+            for m in range(8)
+        ]
         solved = jnp.where(inside, there, here)
         solved_rows = [row_of(solved, m) for m in range(8)]
         for t in range(s + 1, count):
-            weights = [column(rows[t], 8 * s + m) for m in range(8)]
+            if t > s + 1:
+                weights = [column(rows[t], 8 * s + m) for m in range(8)]
             rows[t] = jnp.where(inside, 0.0, rows[t]) - total(
                 weights[m] * solved_rows[m] for m in range(8)
             )
@@ -314,46 +338,93 @@
     return lax.ppermute(x, axis, [(i, i ^ mask) for i in range(lax.axis_size(axis))])
 
 
-def ring(x, axis, step):
-    n = lax.axis_size(axis)
-    return lax.ppermute(x, axis, [(i, (i + step) % n) for i in range(n)])
-
-
-def sum_over_tm(send, keep, near, far):
-    got = swap(send, "tm", 1)
-    away = swap(keep[2:] + got[2:], "tm", 2 * near)
-    near_part = swap((keep[1] + got[1]) + away[1], "tm", 2 * far)
-    return ((keep[0] + got[0]) + away[0]) + near_part
+def permute(x, target):
+    pairs = []
+    for source in range(2 * 4 * NZ):
+        tm, space = divmod(source, NZ)
+        y, core, gx, gz = target(tm >> 1, tm & 1, space >> 3, space & 7)
+        pairs.append((source, (2 * y + core) * NZ + 8 * gx + gz))
+    return lax.ppermute(x, ("tm", "space"), pairs)
+
+
+def step_swap(x, which):
+    return permute(x, lambda y, c, gx, gz: (y ^ step_masks(c)[which], c, gx, gz))
+
+
+def halo_swap(x, which):
+    def target(y, c, gx, gz):
+        plane = 8 * gx + gz
+        if c == which:
+            goal = plane ^ 1
+        else:
+            goal = plane + 1 if plane & 1 else plane - 1
+        return (y, c, goal >> 3, goal & 7) if 0 <= goal < NZ else (y ^ 1, c, gx, gz)
+
+    return permute(x, target)
+
+
+def sum_along_y(mine):
+    mine = mine[:2] + step_swap(mine[2:], 0)
+    return mine[0] + step_swap(mine[1], 1)
+
+
+def parity(y, x, z):
+    return (y ^ x ^ z ^ (z >> 1)) & 1
+
+
+def gram_swap(x, masks):
+    def target(y, c, gx, gz):
+        dy, dx, dz = masks[c ^ parity(y, gx, gz)]
+        return y ^ dy, c ^ parity(dy, dx, dz), gx ^ dx, gz ^ dz
+
+    return permute(x, target)
 
 
 def sum_over_all(gram):
-    core = lax.axis_index("tm") % 2
+    tm, space = lax.axis_index("tm"), lax.axis_index("space")
+    side = (tm & 1) ^ parity(tm >> 1, space >> 3, space & 7)
     n = gram.shape[0] // 2
-    mine = lax.dynamic_slice_in_dim(gram, core * n, n, 0)
-    other = lax.dynamic_slice_in_dim(gram, (1 - core) * n, n, 0)
+    mine = lax.dynamic_slice_in_dim(gram, side * n, n, 0)
+    other = lax.dynamic_slice_in_dim(gram, (1 - side) * n, n, 0)
     mine = mine + swap(other, "tm", 1)
-    for mask in (2, 6):
-        mine = mine + swap(mine, "tm", mask)
-    for mask in (8, 24, 1, 2, 7):
-        mine = mine + swap(mine, "space", mask)
+    for step in GRAM_STEPS:
+        mine = mine + functools.reduce(jnp.add, [gram_swap(mine, masks) for masks in step])
     other = swap(mine, "tm", 1)
     return jnp.where(
-        core == 0, jnp.concatenate([mine, other], 0), jnp.concatenate([other, mine], 0)
+        side == 0, jnp.concatenate([mine, other], 0), jnp.concatenate([other, mine], 0)
     )
 
 
-STEPS = ((1, 3), (3, 1), (1, 3), (3, 1))
+PARTS = ((0, 6), (6, 6))
+def single(a, b):
+    return ((a, b),)
+
+
+def four(a, b):
+    both = [tuple(i ^ j for i, j in zip(*pair)) for pair in (a, b)]
+    return (a[0], b[0]), (a[1], b[1]), (both[0], both[1])
+
+
+Y1, Y3 = (1, 0, 0), (3, 0, 0)
+X1, X3 = (0, 1, 0), (0, 3, 0)
+Z1, Z2, Z6 = (0, 0, 1), (0, 0, 2), (0, 0, 6)
+GRAM_STEPS = (
+    single(Y3, Z6),
+    single(X3, Y3),
+    single(Z6, X3),
+    four((Y1, X1), (Z1, Z2)),
+    four((Z1, Z2), (Y1, X1)),
+)
 
 
 def shards(snapshots, sketch, volume, grad_weight, dilation):
     snaps = jnp.transpose(snapshots[:, :, 0, :], (1, 0, 2))
-    orders = [(0, far, near, near ^ far) for near, far in STEPS]
-    images = sketch_call(snaps, sketch, dilation, grad_weight, orders)
     parts = []
-    for n, (near, far) in enumerate(STEPS):
-        image = sum_over_tm(images[2 * n], images[2 * n + 1], near, far)
-        parts += [image, ring(image, "space", 1), ring(image, "space", -1)]
-    panel, gram = panel_call(volume, [FIELDS // len(STEPS)] * len(STEPS), parts)
+    for first, count in PARTS:
+        send, keep = sketch_call(snaps, sketch, dilation, grad_weight, first, count)
+        image = sum_along_y(keep + swap(send, "tm", 1))
+        parts += [image, halo_swap(image, 0), halo_swap(image, 1)]
+    panel, gram = panel_call(volume, [p.shape[0] for p in parts[::3]], parts)
     gram = sum_over_all(gram)
     basis, upper = basis_call(gram, panel)
     return basis, upper

time: 112 us -> 86.5 us (0.77)
  starting transfers between devices: 52.1 us -> 34.7 us
  other arithmetic: 5.83 us -> 0.52 us
  waiting for transfers between devices: 33.1 us -> 29.8 us
  local copies, waits for them, and re-layouts: 1.32 us -> 2.45 us
    ppermute x21 -> x4, waiting for transfers between devices: 31.1 us -> 2.85 us  [swap(): lax.ppermute(x, axis, [(i, i ^ mask) for i in range(lax.axis_size(axis))])]
    ppermute x8 -> x17, waiting for transfers between devices: 2.03 us -> 27 us  [permute(): return lax.ppermute(x, ('tm', 'space'), pairs)]
    ppermute x21 -> x4, starting transfers between devices: 29.4 us -> 6.76 us  [swap(): lax.ppermute(x, axis, [(i, i ^ mask) for i in range(lax.axis_size(axis))])]
    add x19 -> x11, other arithmetic: 5.8 us -> 0.49 us  [the longest x2 0.25 us: shards(): image = sum_along_y(keep + swap(send, 'tm', 1))]
    ppermute x8 -> x17, starting transfers between devices: 22.7 us -> 28 us  [permute(): return lax.ppermute(x, ('tm', 'space'), pairs)]
    unnamed x6 -> x8, local copies, waits for them, and re-layouts: 1.31 us -> 2.35 us
    pallas_call x1 -> x2, Pallas kernels: 7.45 us -> 7.41 us  [sketch_call(): pl.pallas_call(functools.partial(sketch_kernel, first, count), in_specs=[...]
  transfers between devices with their start and end apart: 29 -> 21, of which waited for: 15 -> 18; matrix products, arithmetic and copies ran while one was open for 5% -> 1% of each run, Pallas kernels for 0% -> 4%
where the time goes in v4:
time: 86.5 us; the launch traced here: 85.9 us
  starting transfers between devices  34.7 us (40%)
  waiting for transfers between devices  29.8 us (34%)
  Pallas kernels  17.6 us (20%)
  local copies, waits for them, and re-layouts  2.45 us (3%)
    ppermute x17, starting transfers between devices, permute(): return lax.ppermute(x, ('tm', 'space'), pairs)  28 us
    ppermute x17, waiting for transfers between devices, permute(): return lax.ppermute(x, ('tm', 'space'), pairs)  27 us
    pallas_call x1, Pallas kernels, basis_call(): pl.pallas_call(basis_kernel, in_specs=[vmem, vmem], out_specs=[vmem, vmem...  9.41 us
    pallas_call x2, Pallas kernels, sketch_call(): pl.pallas_call(functools.partial(sketch_kernel, first, count), in_specs=[...  7.41 us
    ppermute x4, starting transfers between devices, swap(): lax.ppermute(x, axis, [(i, i ^ mask) for i in range(lax.axis_size(axis))])  6.76 us
    ppermute x4, waiting for transfers between devices, swap(): lax.ppermute(x, axis, [(i, i ^ mask) for i in range(lax.axis_size(axis))])  2.85 us
    unnamed x8, local copies, waits for them, and re-layouts  2.35 us
  transfers between devices with their start and end apart: 21, of which 18 were waited for; matrix products, arithmetic and copies ran while one was open for 1% of the time, Pallas kernels for 4%

profile of v4, /device:TPU:1, one launch (start us, length us, event | category | flops | bytes accessed | tf_op | source)
XLA Modules:
  0.0 85.9 jit_solution(11487737286330809744)
XLA Ops:
  3.0 3.7 %shard_map.68 = (f32[4,6,32,256]{3,2,1,0:T(8,128)S(1)}, f32[4,6,32,256]{3,2,1,0:T(8,128)S(1)}) custom-call(bf16[12,1024,256]{2,1,0:T(8,128)(2,1)} %bitcast.16, bf16[1024,256]{1,0:T(8,128)(2,1)S(1)} %copy-done, s32[12]{0:T(128)S(1)} %copy-done.1, f32[12]{0:T(128)S(1)} %copy-done.2), custom_call_target="tpu_custom_call" | custom-call | flops 1610612736 | bytes 6291456 | tf_op jit(solution)/shard_map/pallas_call | solution.py:125
  6.7 3.3 %collective-permute-start = (f32[4,6,32,256]{3,2,1,0:T(8,128)S(1)}, f32[4,6,32,256]{3,2,1,0:T(8,128)S(1)}, u32[]{:S(2)}, u32[]{:S(2)}) collective-permute-start(f32[4,6,32,256]{3,2,1,0:T(8,128)S(1)} %get-tuple-element.11), channel_id=1, source_target_pairs={{0,32},{32,0},{64,96},{96,64},{128,160},{160,128},{192,224},{224,1... | collective-permute-start | bytes 2359304 | tf_op jit(solution)/shard_map/ppermute | solution.py:338
  10.0 3.7 %shard_map.69 = (f32[4,6,32,256]{3,2,1,0:T(8,128)S(1)}, f32[4,6,32,256]{3,2,1,0:T(8,128)S(1)}) custom-call(bf16[12,1024,256]{2,1,0:T(8,128)(2,1)} %bitcast.17, bf16[1024,256]{1,0:T(8,128)(2,1)S(1)} %copy-done, s32[12]{0:T(128)S(1)} %copy-done.1, f32[12]{0:T(128)S(1)} %copy-done.2), custom_call_target="tpu_custom_call" | custom-call | flops 1610612736 | bytes 6291456 | tf_op jit(solution)/shard_map/pallas_call | solution.py:125
  17.4 4.6 %collective-permute-done.1 = f32[2,6,32,256]{3,2,1,0:T(8,128)S(1)} collective-permute-done((f32[2,6,32,256]{3,2,1,0:T(8,128)S(1)}, f32[2,6,32,256]{3,2,1,0:T(8,128)S(1)}, u32[]{:S(2)}, u32[]{:S(2)}) %collective-permute-start.1) | collective-permute-done | bytes 393248 | tf_op jit(solution)/shard_map/ppermute | solution.py:347
  22.1 4.0 %collective-permute-done.6 = f32[2,6,32,256]{3,2,1,0:T(8,128)S(1)} collective-permute-done((f32[2,6,32,256]{3,2,1,0:T(8,128)S(1)}, f32[2,6,32,256]{3,2,1,0:T(8,128)S(1)}, u32[]{:S(2)}, u32[]{:S(2)}) %collective-permute-start.6) | collective-permute-done | bytes 393248 | tf_op jit(solution)/shard_map/ppermute | solution.py:347
  26.4 2.0 %collective-permute-done.2 = f32[6,32,256]{2,1,0:T(8,128)S(1)} collective-permute-done((f32[6,32,256]{2,1,0:T(8,128)S(1)}, f32[6,32,256]{2,1,0:T(8,128)S(1)}, u32[]{:S(2)}, u32[]{:S(2)}) %collective-permute-start.2) | collective-permute-done | bytes 196640 | tf_op jit(solution)/shard_map/ppermute | solution.py:347
  28.4 1.5 %collective-permute-start.4 = (f32[6,32,256]{2,1,0:T(8,128)S(1)}, f32[6,32,256]{2,1,0:T(8,128)S(1)}, u32[]{:S(2)}, u32[]{:S(2)}) collective-permute-start(f32[6,32,256]{2,1,0:T(8,128)S(1)} %fusion.1.refs_0_), channel_id=1, source_target_pairs={{0,64},{1,2},{2,1},{3,4},{4,3},{5,6},{6,5},{7,8},{8,7},{9,10},{10,... | collective-permute-start | bytes 589832 | tf_op jit(solution)/shard_map/ppermute | solution.py:347
  31.3 3.3 %collective-permute-start.9 = (f32[6,32,256]{2,1,0:T(8,128)S(1)}, f32[6,32,256]{2,1,0:T(8,128)S(1)}, u32[]{:S(2)}, u32[]{:S(2)}) collective-permute-start(f32[6,32,256]{2,1,0:T(8,128)S(1)} %fusion.refs_3_), channel_id=1, source_target_pairs={{0,64},{1,2},{2,1},{3,4},{4,3},{5,6},{6,5},{7,8},{8,7},{9,10},{10,... | collective-permute-start | bytes 589832 | tf_op jit(solution)/shard_map/ppermute | solution.py:347
  34.6 2.5 %collective-permute-done.8.refs_4_ = f32[6,32,256]{2,1,0:T(8,128)S(1)} collective-permute-done((f32[6,32,256]{2,1,0:T(8,128)S(1)}, f32[6,32,256]{2,1,0:T(8,128)S(1)}, u32[]{:S(2)}, u32[]{:S(2)}) %collective-permute-start.8) | collective-permute-done | bytes 196640 | tf_op jit(solution)/shard_map/ppermute | solution.py:347
  37.1 1.3 %collective-permute-done.9.refs_5_ = f32[6,32,256]{2,1,0:T(8,128)S(1)} collective-permute-done((f32[6,32,256]{2,1,0:T(8,128)S(1)}, f32[6,32,256]{2,1,0:T(8,128)S(1)}, u32[]{:S(2)}, u32[]{:S(2)}) %collective-permute-start.9) | collective-permute-done | bytes 196640 | tf_op jit(solution)/shard_map/ppermute | solution.py:347
  39.2 2.7 %collective-permute-start.10 = (f32[136,128]{1,0:T(8,128)S(1)}, f32[136,128]{1,0:T(8,128)S(1)}, u32[]{:S(2)}, u32[]{:S(2)}) collective-permute-start(f32[136,128]{1,0:T(8,128)S(1)} %constant_dynamic-slice_fusion), channel_id=1, source_target_pairs={{0,32},{32,0},{64,96},{96,64},{128,160},{160,128},{192,224},{224,1... | collective-permute-start | bytes 208904 | tf_op jit(solution)/shard_map/ppermute | solution.py:338
  42.8 5.5 %collective-permute-start.11 = (f32[136,128]{1,0:T(8,128)S(1)}, f32[136,128]{1,0:T(8,128)S(1)}, u32[]{:S(2)}, u32[]{:S(2)}) collective-permute-start(f32[136,128]{1,0:T(8,128)S(1)} %dynamic-slice_add_fusion), channel_id=1, source_target_pairs={{0,224},{1,39},{2,36},{3,227},{4,228},{5,35},{6,32},{7,231},{8,46}... | collective-permute-start | bytes 208904 | tf_op jit(solution)/shard_map/ppermute | solution.py:347
  48.4 2.0 %collective-permute-done.11 = f32[136,128]{1,0:T(8,128)S(1)} collective-permute-done((f32[136,128]{1,0:T(8,128)S(1)}, f32[136,128]{1,0:T(8,128)S(1)}, u32[]{:S(2)}, u32[]{:S(2)}) %collective-permute-start.11) | collective-permute-done | bytes 69664 | tf_op jit(solution)/shard_map/ppermute | solution.py:347
  50.4 2.8 %collective-permute-start.12 = (f32[136,128]{1,0:T(8,128)S(1)}, f32[136,128]{1,0:T(8,128)S(1)}, u32[]{:S(2)}, u32[]{:S(2)}) collective-permute-start(f32[136,128]{1,0:T(8,128)S(1)} %add.63), channel_id=1, source_target_pairs={{0,56},{1,225},{2,226},{3,59},{4,60},{5,229},{6,230},{7,63},{8,232... | collective-permute-start | bytes 208904 | tf_op jit(solution)/shard_map/ppermute | solution.py:347
  53.2 2.2 %collective-permute-done.12 = f32[136,128]{1,0:T(8,128)S(1)} collective-permute-done((f32[136,128]{1,0:T(8,128)S(1)}, f32[136,128]{1,0:T(8,128)S(1)}, u32[]{:S(2)}, u32[]{:S(2)}) %collective-permute-start.12) | collective-permute-done | bytes 69664 | tf_op jit(solution)/shard_map/ppermute | solution.py:347
  55.4 5.0 %collective-permute-start.13 = (f32[136,128]{1,0:T(8,128)S(1)}, f32[136,128]{1,0:T(8,128)S(1)}, u32[]{:S(2)}, u32[]{:S(2)}) collective-permute-start(f32[136,128]{1,0:T(8,128)S(1)} %add.64), channel_id=1, source_target_pairs={{0,38},{1,57},{2,58},{3,37},{4,34},{5,61},{6,62},{7,33},{8,48},{9,... | collective-permute-start | bytes 208904 | tf_op jit(solution)/shard_map/ppermute | solution.py:347
  60.4 2.1 %collective-permute-done.13 = f32[136,128]{1,0:T(8,128)S(1)} collective-permute-done((f32[136,128]{1,0:T(8,128)S(1)}, f32[136,128]{1,0:T(8,128)S(1)}, u32[]{:S(2)}, u32[]{:S(2)}) %collective-permute-start.13) | collective-permute-done | bytes 69664 | tf_op jit(solution)/shard_map/ppermute | solution.py:347
  64.3 2.1 %collective-permute-start.15 = (f32[136,128]{1,0:T(8,128)S(1)}, f32[136,128]{1,0:T(8,128)S(1)}, u32[]{:S(2)}, u32[]{:S(2)}) collective-permute-start(f32[136,128]{1,0:T(8,128)S(1)} %add.65), channel_id=1, source_target_pairs={{0,40},{1,35},{2,32},{3,43},{4,44},{5,39},{6,36},{7,47},{8,42},{9,... | collective-permute-start | bytes 208904 | tf_op jit(solution)/shard_map/ppermute | solution.py:347
  66.4 1.3 %collective-permute-done.16 = f32[136,128]{1,0:T(8,128)S(1)} collective-permute-done((f32[136,128]{1,0:T(8,128)S(1)}, f32[136,128]{1,0:T(8,128)S(1)}, u32[]{:S(2)}, u32[]{:S(2)}) %collective-permute-start.16) | collective-permute-done | bytes 69664 | tf_op jit(solution)/shard_map/ppermute | solution.py:347
  68.2 1.5 %collective-permute-done.15 = f32[136,128]{1,0:T(8,128)S(1)} collective-permute-done((f32[136,128]{1,0:T(8,128)S(1)}, f32[136,128]{1,0:T(8,128)S(1)}, u32[]{:S(2)}, u32[]{:S(2)}) %collective-permute-start.15) | collective-permute-done | bytes 69664 | tf_op jit(solution)/shard_map/ppermute | solution.py:347
  69.8 1.3 %collective-permute-start.17 = (f32[136,128]{1,0:T(8,128)S(1)}, f32[136,128]{1,0:T(8,128)S(1)}, u32[]{:S(2)}, u32[]{:S(2)}) collective-permute-start(f32[136,128]{1,0:T(8,128)S(1)} %add_add_fusion.1), channel_id=1, source_target_pairs={{0,33},{1,97},{2,98},{3,34},{4,37},{5,101},{6,102},{7,38},{8,104},... | collective-permute-start | bytes 208904 | tf_op jit(solution)/shard_map/ppermute | solution.py:347
  71.1 1.6 %collective-permute-start.18 = (f32[136,128]{1,0:T(8,128)S(1)}, f32[136,128]{1,0:T(8,128)S(1)}, u32[]{:S(2)}, u32[]{:S(2)}) collective-permute-start(f32[136,128]{1,0:T(8,128)S(1)} %add_add_fusion.1), channel_id=1, source_target_pairs={{0,34},{1,41},{2,42},{3,33},{4,38},{5,45},{6,46},{7,37},{8,32},{9,... | collective-permute-start | bytes 208904 | tf_op jit(solution)/shard_map/ppermute | solution.py:347
  72.7 1.4 %collective-permute-done.19 = f32[136,128]{1,0:T(8,128)S(1)} collective-permute-done((f32[136,128]{1,0:T(8,128)S(1)}, f32[136,128]{1,0:T(8,128)S(1)}, u32[]{:S(2)}, u32[]{:S(2)}) %collective-permute-start.19) | collective-permute-done | bytes 69664 | tf_op jit(solution)/shard_map/ppermute | solution.py:347
  76.5 9.4 %shard_map.71 = (f32[768,128]{1,0:T(8,128)}, f32[256,256]{1,0:T(8,128)}) custom-call(f32[272,128]{1,0:T(8,128)S(1)} %maximum_select_fusion.gram_ref, f32[12,32,256]{2,1,0:T(8,128)S(1)} %get-tuple-element.15.panel_ref), custom_call_target="tpu_custom_call" | custom-call | tf_op jit(solution)/shard_map/pallas_call | solution.py:324
  (48 shorter events, 14.3 us)
Async XLA Ops:
  0.6 1.0 %copy-start = (bf16[1024,256]{1,0:T(8,128)(2,1)S(1)}, bf16[1024,256]{1,0:T(8,128)(2,1)}, u32[]{:S(2)}) copy-start(bf16[1024,256]{1,0:T(8,128)(2,1)} %sketch_hbm.3) | copy-start | bytes 1572868
  1.7 0.7 copy-start.1
  6.7 7.2 %collective-permute-start = (f32[4,6,32,256]{3,2,1,0:T(8,128)S(1)}, f32[4,6,32,256]{3,2,1,0:T(8,128)S(1)}, u32[]{:S(2)}, u32[]{:S(2)}) collective-permute-start(f32[4,6,32,256]{3,2,1,0:T(8,128)S(1)} %get-tuple-element.11), channel_id=1, source_target_pairs={{0,32},{32,0},{64,96},{96,64},{128,160},{160,128},{192,224},{224,1... | collective-permute-start | bytes 2359304 | tf_op jit(solution)/shard_map/ppermute | solution.py:338
  13.7 24.7 %copy-start.3 = (f32[1,256]{1,0:T(1,128)S(1)}, f32[1,256]{1,0:T(1,128)}, u32[]{:S(2)}) copy-start(f32[1,256]{1,0:T(1,128)} %volume_ref.1) | copy-start | bytes 3076
  13.7 2.4 %collective-permute-start.5 = (f32[4,6,32,256]{3,2,1,0:T(8,128)S(1)}, f32[4,6,32,256]{3,2,1,0:T(8,128)S(1)}, u32[]{:S(2)}, u32[]{:S(2)}) collective-permute-start(f32[4,6,32,256]{3,2,1,0:T(8,128)S(1)} %get-tuple-element.13), channel_id=1, source_target_pairs={{0,32},{32,0},{64,96},{96,64},{128,160},{160,128},{192,224},{224,1... | collective-permute-start | bytes 2359304 | tf_op jit(solution)/shard_map/ppermute | solution.py:338
  14.0 7.9 %collective-permute-start.1 = (f32[2,6,32,256]{3,2,1,0:T(8,128)S(1)}, f32[2,6,32,256]{3,2,1,0:T(8,128)S(1)}, u32[]{:S(2)}, u32[]{:S(2)}) collective-permute-start(f32[2,6,32,256]{3,2,1,0:T(8,128)S(1)} %slice.33), channel_id=1, source_target_pairs={{0,64},{1,65},{2,66},{3,67},{4,68},{5,69},{6,70},{7,71},{8,72},{9,... | collective-permute-start | bytes 1179656 | tf_op jit(solution)/shard_map/ppermute | solution.py:347
  16.3 9.9 %collective-permute-start.6 = (f32[2,6,32,256]{3,2,1,0:T(8,128)S(1)}, f32[2,6,32,256]{3,2,1,0:T(8,128)S(1)}, u32[]{:S(2)}, u32[]{:S(2)}) collective-permute-start(f32[2,6,32,256]{3,2,1,0:T(8,128)S(1)} %slice.37), channel_id=1, source_target_pairs={{0,64},{1,65},{2,66},{3,67},{4,68},{5,69},{6,70},{7,71},{8,72},{9,... | collective-permute-start | bytes 1179656 | tf_op jit(solution)/shard_map/ppermute | solution.py:347
  22.0 6.3 %collective-permute-start.2 = (f32[6,32,256]{2,1,0:T(8,128)S(1)}, f32[6,32,256]{2,1,0:T(8,128)S(1)}, u32[]{:S(2)}, u32[]{:S(2)}) collective-permute-start(f32[6,32,256]{2,1,0:T(8,128)S(1)} %slice_bitcast_fusion.2), channel_id=1, source_target_pairs={{0,192},{1,193},{2,194},{3,195},{4,196},{5,197},{6,198},{7,199},{8... | collective-permute-start | bytes 589832 | tf_op jit(solution)/shard_map/ppermute | solution.py:347
  26.3 4.6 %collective-permute-start.7 = (f32[6,32,256]{2,1,0:T(8,128)S(1)}, f32[6,32,256]{2,1,0:T(8,128)S(1)}, u32[]{:S(2)}, u32[]{:S(2)}) collective-permute-start(f32[6,32,256]{2,1,0:T(8,128)S(1)} %slice_bitcast_fusion), channel_id=1, source_target_pairs={{0,192},{1,193},{2,194},{3,195},{4,196},{5,197},{6,198},{7,199},{8... | collective-permute-start | bytes 589832 | tf_op jit(solution)/shard_map/ppermute | solution.py:347
  28.3 6.3 %collective-permute-start.3 = (f32[6,32,256]{2,1,0:T(8,128)S(1)}, f32[6,32,256]{2,1,0:T(8,128)S(1)}, u32[]{:S(2)}, u32[]{:S(2)}) collective-permute-start(f32[6,32,256]{2,1,0:T(8,128)S(1)} %fusion.1.refs_0_), channel_id=1, source_target_pairs={{0,1},{1,0},{2,3},{3,2},{4,5},{5,4},{6,7},{7,6},{8,9},{9,8},{10,11... | collective-permute-start | bytes 589832 | tf_op jit(solution)/shard_map/ppermute | solution.py:347
  28.4 6.2 %collective-permute-start.4 = (f32[6,32,256]{2,1,0:T(8,128)S(1)}, f32[6,32,256]{2,1,0:T(8,128)S(1)}, u32[]{:S(2)}, u32[]{:S(2)}) collective-permute-start(f32[6,32,256]{2,1,0:T(8,128)S(1)} %fusion.1.refs_0_), channel_id=1, source_target_pairs={{0,64},{1,2},{2,1},{3,4},{4,3},{5,6},{6,5},{7,8},{8,7},{9,10},{10,... | collective-permute-start | bytes 589832 | tf_op jit(solution)/shard_map/ppermute | solution.py:347
  30.9 6.2 %collective-permute-start.8 = (f32[6,32,256]{2,1,0:T(8,128)S(1)}, f32[6,32,256]{2,1,0:T(8,128)S(1)}, u32[]{:S(2)}, u32[]{:S(2)}) collective-permute-start(f32[6,32,256]{2,1,0:T(8,128)S(1)} %fusion.refs_3_), channel_id=1, source_target_pairs={{0,1},{1,0},{2,3},{3,2},{4,5},{5,4},{6,7},{7,6},{8,9},{9,8},{10,11... | collective-permute-start | bytes 589832 | tf_op jit(solution)/shard_map/ppermute | solution.py:347
  31.3 7.1 %collective-permute-start.9 = (f32[6,32,256]{2,1,0:T(8,128)S(1)}, f32[6,32,256]{2,1,0:T(8,128)S(1)}, u32[]{:S(2)}, u32[]{:S(2)}) collective-permute-start(f32[6,32,256]{2,1,0:T(8,128)S(1)} %fusion.refs_3_), channel_id=1, source_target_pairs={{0,64},{1,2},{2,1},{3,4},{4,3},{5,6},{6,5},{7,8},{8,7},{9,10},{10,... | collective-permute-start | bytes 589832 | tf_op jit(solution)/shard_map/ppermute | solution.py:347
  39.2 3.6 %collective-permute-start.10 = (f32[136,128]{1,0:T(8,128)S(1)}, f32[136,128]{1,0:T(8,128)S(1)}, u32[]{:S(2)}, u32[]{:S(2)}) collective-permute-start(f32[136,128]{1,0:T(8,128)S(1)} %constant_dynamic-slice_fusion), channel_id=1, source_target_pairs={{0,32},{32,0},{64,96},{96,64},{128,160},{160,128},{192,224},{224,1... | collective-permute-start | bytes 208904 | tf_op jit(solution)/shard_map/ppermute | solution.py:338
  42.8 7.5 %collective-permute-start.11 = (f32[136,128]{1,0:T(8,128)S(1)}, f32[136,128]{1,0:T(8,128)S(1)}, u32[]{:S(2)}, u32[]{:S(2)}) collective-permute-start(f32[136,128]{1,0:T(8,128)S(1)} %dynamic-slice_add_fusion), channel_id=1, source_target_pairs={{0,224},{1,39},{2,36},{3,227},{4,228},{5,35},{6,32},{7,231},{8,46}... | collective-permute-start | bytes 208904 | tf_op jit(solution)/shard_map/ppermute | solution.py:347
  50.4 5.0 %collective-permute-start.12 = (f32[136,128]{1,0:T(8,128)S(1)}, f32[136,128]{1,0:T(8,128)S(1)}, u32[]{:S(2)}, u32[]{:S(2)}) collective-permute-start(f32[136,128]{1,0:T(8,128)S(1)} %add.63), channel_id=1, source_target_pairs={{0,56},{1,225},{2,226},{3,59},{4,60},{5,229},{6,230},{7,63},{8,232... | collective-permute-start | bytes 208904 | tf_op jit(solution)/shard_map/ppermute | solution.py:347
  55.4 7.0 %collective-permute-start.13 = (f32[136,128]{1,0:T(8,128)S(1)}, f32[136,128]{1,0:T(8,128)S(1)}, u32[]{:S(2)}, u32[]{:S(2)}) collective-permute-start(f32[136,128]{1,0:T(8,128)S(1)} %add.64), channel_id=1, source_target_pairs={{0,38},{1,57},{2,58},{3,37},{4,34},{5,61},{6,62},{7,33},{8,48},{9,... | collective-permute-start | bytes 208904 | tf_op jit(solution)/shard_map/ppermute | solution.py:347
  62.4 5.2 %collective-permute-start.16 = (f32[136,128]{1,0:T(8,128)S(1)}, f32[136,128]{1,0:T(8,128)S(1)}, u32[]{:S(2)}, u32[]{:S(2)}) collective-permute-start(f32[136,128]{1,0:T(8,128)S(1)} %add.65), channel_id=1, source_target_pairs={{0,72},{1,2},{2,1},{3,75},{4,76},{5,6},{6,5},{7,79},{8,11},{9,65},... | collective-permute-start | bytes 208904 | tf_op jit(solution)/shard_map/ppermute | solution.py:347
  63.7 4.5 %collective-permute-start.14 = (f32[136,128]{1,0:T(8,128)S(1)}, f32[136,128]{1,0:T(8,128)S(1)}, u32[]{:S(2)}, u32[]{:S(2)}) collective-permute-start(f32[136,128]{1,0:T(8,128)S(1)} %add.65), channel_id=1, source_target_pairs={{0,96},{1,32},{2,35},{3,99},{4,100},{5,36},{6,39},{7,103},{8,41},{... | collective-permute-start | bytes 208904 | tf_op jit(solution)/shard_map/ppermute | solution.py:347
  64.3 5.4 %collective-permute-start.15 = (f32[136,128]{1,0:T(8,128)S(1)}, f32[136,128]{1,0:T(8,128)S(1)}, u32[]{:S(2)}, u32[]{:S(2)}) collective-permute-start(f32[136,128]{1,0:T(8,128)S(1)} %add.65), channel_id=1, source_target_pairs={{0,40},{1,35},{2,32},{3,43},{4,44},{5,39},{6,36},{7,47},{8,42},{9,... | collective-permute-start | bytes 208904 | tf_op jit(solution)/shard_map/ppermute | solution.py:347
  69.7 4.4 %collective-permute-start.19 = (f32[136,128]{1,0:T(8,128)S(1)}, f32[136,128]{1,0:T(8,128)S(1)}, u32[]{:S(2)}, u32[]{:S(2)}) collective-permute-start(f32[136,128]{1,0:T(8,128)S(1)} %add_add_fusion.1), channel_id=1, source_target_pairs={{0,3},{1,73},{2,74},{3,0},{4,7},{5,77},{6,78},{7,4},{8,64},{9,10},... | collective-permute-start | bytes 208904 | tf_op jit(solution)/shard_map/ppermute | solution.py:347
  69.8 4.9 %collective-permute-start.17 = (f32[136,128]{1,0:T(8,128)S(1)}, f32[136,128]{1,0:T(8,128)S(1)}, u32[]{:S(2)}, u32[]{:S(2)}) collective-permute-start(f32[136,128]{1,0:T(8,128)S(1)} %add_add_fusion.1), channel_id=1, source_target_pairs={{0,33},{1,97},{2,98},{3,34},{4,37},{5,101},{6,102},{7,38},{8,104},... | collective-permute-start | bytes 208904 | tf_op jit(solution)/shard_map/ppermute | solution.py:347
  71.1 3.7 %collective-permute-start.18 = (f32[136,128]{1,0:T(8,128)S(1)}, f32[136,128]{1,0:T(8,128)S(1)}, u32[]{:S(2)}, u32[]{:S(2)}) collective-permute-start(f32[136,128]{1,0:T(8,128)S(1)} %add_add_fusion.1), channel_id=1, source_target_pairs={{0,34},{1,41},{2,42},{3,33},{4,38},{5,45},{6,46},{7,37},{8,32},{9,... | collective-permute-start | bytes 208904 | tf_op jit(solution)/shard_map/ppermute | solution.py:347
  74.9 1.6 %collective-permute-start.20 = (f32[136,128]{1,0:T(8,128)S(1)}, f32[136,128]{1,0:T(8,128)S(1)}, u32[]{:S(2)}, u32[]{:S(2)}) collective-permute-start(f32[136,128]{1,0:T(8,128)S(1)} %add_add_fusion), channel_id=1, source_target_pairs={{0,32},{32,0},{64,96},{96,64},{128,160},{160,128},{192,224},{224,1... | collective-permute-start | bytes 208904 | tf_op jit(solution)/shard_map/ppermute | solution.py:338
  (1 other events, 0.7 us)

commit v5 on v4

--- a/solution.py
+++ b/solution.py
@@ -50,13 +50,13 @@
                 table[d + 1, rows, :] = mixed.astype(jnp.bfloat16)
 
 
-def step_masks(core):
-    return 1 + 2 * core, 3 - 2 * core
-
-
-def step_order(core):
-    near, far = step_masks(core)
-    return 0, far, near, near ^ far
+def step_masks(side):
+    return 1 + 2 * side, 3 - 2 * side
+
+
+def step_blocks(y, core):
+    near, far = step_masks(core ^ (y & 1))
+    return [2 * (y ^ m) + (core ^ (m & 1)) for m in (0, far, near, near ^ far)]
 
 
 def split(x):
@@ -64,27 +64,29 @@
     return high, (x - high.astype(jnp.float32)).astype(jnp.bfloat16)
 
 
-def sketch_kernel(first, count, snap_hbm, sketch_hbm, shift_hbm, weight_hbm, *refs):
-    send_ref, keep_ref, snap, sketch, turned, table, shift, weight, snap_sem, sem = refs
+def sketch_kernel(first, count, later, snap_ref, sketch_hbm, shift_hbm, weight_hbm, *refs):
+    held_refs = refs[2 : 2 + (later > 0)]
+    send_ref, keep_ref = refs[:2]
+    snap, sketch, turned, table, shift, weight, snap_sem, sem = refs[2 + (later > 0) :]
     heads = [
         pltpu.make_async_copy(sketch_hbm, sketch, sem.at[0]),
         pltpu.make_async_copy(shift_hbm, shift, sem.at[1]),
         pltpu.make_async_copy(weight_hbm, weight, sem.at[2]),
     ]
-    copies = [
-        pltpu.make_async_copy(snap_hbm.at[first + f], snap.at[f], snap_sem.at[f])
-        for f in range(count)
-    ]
+    copies = []
+    if later:
+        places = [snap.at[f] for f in range(count)] + [held_refs[0].at[f] for f in range(later)]
+        copies = [
+            pltpu.make_async_copy(snap_ref.at[f], place, snap_sem.at[f])
+            for f, place in enumerate(places)
+        ]
+    else:
+        snap = snap_ref
     for copy in heads + copies:
         copy.start()
     me = lax.axis_index("tm")
     y, core = me // 2, me % 2
-    other = 1 - core
-    filter_tables(
-        table,
-        [2 * (y ^ m) + other for m in step_order(other)]
-        + [2 * (y ^ m) + core for m in step_order(core)],
-    )
+    filter_tables(table, step_blocks(y, 1 - core) + step_blocks(y, core))
     for copy in heads:
         copy.wait()
     turned[...] = sketch[...].T
@@ -106,8 +108,8 @@
     held = None
     for g in range(0, count + GROUP, GROUP):
         if g < count:
-            for f in range(g, g + GROUP):
-                copies[f].wait()
+            for copy in copies[g : g + GROUP]:
+                copy.wait()
             raws = [
                 jnp.dot(turned[...], snap[f], preferred_element_type=jnp.float32)
                 for f in range(g, g + GROUP)
@@ -116,28 +118,31 @@
             for k in range(GROUP):
                 filtered(g - GROUP + k, held[k])
         held = raws
-
-
-def sketch_call(snaps, sketch, dilation, weight, first, count):
+    for copy in copies[count:]:
+        copy.wait()
+
+
+def sketch_call(snaps, sketch, dilation, weight, first, count, later):
     out = jax.ShapeDtypeStruct((4, count, SHARE, RANK), jnp.float32)
     hbm = pl.BlockSpec(memory_space=pltpu.HBM)
     vmem = pl.BlockSpec(memory_space=pltpu.VMEM)
+    rest = [jax.ShapeDtypeStruct((later, SNAP_DEV, PLANE), jnp.bfloat16)] if later else []
     return pl.pallas_call(
-        functools.partial(sketch_kernel, first, count),
-        in_specs=[hbm] * 4,
-        out_specs=[vmem] * 2,
-        out_shape=[out] * 2,
+        functools.partial(sketch_kernel, first, count, later),
+        in_specs=[hbm if later else vmem] + [hbm] * 3,
+        out_specs=[vmem] * (2 + len(rest)),
+        out_shape=[out] * 2 + rest,
         scratch_shapes=[
-            pltpu.VMEM((count, SNAP_DEV, PLANE), jnp.bfloat16),
+            pltpu.VMEM((count if later else 1, SNAP_DEV, PLANE), jnp.bfloat16),
             pltpu.VMEM((SNAP_DEV, RANK), jnp.bfloat16),
             pltpu.VMEM((RANK, SNAP_DEV), jnp.bfloat16),
             pltpu.VMEM((DILATIONS + 1, PLANE, PLANE), jnp.bfloat16),
             pltpu.SMEM((FIELDS,), jnp.int32),
             pltpu.SMEM((FIELDS,), jnp.float32),
-            pltpu.SemaphoreType.DMA((count,)),
+            pltpu.SemaphoreType.DMA((count + later,)),
             pltpu.SemaphoreType.DMA((3,)),
         ],
-        compiler_params=pltpu.CompilerParams(vmem_limit_bytes=50 * 2**20),
+        compiler_params=pltpu.CompilerParams(vmem_limit_bytes=46 * 2**20),
         cost_estimate=pl.CostEstimate(
             flops=count * 2**28, bytes_accessed=count * 2**20, transcendentals=0
         ),
@@ -348,7 +353,9 @@
 
 
 def step_swap(x, which):
-    return permute(x, lambda y, c, gx, gz: (y ^ step_masks(c)[which], c, gx, gz))
+    return permute(
+        x, lambda y, c, gx, gz: (y ^ step_masks(c ^ (y & 1))[which], c ^ 1, gx, gz)
+    )
 
 
 def halo_swap(x, which):
@@ -395,7 +402,7 @@
     )
 
 
-PARTS = ((0, 6), (6, 6))
+PARTS = ((0, 6, 6), (6, 6, 0))
 def single(a, b):
     return ((a, b),)
 
@@ -420,8 +427,11 @@
 def shards(snapshots, sketch, volume, grad_weight, dilation):
     snaps = jnp.transpose(snapshots[:, :, 0, :], (1, 0, 2))
     parts = []
-    for first, count in PARTS:
-        send, keep = sketch_call(snaps, sketch, dilation, grad_weight, first, count)
+    for first, count, later in PARTS:
+        send, keep, *snaps = sketch_call(
+            snaps, sketch, dilation, grad_weight, first, count, later
+        )
+        snaps = snaps[0] if snaps else None
         image = sum_along_y(keep + swap(send, "tm", 1))
         parts += [image, halo_swap(image, 0), halo_swap(image, 1)]
     panel, gram = panel_call(volume, [p.shape[0] for p in parts[::3]], parts)

time: 86.5 us -> 84.9 us (0.982)
  starting transfers between devices: 34.7 us -> 26.6 us
  waiting for transfers between devices: 29.8 us -> 37.8 us
  Pallas kernels: 17.6 us -> 16.4 us
    ppermute x17, waiting for transfers between devices: 27 us -> 34.8 us  [permute(): return lax.ppermute(x, ('tm', 'space'), pairs)]
    ppermute x17, starting transfers between devices: 28 us -> 22.6 us  [permute(): return lax.ppermute(x, ('tm', 'space'), pairs)]
    ppermute x4, starting transfers between devices: 6.76 us -> 4 us  [swap(): lax.ppermute(x, axis, [(i, i ^ mask) for i in range(lax.axis_size(axis))])]
    pallas_call x2, Pallas kernels: 7.41 us -> 6.28 us  [sketch_call(): pl.pallas_call(functools.partial(sketch_kernel, first, count, later), in_...]
  transfers between devices with their start and end apart: 21 -> 21, of which waited for: 18 -> 15; matrix products, arithmetic and copies ran while one was open for 1% -> 1% of each run, Pallas kernels for 4% -> 3%
where the time goes in v5:
time: 84.9 us; the launch traced here: 84.7 us
  waiting for transfers between devices  37.8 us (45%)
  starting transfers between devices  26.6 us (31%)
  Pallas kernels  16.4 us (19%)
  local copies, waits for them, and re-layouts  2.45 us (3%)
  between operations  0.85 us (1%)
    ppermute x17, waiting for transfers between devices, permute(): return lax.ppermute(x, ('tm', 'space'), pairs)  34.8 us
    ppermute x17, starting transfers between devices, permute(): return lax.ppermute(x, ('tm', 'space'), pairs)  22.6 us
    pallas_call x1, Pallas kernels, basis_call(): pl.pallas_call(basis_kernel, in_specs=[vmem, vmem], out_specs=[vmem, vmem...  9.4 us
    pallas_call x2, Pallas kernels, sketch_call(): pl.pallas_call(functools.partial(sketch_kernel, first, count, later), in_...  6.28 us
    ppermute x4, starting transfers between devices, swap(): lax.ppermute(x, axis, [(i, i ^ mask) for i in range(lax.axis_size(axis))])  4 us
    ppermute x4, waiting for transfers between devices, swap(): lax.ppermute(x, axis, [(i, i ^ mask) for i in range(lax.axis_size(axis))])  2.96 us
    unnamed x8, local copies, waits for them, and re-layouts  2.35 us
  transfers between devices with their start and end apart: 21, of which 15 were waited for; matrix products, arithmetic and copies ran while one was open for 1% of the time, Pallas kernels for 3%

profile of v5, /device:TPU:1, one launch (start us, length us, event | category | flops | bytes accessed | tf_op | source)
XLA Modules:
  0.0 84.7 jit_solution(12882595468866214566)
XLA Ops:
  3.0 3.8 %shard_map.68 = (f32[4,6,32,256]{3,2,1,0:T(8,128)S(1)}, f32[4,6,32,256]{3,2,1,0:T(8,128)S(1)}, bf16[6,1024,256]{2,1,0:T(8,128)(2,1)S(1)}) custom-call(bf16[12,1024,256]{2,1,0:T(8,128)(2,1)} %bitcast.16, bf16[1024,256]{1,0:T(8,128)(2,1)S(1)} %copy-done, s32[12]{0:T(128)S(1)} %copy-done.2, f32[12]{0:T(128)S(1)} %copy-done.3), custom_call_target="tpu_custom_call" | custom-call | flops 1610612736 | bytes 6291456 | tf_op jit(solution)/shard_map/pallas_call | solution.py:130
  6.8 3.3 %collective-permute-start = (f32[4,6,32,256]{3,2,1,0:T(8,128)S(1)}, f32[4,6,32,256]{3,2,1,0:T(8,128)S(1)}, u32[]{:S(2)}, u32[]{:S(2)}) collective-permute-start(f32[4,6,32,256]{3,2,1,0:T(8,128)S(1)} %get-tuple-element.12), channel_id=1, source_target_pairs={{0,32},{32,0},{64,96},{96,64},{128,160},{160,128},{192,224},{224,1... | collective-permute-start | bytes 2359304 | tf_op jit(solution)/shard_map/ppermute | solution.py:343
  10.1 2.5 %shard_map.69 = (f32[4,6,32,256]{3,2,1,0:T(8,128)S(1)}, f32[4,6,32,256]{3,2,1,0:T(8,128)S(1)}) custom-call(bf16[6,1024,256]{2,1,0:T(8,128)(2,1)S(1)} %get-tuple-element.13.snap_ref, bf16[1024,256]{1,0:T(8,128)(2,1)S(1)} %copy-done, s32[12]{0:T(128)S(1)} %copy-done.2, f32[12]{0:T(128)S(1)} %copy-done.3), custom_call_target="tpu_custom_call" | custom-call | flops 1610612736 | bytes 6291456 | tf_op jit(solution)/shard_map/pallas_call | solution.py:130
  12.9 1.5 %collective-permute-start.1 = (f32[2,6,32,256]{3,2,1,0:T(8,128)S(1)}, f32[2,6,32,256]{3,2,1,0:T(8,128)S(1)}, u32[]{:S(2)}, u32[]{:S(2)}) collective-permute-start(f32[2,6,32,256]{3,2,1,0:T(8,128)S(1)} %slice.33), channel_id=1, source_target_pairs={{0,96},{1,97},{2,98},{3,99},{4,100},{5,101},{6,102},{7,103},{8,104... | collective-permute-start | bytes 1179656 | tf_op jit(solution)/shard_map/ppermute | solution.py:352
  15.2 1.1 %collective-permute-start.6 = (f32[2,6,32,256]{3,2,1,0:T(8,128)S(1)}, f32[2,6,32,256]{3,2,1,0:T(8,128)S(1)}, u32[]{:S(2)}, u32[]{:S(2)}) collective-permute-start(f32[2,6,32,256]{3,2,1,0:T(8,128)S(1)} %slice.37), channel_id=1, source_target_pairs={{0,96},{1,97},{2,98},{3,99},{4,100},{5,101},{6,102},{7,103},{8,104... | collective-permute-start | bytes 1179656 | tf_op jit(solution)/shard_map/ppermute | solution.py:352
  16.3 5.1 %collective-permute-done.1 = f32[2,6,32,256]{3,2,1,0:T(8,128)S(1)} collective-permute-done((f32[2,6,32,256]{3,2,1,0:T(8,128)S(1)}, f32[2,6,32,256]{3,2,1,0:T(8,128)S(1)}, u32[]{:S(2)}, u32[]{:S(2)}) %collective-permute-start.1) | collective-permute-done | bytes 393248 | tf_op jit(solution)/shard_map/ppermute | solution.py:352
  21.6 5.5 %collective-permute-done.6 = f32[2,6,32,256]{3,2,1,0:T(8,128)S(1)} collective-permute-done((f32[2,6,32,256]{3,2,1,0:T(8,128)S(1)}, f32[2,6,32,256]{3,2,1,0:T(8,128)S(1)}, u32[]{:S(2)}, u32[]{:S(2)}) %collective-permute-start.6) | collective-permute-done | bytes 393248 | tf_op jit(solution)/shard_map/ppermute | solution.py:352
  27.4 1.8 %collective-permute-start.4 = (f32[6,32,256]{2,1,0:T(8,128)S(1)}, f32[6,32,256]{2,1,0:T(8,128)S(1)}, u32[]{:S(2)}, u32[]{:S(2)}) collective-permute-start(f32[6,32,256]{2,1,0:T(8,128)S(1)} %fusion.1.refs_0_), channel_id=1, source_target_pairs={{0,64},{1,2},{2,1},{3,4},{4,3},{5,6},{6,5},{7,8},{8,7},{9,10},{10,... | collective-permute-start | bytes 589832 | tf_op jit(solution)/shard_map/ppermute | solution.py:352
  29.3 5.1 %collective-permute-done.7 = f32[6,32,256]{2,1,0:T(8,128)S(1)} collective-permute-done((f32[6,32,256]{2,1,0:T(8,128)S(1)}, f32[6,32,256]{2,1,0:T(8,128)S(1)}, u32[]{:S(2)}, u32[]{:S(2)}) %collective-permute-start.7) | collective-permute-done | bytes 196640 | tf_op jit(solution)/shard_map/ppermute | solution.py:352
  34.6 5.7 %collective-permute-done.8.refs_4_ = f32[6,32,256]{2,1,0:T(8,128)S(1)} collective-permute-done((f32[6,32,256]{2,1,0:T(8,128)S(1)}, f32[6,32,256]{2,1,0:T(8,128)S(1)}, u32[]{:S(2)}, u32[]{:S(2)}) %collective-permute-start.8) | collective-permute-done | bytes 196640 | tf_op jit(solution)/shard_map/ppermute | solution.py:352
  41.3 1.2 %collective-permute-done.10 = f32[136,128]{1,0:T(8,128)S(1)} collective-permute-done((f32[136,128]{1,0:T(8,128)S(1)}, f32[136,128]{1,0:T(8,128)S(1)}, u32[]{:S(2)}, u32[]{:S(2)}) %collective-permute-start.10) | collective-permute-done | bytes 69664 | tf_op jit(solution)/shard_map/ppermute | solution.py:343
  42.5 4.5 %collective-permute-start.11 = (f32[136,128]{1,0:T(8,128)S(1)}, f32[136,128]{1,0:T(8,128)S(1)}, u32[]{:S(2)}, u32[]{:S(2)}) collective-permute-start(f32[136,128]{1,0:T(8,128)S(1)} %dynamic-slice_add_fusion), channel_id=1, source_target_pairs={{0,224},{1,39},{2,36},{3,227},{4,228},{5,35},{6,32},{7,231},{8,46}... | collective-permute-start | bytes 208904 | tf_op jit(solution)/shard_map/ppermute | solution.py:352
  47.0 2.0 %collective-permute-done.11 = f32[136,128]{1,0:T(8,128)S(1)} collective-permute-done((f32[136,128]{1,0:T(8,128)S(1)}, f32[136,128]{1,0:T(8,128)S(1)}, u32[]{:S(2)}, u32[]{:S(2)}) %collective-permute-start.11) | collective-permute-done | bytes 69664 | tf_op jit(solution)/shard_map/ppermute | solution.py:352
  49.0 1.8 %collective-permute-start.12 = (f32[136,128]{1,0:T(8,128)S(1)}, f32[136,128]{1,0:T(8,128)S(1)}, u32[]{:S(2)}, u32[]{:S(2)}) collective-permute-start(f32[136,128]{1,0:T(8,128)S(1)} %add.63), channel_id=1, source_target_pairs={{0,56},{1,225},{2,226},{3,59},{4,60},{5,229},{6,230},{7,63},{8,232... | collective-permute-start | bytes 208904 | tf_op jit(solution)/shard_map/ppermute | solution.py:352
  50.8 3.5 %collective-permute-done.12 = f32[136,128]{1,0:T(8,128)S(1)} collective-permute-done((f32[136,128]{1,0:T(8,128)S(1)}, f32[136,128]{1,0:T(8,128)S(1)}, u32[]{:S(2)}, u32[]{:S(2)}) %collective-permute-start.12) | collective-permute-done | bytes 69664 | tf_op jit(solution)/shard_map/ppermute | solution.py:352
  54.4 4.5 %collective-permute-start.13 = (f32[136,128]{1,0:T(8,128)S(1)}, f32[136,128]{1,0:T(8,128)S(1)}, u32[]{:S(2)}, u32[]{:S(2)}) collective-permute-start(f32[136,128]{1,0:T(8,128)S(1)} %add.64), channel_id=1, source_target_pairs={{0,38},{1,57},{2,58},{3,37},{4,34},{5,61},{6,62},{7,33},{8,48},{9,... | collective-permute-start | bytes 208904 | tf_op jit(solution)/shard_map/ppermute | solution.py:352
  58.8 2.1 %collective-permute-done.13 = f32[136,128]{1,0:T(8,128)S(1)} collective-permute-done((f32[136,128]{1,0:T(8,128)S(1)}, f32[136,128]{1,0:T(8,128)S(1)}, u32[]{:S(2)}, u32[]{:S(2)}) %collective-permute-start.13) | collective-permute-done | bytes 69664 | tf_op jit(solution)/shard_map/ppermute | solution.py:352
  60.9 1.6 %collective-permute-start.16 = (f32[136,128]{1,0:T(8,128)S(1)}, f32[136,128]{1,0:T(8,128)S(1)}, u32[]{:S(2)}, u32[]{:S(2)}) collective-permute-start(f32[136,128]{1,0:T(8,128)S(1)} %add.65), channel_id=1, source_target_pairs={{0,72},{1,2},{2,1},{3,75},{4,76},{5,6},{6,5},{7,79},{8,11},{9,65},... | collective-permute-start | bytes 208904 | tf_op jit(solution)/shard_map/ppermute | solution.py:352
  62.7 2.1 %collective-permute-start.15 = (f32[136,128]{1,0:T(8,128)S(1)}, f32[136,128]{1,0:T(8,128)S(1)}, u32[]{:S(2)}, u32[]{:S(2)}) collective-permute-start(f32[136,128]{1,0:T(8,128)S(1)} %add.65), channel_id=1, source_target_pairs={{0,40},{1,35},{2,32},{3,43},{4,44},{5,39},{6,36},{7,47},{8,42},{9,... | collective-permute-start | bytes 208904 | tf_op jit(solution)/shard_map/ppermute | solution.py:352
  64.8 1.3 %collective-permute-done.16 = f32[136,128]{1,0:T(8,128)S(1)} collective-permute-done((f32[136,128]{1,0:T(8,128)S(1)}, f32[136,128]{1,0:T(8,128)S(1)}, u32[]{:S(2)}, u32[]{:S(2)}) %collective-permute-start.16) | collective-permute-done | bytes 69664 | tf_op jit(solution)/shard_map/ppermute | solution.py:352
  66.1 1.4 %collective-permute-done.14 = f32[136,128]{1,0:T(8,128)S(1)} collective-permute-done((f32[136,128]{1,0:T(8,128)S(1)}, f32[136,128]{1,0:T(8,128)S(1)}, u32[]{:S(2)}, u32[]{:S(2)}) %collective-permute-start.14) | collective-permute-done | bytes 69664 | tf_op jit(solution)/shard_map/ppermute | solution.py:352
  67.7 2.3 %collective-permute-start.17 = (f32[136,128]{1,0:T(8,128)S(1)}, f32[136,128]{1,0:T(8,128)S(1)}, u32[]{:S(2)}, u32[]{:S(2)}) collective-permute-start(f32[136,128]{1,0:T(8,128)S(1)} %add_add_fusion.1), channel_id=1, source_target_pairs={{0,33},{1,97},{2,98},{3,34},{4,37},{5,101},{6,102},{7,38},{8,104},... | collective-permute-start | bytes 208904 | tf_op jit(solution)/shard_map/ppermute | solution.py:352
  70.6 1.4 %collective-permute-done.19 = f32[136,128]{1,0:T(8,128)S(1)} collective-permute-done((f32[136,128]{1,0:T(8,128)S(1)}, f32[136,128]{1,0:T(8,128)S(1)}, u32[]{:S(2)}, u32[]{:S(2)}) %collective-permute-start.19) | collective-permute-done | bytes 69664 | tf_op jit(solution)/shard_map/ppermute | solution.py:352
  75.3 9.4 %shard_map.71 = (f32[768,128]{1,0:T(8,128)}, f32[256,256]{1,0:T(8,128)}) custom-call(f32[272,128]{1,0:T(8,128)S(1)} %maximum_select_fusion.gram_ref, f32[12,32,256]{2,1,0:T(8,128)S(1)} %get-tuple-element.17.panel_ref), custom_call_target="tpu_custom_call" | custom-call | tf_op jit(solution)/shard_map/pallas_call | solution.py:329
  (48 shorter events, 9.3 us)
Async XLA Ops:
  0.6 1.0 %copy-start = (bf16[1024,256]{1,0:T(8,128)(2,1)S(1)}, bf16[1024,256]{1,0:T(8,128)(2,1)}, u32[]{:S(2)}) copy-start(bf16[1024,256]{1,0:T(8,128)(2,1)} %sketch_hbm.3) | copy-start | bytes 1572868
  2.3 0.7 copy-start.3
  6.8 6.0 %collective-permute-start = (f32[4,6,32,256]{3,2,1,0:T(8,128)S(1)}, f32[4,6,32,256]{3,2,1,0:T(8,128)S(1)}, u32[]{:S(2)}, u32[]{:S(2)}) collective-permute-start(f32[4,6,32,256]{3,2,1,0:T(8,128)S(1)} %get-tuple-element.12), channel_id=1, source_target_pairs={{0,32},{32,0},{64,96},{96,64},{128,160},{160,128},{192,224},{224,1... | collective-permute-start | bytes 2359304 | tf_op jit(solution)/shard_map/ppermute | solution.py:343
  12.6 27.8 %copy-start.1 = (f32[1,256]{1,0:T(1,128)S(1)}, f32[1,256]{1,0:T(1,128)}, u32[]{:S(2)}) copy-start(f32[1,256]{1,0:T(1,128)} %volume_ref.1) | copy-start | bytes 3076
  12.6 2.4 %collective-permute-start.5 = (f32[4,6,32,256]{3,2,1,0:T(8,128)S(1)}, f32[4,6,32,256]{3,2,1,0:T(8,128)S(1)}, u32[]{:S(2)}, u32[]{:S(2)}) collective-permute-start(f32[4,6,32,256]{3,2,1,0:T(8,128)S(1)} %get-tuple-element.15), channel_id=1, source_target_pairs={{0,32},{32,0},{64,96},{96,64},{128,160},{160,128},{192,224},{224,1... | collective-permute-start | bytes 2359304 | tf_op jit(solution)/shard_map/ppermute | solution.py:343
  12.9 8.5 %collective-permute-start.1 = (f32[2,6,32,256]{3,2,1,0:T(8,128)S(1)}, f32[2,6,32,256]{3,2,1,0:T(8,128)S(1)}, u32[]{:S(2)}, u32[]{:S(2)}) collective-permute-start(f32[2,6,32,256]{3,2,1,0:T(8,128)S(1)} %slice.33), channel_id=1, source_target_pairs={{0,96},{1,97},{2,98},{3,99},{4,100},{5,101},{6,102},{7,103},{8,104... | collective-permute-start | bytes 1179656 | tf_op jit(solution)/shard_map/ppermute | solution.py:352
  15.2 11.9 %collective-permute-start.6 = (f32[2,6,32,256]{3,2,1,0:T(8,128)S(1)}, f32[2,6,32,256]{3,2,1,0:T(8,128)S(1)}, u32[]{:S(2)}, u32[]{:S(2)}) collective-permute-start(f32[2,6,32,256]{3,2,1,0:T(8,128)S(1)} %slice.37), channel_id=1, source_target_pairs={{0,96},{1,97},{2,98},{3,99},{4,100},{5,101},{6,102},{7,103},{8,104... | collective-permute-start | bytes 1179656 | tf_op jit(solution)/shard_map/ppermute | solution.py:352
  21.5 5.8 %collective-permute-start.2 = (f32[6,32,256]{2,1,0:T(8,128)S(1)}, f32[6,32,256]{2,1,0:T(8,128)S(1)}, u32[]{:S(2)}, u32[]{:S(2)}) collective-permute-start(f32[6,32,256]{2,1,0:T(8,128)S(1)} %slice_bitcast_fusion.2), channel_id=1, source_target_pairs={{0,224},{1,225},{2,226},{3,227},{4,228},{5,229},{6,230},{7,231},{8... | collective-permute-start | bytes 589832 | tf_op jit(solution)/shard_map/ppermute | solution.py:352
  27.2 7.2 %collective-permute-start.7 = (f32[6,32,256]{2,1,0:T(8,128)S(1)}, f32[6,32,256]{2,1,0:T(8,128)S(1)}, u32[]{:S(2)}, u32[]{:S(2)}) collective-permute-start(f32[6,32,256]{2,1,0:T(8,128)S(1)} %slice_bitcast_fusion), channel_id=1, source_target_pairs={{0,224},{1,225},{2,226},{3,227},{4,228},{5,229},{6,230},{7,231},{8... | collective-permute-start | bytes 589832 | tf_op jit(solution)/shard_map/ppermute | solution.py:352
  27.3 7.3 %collective-permute-start.3 = (f32[6,32,256]{2,1,0:T(8,128)S(1)}, f32[6,32,256]{2,1,0:T(8,128)S(1)}, u32[]{:S(2)}, u32[]{:S(2)}) collective-permute-start(f32[6,32,256]{2,1,0:T(8,128)S(1)} %fusion.1.refs_0_), channel_id=1, source_target_pairs={{0,1},{1,0},{2,3},{3,2},{4,5},{5,4},{6,7},{7,6},{8,9},{9,8},{10,11... | collective-permute-start | bytes 589832 | tf_op jit(solution)/shard_map/ppermute | solution.py:352
  27.4 7.2 %collective-permute-start.4 = (f32[6,32,256]{2,1,0:T(8,128)S(1)}, f32[6,32,256]{2,1,0:T(8,128)S(1)}, u32[]{:S(2)}, u32[]{:S(2)}) collective-permute-start(f32[6,32,256]{2,1,0:T(8,128)S(1)} %fusion.1.refs_0_), channel_id=1, source_target_pairs={{0,64},{1,2},{2,1},{3,4},{4,3},{5,6},{6,5},{7,8},{8,7},{9,10},{10,... | collective-permute-start | bytes 589832 | tf_op jit(solution)/shard_map/ppermute | solution.py:352
  34.4 6.0 %collective-permute-start.8 = (f32[6,32,256]{2,1,0:T(8,128)S(1)}, f32[6,32,256]{2,1,0:T(8,128)S(1)}, u32[]{:S(2)}, u32[]{:S(2)}) collective-permute-start(f32[6,32,256]{2,1,0:T(8,128)S(1)} %fusion.refs_3_), channel_id=1, source_target_pairs={{0,1},{1,0},{2,3},{3,2},{4,5},{5,4},{6,7},{7,6},{8,9},{9,8},{10,11... | collective-permute-start | bytes 589832 | tf_op jit(solution)/shard_map/ppermute | solution.py:352
  34.5 5.9 %collective-permute-start.9 = (f32[6,32,256]{2,1,0:T(8,128)S(1)}, f32[6,32,256]{2,1,0:T(8,128)S(1)}, u32[]{:S(2)}, u32[]{:S(2)}) collective-permute-start(f32[6,32,256]{2,1,0:T(8,128)S(1)} %fusion.refs_3_), channel_id=1, source_target_pairs={{0,64},{1,2},{2,1},{3,4},{4,3},{5,6},{6,5},{7,8},{8,7},{9,10},{10,... | collective-permute-start | bytes 589832 | tf_op jit(solution)/shard_map/ppermute | solution.py:352
  41.2 1.3 %collective-permute-start.10 = (f32[136,128]{1,0:T(8,128)S(1)}, f32[136,128]{1,0:T(8,128)S(1)}, u32[]{:S(2)}, u32[]{:S(2)}) collective-permute-start(f32[136,128]{1,0:T(8,128)S(1)} %constant_dynamic-slice_fusion), channel_id=1, source_target_pairs={{0,32},{32,0},{64,96},{96,64},{128,160},{160,128},{192,224},{224,1... | collective-permute-start | bytes 208904 | tf_op jit(solution)/shard_map/ppermute | solution.py:343
  42.5 6.5 %collective-permute-start.11 = (f32[136,128]{1,0:T(8,128)S(1)}, f32[136,128]{1,0:T(8,128)S(1)}, u32[]{:S(2)}, u32[]{:S(2)}) collective-permute-start(f32[136,128]{1,0:T(8,128)S(1)} %dynamic-slice_add_fusion), channel_id=1, source_target_pairs={{0,224},{1,39},{2,36},{3,227},{4,228},{5,35},{6,32},{7,231},{8,46}... | collective-permute-start | bytes 208904 | tf_op jit(solution)/shard_map/ppermute | solution.py:352
  49.0 5.3 %collective-permute-start.12 = (f32[136,128]{1,0:T(8,128)S(1)}, f32[136,128]{1,0:T(8,128)S(1)}, u32[]{:S(2)}, u32[]{:S(2)}) collective-permute-start(f32[136,128]{1,0:T(8,128)S(1)} %add.63), channel_id=1, source_target_pairs={{0,56},{1,225},{2,226},{3,59},{4,60},{5,229},{6,230},{7,63},{8,232... | collective-permute-start | bytes 208904 | tf_op jit(solution)/shard_map/ppermute | solution.py:352
  54.4 6.5 %collective-permute-start.13 = (f32[136,128]{1,0:T(8,128)S(1)}, f32[136,128]{1,0:T(8,128)S(1)}, u32[]{:S(2)}, u32[]{:S(2)}) collective-permute-start(f32[136,128]{1,0:T(8,128)S(1)} %add.64), channel_id=1, source_target_pairs={{0,38},{1,57},{2,58},{3,37},{4,34},{5,61},{6,62},{7,33},{8,48},{9,... | collective-permute-start | bytes 208904 | tf_op jit(solution)/shard_map/ppermute | solution.py:352
  60.9 5.2 %collective-permute-start.16 = (f32[136,128]{1,0:T(8,128)S(1)}, f32[136,128]{1,0:T(8,128)S(1)}, u32[]{:S(2)}, u32[]{:S(2)}) collective-permute-start(f32[136,128]{1,0:T(8,128)S(1)} %add.65), channel_id=1, source_target_pairs={{0,72},{1,2},{2,1},{3,75},{4,76},{5,6},{6,5},{7,79},{8,11},{9,65},... | collective-permute-start | bytes 208904 | tf_op jit(solution)/shard_map/ppermute | solution.py:352
  62.5 5.0 %collective-permute-start.14 = (f32[136,128]{1,0:T(8,128)S(1)}, f32[136,128]{1,0:T(8,128)S(1)}, u32[]{:S(2)}, u32[]{:S(2)}) collective-permute-start(f32[136,128]{1,0:T(8,128)S(1)} %add.65), channel_id=1, source_target_pairs={{0,96},{1,32},{2,35},{3,99},{4,100},{5,36},{6,39},{7,103},{8,41},{... | collective-permute-start | bytes 208904 | tf_op jit(solution)/shard_map/ppermute | solution.py:352
  62.7 4.9 %collective-permute-start.15 = (f32[136,128]{1,0:T(8,128)S(1)}, f32[136,128]{1,0:T(8,128)S(1)}, u32[]{:S(2)}, u32[]{:S(2)}) collective-permute-start(f32[136,128]{1,0:T(8,128)S(1)} %add.65), channel_id=1, source_target_pairs={{0,40},{1,35},{2,32},{3,43},{4,44},{5,39},{6,36},{7,47},{8,42},{9,... | collective-permute-start | bytes 208904 | tf_op jit(solution)/shard_map/ppermute | solution.py:352
  67.6 4.4 %collective-permute-start.19 = (f32[136,128]{1,0:T(8,128)S(1)}, f32[136,128]{1,0:T(8,128)S(1)}, u32[]{:S(2)}, u32[]{:S(2)}) collective-permute-start(f32[136,128]{1,0:T(8,128)S(1)} %add_add_fusion.1), channel_id=1, source_target_pairs={{0,3},{1,73},{2,74},{3,0},{4,7},{5,77},{6,78},{7,4},{8,64},{9,10},... | collective-permute-start | bytes 208904 | tf_op jit(solution)/shard_map/ppermute | solution.py:352
  67.7 5.1 %collective-permute-start.17 = (f32[136,128]{1,0:T(8,128)S(1)}, f32[136,128]{1,0:T(8,128)S(1)}, u32[]{:S(2)}, u32[]{:S(2)}) collective-permute-start(f32[136,128]{1,0:T(8,128)S(1)} %add_add_fusion.1), channel_id=1, source_target_pairs={{0,33},{1,97},{2,98},{3,34},{4,37},{5,101},{6,102},{7,38},{8,104},... | collective-permute-start | bytes 208904 | tf_op jit(solution)/shard_map/ppermute | solution.py:352
  69.9 3.7 %collective-permute-start.18 = (f32[136,128]{1,0:T(8,128)S(1)}, f32[136,128]{1,0:T(8,128)S(1)}, u32[]{:S(2)}, u32[]{:S(2)}) collective-permute-start(f32[136,128]{1,0:T(8,128)S(1)} %add_add_fusion.1), channel_id=1, source_target_pairs={{0,34},{1,41},{2,42},{3,33},{4,38},{5,45},{6,46},{7,37},{8,32},{9,... | collective-permute-start | bytes 208904 | tf_op jit(solution)/shard_map/ppermute | solution.py:352
  73.7 1.6 %collective-permute-start.20 = (f32[136,128]{1,0:T(8,128)S(1)}, f32[136,128]{1,0:T(8,128)S(1)}, u32[]{:S(2)}, u32[]{:S(2)}) collective-permute-start(f32[136,128]{1,0:T(8,128)S(1)} %add_add_fusion), channel_id=1, source_target_pairs={{0,32},{32,0},{64,96},{96,64},{128,160},{160,128},{192,224},{224,1... | collective-permute-start | bytes 208904 | tf_op jit(solution)/shard_map/ppermute | solution.py:343
  (1 other events, 0.7 us)

commit v6 on v5

--- a/solution.py
+++ b/solution.py
@@ -17,7 +17,7 @@
 NZ = 32
 ROWS = 98304
 HALF = 128
-GROUP = 3
+GROUP = 4
 DILATIONS = 4
 EXACT = lax.Precision.HIGHEST
 
@@ -402,7 +402,7 @@
     )
 
 
-PARTS = ((0, 6, 6), (6, 6, 0))
+PARTS = ((0, 8, 4), (8, 4, 0))
 def single(a, b):
     return ((a, b),)
 

time: 84.9 us -> 87.7 us (1.033)
  starting transfers between devices: 26.6 us -> 34.5 us
  waiting for transfers between devices: 37.8 us -> 32.5 us
    ppermute x17, starting transfers between devices: 22.6 us -> 27.7 us  [permute(): return lax.ppermute(x, ('tm', 'space'), pairs)]
    ppermute x17, waiting for transfers between devices: 34.8 us -> 30.4 us  [permute(): return lax.ppermute(x, ('tm', 'space'), pairs)]
    ppermute x4, starting transfers between devices: 4 us -> 6.71 us  [swap(): lax.ppermute(x, axis, [(i, i ^ mask) for i in range(lax.axis_size(axis))])]
  transfers between devices with their start and end apart: 21 -> 21, of which waited for: 15 -> 18; matrix products, arithmetic and copies ran while one was open for 1% -> 1% of each run, Pallas kernels for 3% -> 2%
where the time goes in v6:
time: 87.7 us; the launch traced here: 87.1 us
  starting transfers between devices  34.5 us (39%)
  waiting for transfers between devices  32.5 us (37%)
  Pallas kernels  16.3 us (19%)
  local copies, waits for them, and re-layouts  2.45 us (3%)
    ppermute x17, waiting for transfers between devices, permute(): return lax.ppermute(x, ('tm', 'space'), pairs)  30.4 us
    ppermute x17, starting transfers between devices, permute(): return lax.ppermute(x, ('tm', 'space'), pairs)  27.7 us
    pallas_call x1, Pallas kernels, basis_call(): pl.pallas_call(basis_kernel, in_specs=[vmem, vmem], out_specs=[vmem, vmem...  9.41 us
    ppermute x4, starting transfers between devices, swap(): lax.ppermute(x, axis, [(i, i ^ mask) for i in range(lax.axis_size(axis))])  6.71 us
    pallas_call x2, Pallas kernels, sketch_call(): pl.pallas_call(functools.partial(sketch_kernel, first, count, later), in_...  6.15 us
    unnamed x8, local copies, waits for them, and re-layouts  2.35 us
    ppermute x4, waiting for transfers between devices, swap(): lax.ppermute(x, axis, [(i, i ^ mask) for i in range(lax.axis_size(axis))])  2.12 us
  transfers between devices with their start and end apart: 21, of which 18 were waited for; matrix products, arithmetic and copies ran while one was open for 1% of the time, Pallas kernels for 2%

profile of v6, /device:TPU:1, one launch (start us, length us, event | category | flops | bytes accessed | tf_op | source)
XLA Modules:
  0.0 87.1 jit_solution(14555801465782413962)
XLA Ops:
  3.0 4.2 %shard_map.68 = (f32[4,8,32,256]{3,2,1,0:T(8,128)S(1)}, f32[4,8,32,256]{3,2,1,0:T(8,128)S(1)}, bf16[4,1024,256]{2,1,0:T(8,128)(2,1)S(1)}) custom-call(bf16[12,1024,256]{2,1,0:T(8,128)(2,1)} %bitcast.16, bf16[1024,256]{1,0:T(8,128)(2,1)S(1)} %copy-done.1, s32[12]{0:T(128)S(1)} %copy-done.2, f32[12]{0:T(128)S(1)} %copy-done.3), custom_call_target="tpu_custom_call" | custom-call | flops 2147483648 | bytes 8388608 | tf_op jit(solution)/shard_map/pallas_call | solution.py:130
  7.2 3.3 %collective-permute-start = (f32[4,8,32,256]{3,2,1,0:T(8,128)S(1)}, f32[4,8,32,256]{3,2,1,0:T(8,128)S(1)}, u32[]{:S(2)}, u32[]{:S(2)}) collective-permute-start(f32[4,8,32,256]{3,2,1,0:T(8,128)S(1)} %get-tuple-element.12), channel_id=1, source_target_pairs={{0,32},{32,0},{64,96},{96,64},{128,160},{160,128},{192,224},{224,1... | collective-permute-start | bytes 3145736 | tf_op jit(solution)/shard_map/ppermute | solution.py:343
  10.5 1.9 %shard_map.69 = (f32[4,4,32,256]{3,2,1,0:T(8,128)S(1)}, f32[4,4,32,256]{3,2,1,0:T(8,128)S(1)}) custom-call(bf16[4,1024,256]{2,1,0:T(8,128)(2,1)S(1)} %get-tuple-element.13.snap_ref, bf16[1024,256]{1,0:T(8,128)(2,1)S(1)} %copy-done.1, s32[12]{0:T(128)S(1)} %copy-done.2, f32[12]{0:T(128)S(1)} %copy-done.3), custom_call_target="tpu_custom_call" | custom-call | flops 1073741824 | bytes 4194304 | tf_op jit(solution)/shard_map/pallas_call | solution.py:130
  13.1 1.3 %collective-permute-start.1 = (f32[2,8,32,256]{3,2,1,0:T(8,128)S(1)}, f32[2,8,32,256]{3,2,1,0:T(8,128)S(1)}, u32[]{:S(2)}, u32[]{:S(2)}) collective-permute-start(f32[2,8,32,256]{3,2,1,0:T(8,128)S(1)} %slice.33), channel_id=1, source_target_pairs={{0,96},{1,97},{2,98},{3,99},{4,100},{5,101},{6,102},{7,103},{8,104... | collective-permute-start | bytes 1572872 | tf_op jit(solution)/shard_map/ppermute | solution.py:352
  14.6 1.7 %collective-permute-start.6 = (f32[2,4,32,256]{3,2,1,0:T(8,128)S(1)}, f32[2,4,32,256]{3,2,1,0:T(8,128)S(1)}, u32[]{:S(2)}, u32[]{:S(2)}) collective-permute-start(f32[2,4,32,256]{3,2,1,0:T(8,128)S(1)} %slice.37), channel_id=1, source_target_pairs={{0,96},{1,97},{2,98},{3,99},{4,100},{5,101},{6,102},{7,103},{8,104... | collective-permute-start | bytes 786440 | tf_op jit(solution)/shard_map/ppermute | solution.py:352
  16.3 6.7 %collective-permute-done.1 = f32[2,8,32,256]{3,2,1,0:T(8,128)S(1)} collective-permute-done((f32[2,8,32,256]{3,2,1,0:T(8,128)S(1)}, f32[2,8,32,256]{3,2,1,0:T(8,128)S(1)}, u32[]{:S(2)}, u32[]{:S(2)}) %collective-permute-start.1) | collective-permute-done | bytes 524320 | tf_op jit(solution)/shard_map/ppermute | solution.py:352
  23.2 2.6 %collective-permute-done.6 = f32[2,4,32,256]{3,2,1,0:T(8,128)S(1)} collective-permute-done((f32[2,4,32,256]{3,2,1,0:T(8,128)S(1)}, f32[2,4,32,256]{3,2,1,0:T(8,128)S(1)}, u32[]{:S(2)}, u32[]{:S(2)}) %collective-permute-start.6) | collective-permute-done | bytes 262176 | tf_op jit(solution)/shard_map/ppermute | solution.py:352
  25.9 3.3 %collective-permute-done.2 = f32[8,32,256]{2,1,0:T(8,128)S(1)} collective-permute-done((f32[8,32,256]{2,1,0:T(8,128)S(1)}, f32[8,32,256]{2,1,0:T(8,128)S(1)}, u32[]{:S(2)}, u32[]{:S(2)}) %collective-permute-start.2) | collective-permute-done | bytes 262176 | tf_op jit(solution)/shard_map/ppermute | solution.py:352
  29.4 1.3 %collective-permute-start.4 = (f32[8,32,256]{2,1,0:T(8,128)S(1)}, f32[8,32,256]{2,1,0:T(8,128)S(1)}, u32[]{:S(2)}, u32[]{:S(2)}) collective-permute-start(f32[8,32,256]{2,1,0:T(8,128)S(1)} %fusion.refs_0_), channel_id=1, source_target_pairs={{0,64},{1,2},{2,1},{3,4},{4,3},{5,6},{6,5},{7,8},{8,7},{9,10},{10,... | collective-permute-start | bytes 786440 | tf_op jit(solution)/shard_map/ppermute | solution.py:352
  31.4 3.9 %collective-permute-start.9 = (f32[4,32,256]{2,1,0:T(8,128)S(1)}, f32[4,32,256]{2,1,0:T(8,128)S(1)}, u32[]{:S(2)}, u32[]{:S(2)}) collective-permute-start(f32[4,32,256]{2,1,0:T(8,128)S(1)} %fusion.1.refs_3_), channel_id=1, source_target_pairs={{0,64},{1,2},{2,1},{3,4},{4,3},{5,6},{6,5},{7,8},{8,7},{9,10},{10,... | collective-permute-start | bytes 393224 | tf_op jit(solution)/shard_map/ppermute | solution.py:352
  35.3 4.4 %collective-permute-done.8.refs_4_ = f32[4,32,256]{2,1,0:T(8,128)S(1)} collective-permute-done((f32[4,32,256]{2,1,0:T(8,128)S(1)}, f32[4,32,256]{2,1,0:T(8,128)S(1)}, u32[]{:S(2)}, u32[]{:S(2)}) %collective-permute-start.8) | collective-permute-done | bytes 131104 | tf_op jit(solution)/shard_map/ppermute | solution.py:352
  42.9 5.0 %collective-permute-start.11 = (f32[136,128]{1,0:T(8,128)S(1)}, f32[136,128]{1,0:T(8,128)S(1)}, u32[]{:S(2)}, u32[]{:S(2)}) collective-permute-start(f32[136,128]{1,0:T(8,128)S(1)} %dynamic-slice_add_fusion), channel_id=1, source_target_pairs={{0,224},{1,39},{2,36},{3,227},{4,228},{5,35},{6,32},{7,231},{8,46}... | collective-permute-start | bytes 208904 | tf_op jit(solution)/shard_map/ppermute | solution.py:352
  47.9 2.0 %collective-permute-done.11 = f32[136,128]{1,0:T(8,128)S(1)} collective-permute-done((f32[136,128]{1,0:T(8,128)S(1)}, f32[136,128]{1,0:T(8,128)S(1)}, u32[]{:S(2)}, u32[]{:S(2)}) %collective-permute-start.11) | collective-permute-done | bytes 69664 | tf_op jit(solution)/shard_map/ppermute | solution.py:352
  49.9 2.8 %collective-permute-start.12 = (f32[136,128]{1,0:T(8,128)S(1)}, f32[136,128]{1,0:T(8,128)S(1)}, u32[]{:S(2)}, u32[]{:S(2)}) collective-permute-start(f32[136,128]{1,0:T(8,128)S(1)} %add.63), channel_id=1, source_target_pairs={{0,56},{1,225},{2,226},{3,59},{4,60},{5,229},{6,230},{7,63},{8,232... | collective-permute-start | bytes 208904 | tf_op jit(solution)/shard_map/ppermute | solution.py:352
  52.8 2.7 %collective-permute-done.12 = f32[136,128]{1,0:T(8,128)S(1)} collective-permute-done((f32[136,128]{1,0:T(8,128)S(1)}, f32[136,128]{1,0:T(8,128)S(1)}, u32[]{:S(2)}, u32[]{:S(2)}) %collective-permute-start.12) | collective-permute-done | bytes 69664 | tf_op jit(solution)/shard_map/ppermute | solution.py:352
  55.4 3.7 %collective-permute-start.13 = (f32[136,128]{1,0:T(8,128)S(1)}, f32[136,128]{1,0:T(8,128)S(1)}, u32[]{:S(2)}, u32[]{:S(2)}) collective-permute-start(f32[136,128]{1,0:T(8,128)S(1)} %add.64), channel_id=1, source_target_pairs={{0,38},{1,57},{2,58},{3,37},{4,34},{5,61},{6,62},{7,33},{8,48},{9,... | collective-permute-start | bytes 208904 | tf_op jit(solution)/shard_map/ppermute | solution.py:352
  59.2 2.2 %collective-permute-done.13 = f32[136,128]{1,0:T(8,128)S(1)} collective-permute-done((f32[136,128]{1,0:T(8,128)S(1)}, f32[136,128]{1,0:T(8,128)S(1)}, u32[]{:S(2)}, u32[]{:S(2)}) %collective-permute-start.13) | collective-permute-done | bytes 69664 | tf_op jit(solution)/shard_map/ppermute | solution.py:352
  61.5 1.3 %collective-permute-start.14 = (f32[136,128]{1,0:T(8,128)S(1)}, f32[136,128]{1,0:T(8,128)S(1)}, u32[]{:S(2)}, u32[]{:S(2)}) collective-permute-start(f32[136,128]{1,0:T(8,128)S(1)} %add.65), channel_id=1, source_target_pairs={{0,96},{1,32},{2,35},{3,99},{4,100},{5,36},{6,39},{7,103},{8,41},{... | collective-permute-start | bytes 208904 | tf_op jit(solution)/shard_map/ppermute | solution.py:352
  63.7 1.6 %collective-permute-start.16 = (f32[136,128]{1,0:T(8,128)S(1)}, f32[136,128]{1,0:T(8,128)S(1)}, u32[]{:S(2)}, u32[]{:S(2)}) collective-permute-start(f32[136,128]{1,0:T(8,128)S(1)} %add.65), channel_id=1, source_target_pairs={{0,72},{1,2},{2,1},{3,75},{4,76},{5,6},{6,5},{7,79},{8,11},{9,65},... | collective-permute-start | bytes 208904 | tf_op jit(solution)/shard_map/ppermute | solution.py:352
  65.5 2.4 %collective-permute-done.15 = f32[136,128]{1,0:T(8,128)S(1)} collective-permute-done((f32[136,128]{1,0:T(8,128)S(1)}, f32[136,128]{1,0:T(8,128)S(1)}, u32[]{:S(2)}, u32[]{:S(2)}) %collective-permute-start.15) | collective-permute-done | bytes 69664 | tf_op jit(solution)/shard_map/ppermute | solution.py:352
  70.2 1.7 %collective-permute-start.19 = (f32[136,128]{1,0:T(8,128)S(1)}, f32[136,128]{1,0:T(8,128)S(1)}, u32[]{:S(2)}, u32[]{:S(2)}) collective-permute-start(f32[136,128]{1,0:T(8,128)S(1)} %add_add_fusion.1), channel_id=1, source_target_pairs={{0,3},{1,73},{2,74},{3,0},{4,7},{5,77},{6,78},{7,4},{8,64},{9,10},... | collective-permute-start | bytes 208904 | tf_op jit(solution)/shard_map/ppermute | solution.py:352
  71.8 1.1 %collective-permute-done.17 = f32[136,128]{1,0:T(8,128)S(1)} collective-permute-done((f32[136,128]{1,0:T(8,128)S(1)}, f32[136,128]{1,0:T(8,128)S(1)}, u32[]{:S(2)}, u32[]{:S(2)}) %collective-permute-start.17) | collective-permute-done | bytes 69664 | tf_op jit(solution)/shard_map/ppermute | solution.py:352
  74.3 2.4 %collective-permute-start.20 = (f32[136,128]{1,0:T(8,128)S(1)}, f32[136,128]{1,0:T(8,128)S(1)}, u32[]{:S(2)}, u32[]{:S(2)}) collective-permute-start(f32[136,128]{1,0:T(8,128)S(1)} %add_add_fusion), channel_id=1, source_target_pairs={{0,32},{32,0},{64,96},{96,64},{128,160},{160,128},{192,224},{224,1... | collective-permute-start | bytes 208904 | tf_op jit(solution)/shard_map/ppermute | solution.py:343
  77.7 9.4 %shard_map.71 = (f32[768,128]{1,0:T(8,128)}, f32[256,256]{1,0:T(8,128)}) custom-call(f32[272,128]{1,0:T(8,128)S(1)} %maximum_select_fusion.gram_ref, f32[12,32,256]{2,1,0:T(8,128)S(1)} %get-tuple-element.17.panel_ref), custom_call_target="tpu_custom_call" | custom-call | tf_op jit(solution)/shard_map/pallas_call | solution.py:329
  (48 shorter events, 13.1 us)
Async XLA Ops:
  0.6 1.0 %copy-start.1 = (bf16[1024,256]{1,0:T(8,128)(2,1)S(1)}, bf16[1024,256]{1,0:T(8,128)(2,1)}, u32[]{:S(2)}) copy-start(bf16[1024,256]{1,0:T(8,128)(2,1)} %sketch_hbm.3) | copy-start | bytes 1572868
  1.7 0.7 copy-start.2
  7.2 5.6 %collective-permute-start = (f32[4,8,32,256]{3,2,1,0:T(8,128)S(1)}, f32[4,8,32,256]{3,2,1,0:T(8,128)S(1)}, u32[]{:S(2)}, u32[]{:S(2)}) collective-permute-start(f32[4,8,32,256]{3,2,1,0:T(8,128)S(1)} %get-tuple-element.12), channel_id=1, source_target_pairs={{0,32},{32,0},{64,96},{96,64},{128,160},{160,128},{192,224},{224,1... | collective-permute-start | bytes 3145736 | tf_op jit(solution)/shard_map/ppermute | solution.py:343
  12.5 27.8 %copy-start = (f32[1,256]{1,0:T(1,128)S(1)}, f32[1,256]{1,0:T(1,128)}, u32[]{:S(2)}) copy-start(f32[1,256]{1,0:T(1,128)} %volume_ref.1) | copy-start | bytes 3076
  12.5 2.0 %collective-permute-start.5 = (f32[4,4,32,256]{3,2,1,0:T(8,128)S(1)}, f32[4,4,32,256]{3,2,1,0:T(8,128)S(1)}, u32[]{:S(2)}, u32[]{:S(2)}) collective-permute-start(f32[4,4,32,256]{3,2,1,0:T(8,128)S(1)} %get-tuple-element.15), channel_id=1, source_target_pairs={{0,32},{32,0},{64,96},{96,64},{128,160},{160,128},{192,224},{224,1... | collective-permute-start | bytes 1572872 | tf_op jit(solution)/shard_map/ppermute | solution.py:343
  13.1 9.9 %collective-permute-start.1 = (f32[2,8,32,256]{3,2,1,0:T(8,128)S(1)}, f32[2,8,32,256]{3,2,1,0:T(8,128)S(1)}, u32[]{:S(2)}, u32[]{:S(2)}) collective-permute-start(f32[2,8,32,256]{3,2,1,0:T(8,128)S(1)} %slice.33), channel_id=1, source_target_pairs={{0,96},{1,97},{2,98},{3,99},{4,100},{5,101},{6,102},{7,103},{8,104... | collective-permute-start | bytes 1572872 | tf_op jit(solution)/shard_map/ppermute | solution.py:352
  14.6 11.2 %collective-permute-start.6 = (f32[2,4,32,256]{3,2,1,0:T(8,128)S(1)}, f32[2,4,32,256]{3,2,1,0:T(8,128)S(1)}, u32[]{:S(2)}, u32[]{:S(2)}) collective-permute-start(f32[2,4,32,256]{3,2,1,0:T(8,128)S(1)} %slice.37), channel_id=1, source_target_pairs={{0,96},{1,97},{2,98},{3,99},{4,100},{5,101},{6,102},{7,103},{8,104... | collective-permute-start | bytes 786440 | tf_op jit(solution)/shard_map/ppermute | solution.py:352
  23.1 6.2 %collective-permute-start.2 = (f32[8,32,256]{2,1,0:T(8,128)S(1)}, f32[8,32,256]{2,1,0:T(8,128)S(1)}, u32[]{:S(2)}, u32[]{:S(2)}) collective-permute-start(f32[8,32,256]{2,1,0:T(8,128)S(1)} %slice_bitcast_fusion), channel_id=1, source_target_pairs={{0,224},{1,225},{2,226},{3,227},{4,228},{5,229},{6,230},{7,231},{8... | collective-permute-start | bytes 786440 | tf_op jit(solution)/shard_map/ppermute | solution.py:352
  25.8 4.9 %collective-permute-start.7 = (f32[4,32,256]{2,1,0:T(8,128)S(1)}, f32[4,32,256]{2,1,0:T(8,128)S(1)}, u32[]{:S(2)}, u32[]{:S(2)}) collective-permute-start(f32[4,32,256]{2,1,0:T(8,128)S(1)} %slice_bitcast_fusion.2), channel_id=1, source_target_pairs={{0,224},{1,225},{2,226},{3,227},{4,228},{5,229},{6,230},{7,231},{8... | collective-permute-start | bytes 393224 | tf_op jit(solution)/shard_map/ppermute | solution.py:352
  29.3 11.0 %collective-permute-start.3 = (f32[8,32,256]{2,1,0:T(8,128)S(1)}, f32[8,32,256]{2,1,0:T(8,128)S(1)}, u32[]{:S(2)}, u32[]{:S(2)}) collective-permute-start(f32[8,32,256]{2,1,0:T(8,128)S(1)} %fusion.refs_0_), channel_id=1, source_target_pairs={{0,1},{1,0},{2,3},{3,2},{4,5},{5,4},{6,7},{7,6},{8,9},{9,8},{10,11... | collective-permute-start | bytes 786440 | tf_op jit(solution)/shard_map/ppermute | solution.py:352
  29.4 10.9 %collective-permute-start.4 = (f32[8,32,256]{2,1,0:T(8,128)S(1)}, f32[8,32,256]{2,1,0:T(8,128)S(1)}, u32[]{:S(2)}, u32[]{:S(2)}) collective-permute-start(f32[8,32,256]{2,1,0:T(8,128)S(1)} %fusion.refs_0_), channel_id=1, source_target_pairs={{0,64},{1,2},{2,1},{3,4},{4,3},{5,6},{6,5},{7,8},{8,7},{9,10},{10,... | collective-permute-start | bytes 786440 | tf_op jit(solution)/shard_map/ppermute | solution.py:352
  30.7 9.0 %collective-permute-start.8 = (f32[4,32,256]{2,1,0:T(8,128)S(1)}, f32[4,32,256]{2,1,0:T(8,128)S(1)}, u32[]{:S(2)}, u32[]{:S(2)}) collective-permute-start(f32[4,32,256]{2,1,0:T(8,128)S(1)} %fusion.1.refs_3_), channel_id=1, source_target_pairs={{0,1},{1,0},{2,3},{3,2},{4,5},{5,4},{6,7},{7,6},{8,9},{9,8},{10,11... | collective-permute-start | bytes 393224 | tf_op jit(solution)/shard_map/ppermute | solution.py:352
  31.4 8.8 %collective-permute-start.9 = (f32[4,32,256]{2,1,0:T(8,128)S(1)}, f32[4,32,256]{2,1,0:T(8,128)S(1)}, u32[]{:S(2)}, u32[]{:S(2)}) collective-permute-start(f32[4,32,256]{2,1,0:T(8,128)S(1)} %fusion.1.refs_3_), channel_id=1, source_target_pairs={{0,64},{1,2},{2,1},{3,4},{4,3},{5,6},{6,5},{7,8},{8,7},{9,10},{10,... | collective-permute-start | bytes 393224 | tf_op jit(solution)/shard_map/ppermute | solution.py:352
  41.1 1.8 %collective-permute-start.10 = (f32[136,128]{1,0:T(8,128)S(1)}, f32[136,128]{1,0:T(8,128)S(1)}, u32[]{:S(2)}, u32[]{:S(2)}) collective-permute-start(f32[136,128]{1,0:T(8,128)S(1)} %constant_dynamic-slice_fusion), channel_id=1, source_target_pairs={{0,32},{32,0},{64,96},{96,64},{128,160},{160,128},{192,224},{224,1... | collective-permute-start | bytes 208904 | tf_op jit(solution)/shard_map/ppermute | solution.py:343
  42.9 7.1 %collective-permute-start.11 = (f32[136,128]{1,0:T(8,128)S(1)}, f32[136,128]{1,0:T(8,128)S(1)}, u32[]{:S(2)}, u32[]{:S(2)}) collective-permute-start(f32[136,128]{1,0:T(8,128)S(1)} %dynamic-slice_add_fusion), channel_id=1, source_target_pairs={{0,224},{1,39},{2,36},{3,227},{4,228},{5,35},{6,32},{7,231},{8,46}... | collective-permute-start | bytes 208904 | tf_op jit(solution)/shard_map/ppermute | solution.py:352
  49.9 5.5 %collective-permute-start.12 = (f32[136,128]{1,0:T(8,128)S(1)}, f32[136,128]{1,0:T(8,128)S(1)}, u32[]{:S(2)}, u32[]{:S(2)}) collective-permute-start(f32[136,128]{1,0:T(8,128)S(1)} %add.63), channel_id=1, source_target_pairs={{0,56},{1,225},{2,226},{3,59},{4,60},{5,229},{6,230},{7,63},{8,232... | collective-permute-start | bytes 208904 | tf_op jit(solution)/shard_map/ppermute | solution.py:352
  55.4 6.0 %collective-permute-start.13 = (f32[136,128]{1,0:T(8,128)S(1)}, f32[136,128]{1,0:T(8,128)S(1)}, u32[]{:S(2)}, u32[]{:S(2)}) collective-permute-start(f32[136,128]{1,0:T(8,128)S(1)} %add.64), channel_id=1, source_target_pairs={{0,38},{1,57},{2,58},{3,37},{4,34},{5,61},{6,62},{7,33},{8,48},{9,... | collective-permute-start | bytes 208904 | tf_op jit(solution)/shard_map/ppermute | solution.py:352
  61.5 4.0 %collective-permute-start.14 = (f32[136,128]{1,0:T(8,128)S(1)}, f32[136,128]{1,0:T(8,128)S(1)}, u32[]{:S(2)}, u32[]{:S(2)}) collective-permute-start(f32[136,128]{1,0:T(8,128)S(1)} %add.65), channel_id=1, source_target_pairs={{0,96},{1,32},{2,35},{3,99},{4,100},{5,36},{6,39},{7,103},{8,41},{... | collective-permute-start | bytes 208904 | tf_op jit(solution)/shard_map/ppermute | solution.py:352
  62.8 5.1 %collective-permute-start.15 = (f32[136,128]{1,0:T(8,128)S(1)}, f32[136,128]{1,0:T(8,128)S(1)}, u32[]{:S(2)}, u32[]{:S(2)}) collective-permute-start(f32[136,128]{1,0:T(8,128)S(1)} %add.65), channel_id=1, source_target_pairs={{0,40},{1,35},{2,32},{3,43},{4,44},{5,39},{6,36},{7,47},{8,42},{9,... | collective-permute-start | bytes 208904 | tf_op jit(solution)/shard_map/ppermute | solution.py:352
  63.7 5.1 %collective-permute-start.16 = (f32[136,128]{1,0:T(8,128)S(1)}, f32[136,128]{1,0:T(8,128)S(1)}, u32[]{:S(2)}, u32[]{:S(2)}) collective-permute-start(f32[136,128]{1,0:T(8,128)S(1)} %add.65), channel_id=1, source_target_pairs={{0,72},{1,2},{2,1},{3,75},{4,76},{5,6},{6,5},{7,79},{8,11},{9,65},... | collective-permute-start | bytes 208904 | tf_op jit(solution)/shard_map/ppermute | solution.py:352
  68.8 4.1 %collective-permute-start.17 = (f32[136,128]{1,0:T(8,128)S(1)}, f32[136,128]{1,0:T(8,128)S(1)}, u32[]{:S(2)}, u32[]{:S(2)}) collective-permute-start(f32[136,128]{1,0:T(8,128)S(1)} %add_add_fusion.1), channel_id=1, source_target_pairs={{0,33},{1,97},{2,98},{3,34},{4,37},{5,101},{6,102},{7,38},{8,104},... | collective-permute-start | bytes 208904 | tf_op jit(solution)/shard_map/ppermute | solution.py:352
  69.3 3.9 %collective-permute-start.18 = (f32[136,128]{1,0:T(8,128)S(1)}, f32[136,128]{1,0:T(8,128)S(1)}, u32[]{:S(2)}, u32[]{:S(2)}) collective-permute-start(f32[136,128]{1,0:T(8,128)S(1)} %add_add_fusion.1), channel_id=1, source_target_pairs={{0,34},{1,41},{2,42},{3,33},{4,38},{5,45},{6,46},{7,37},{8,32},{9,... | collective-permute-start | bytes 208904 | tf_op jit(solution)/shard_map/ppermute | solution.py:352
  70.2 4.1 %collective-permute-start.19 = (f32[136,128]{1,0:T(8,128)S(1)}, f32[136,128]{1,0:T(8,128)S(1)}, u32[]{:S(2)}, u32[]{:S(2)}) collective-permute-start(f32[136,128]{1,0:T(8,128)S(1)} %add_add_fusion.1), channel_id=1, source_target_pairs={{0,3},{1,73},{2,74},{3,0},{4,7},{5,77},{6,78},{7,4},{8,64},{9,10},... | collective-permute-start | bytes 208904 | tf_op jit(solution)/shard_map/ppermute | solution.py:352
  74.3 3.3 %collective-permute-start.20 = (f32[136,128]{1,0:T(8,128)S(1)}, f32[136,128]{1,0:T(8,128)S(1)}, u32[]{:S(2)}, u32[]{:S(2)}) collective-permute-start(f32[136,128]{1,0:T(8,128)S(1)} %add_add_fusion), channel_id=1, source_target_pairs={{0,32},{32,0},{64,96},{96,64},{128,160},{160,128},{192,224},{224,1... | collective-permute-start | bytes 208904 | tf_op jit(solution)/shard_map/ppermute | solution.py:343
  (1 other events, 0.7 us)
